TPU v7x, 32 devices: a whole 2x2x4 slice. The times are simulated.
32 devices in a mesh: blk: 8 (over z, x), head: 4 (over y, core).
Axes of the slice: x: 2, y: 2, z: 4, core: 2. Of those that a mesh axis runs over, the one named last changes fastest.
Arguments:
- block_in: bfloat16 [4, 1024, 2048], P('head', 'blk'), may hold values from -6 to 6
- lengths: int32 [4], replicated, may hold values from 256 to 1024, as said below
- out_cot: bfloat16 [4, 1024, 2048], P('head', 'blk'), may hold values from -6 to 6
- ln1_gain: float32 [2048], replicated, may hold values from 0.5 to 1.5
- ln1_bias: float32 [2048], replicated, may hold values from -1 to 1
- w_q: bfloat16 [2048, 2048], P('blk', 'head'), may hold values from -0.1875 to 0.1875
- b_q: float32 [2048], replicated, may hold values from -1 to 1
- w_kv: bfloat16 [2048, 256], replicated, may hold values from -0.1875 to 0.1875
- b_v: float32 [128], replicated, may hold values from -1 to 1
- w_out: bfloat16 [2048, 2048], P('blk', 'head'), may hold values from -0.75 to 0.75
- b_out: float32 [2048], replicated, may hold values from -1 to 1
- ln2_gain: float32 [2048], replicated, may hold values from 0.5 to 1.5
- ln2_bias: float32 [2048], replicated, may hold values from -1 to 1
- w_up: bfloat16 [2048, 8192], P('blk', 'head'), may hold values from -0.125 to 0.125
- b_up: float32 [8192], replicated, may hold values from -1 to 1
- w_down: bfloat16 [2048, 8192], P('blk', 'head'), may hold values from -0.0625 to 0.0625
- b_down: float32 [2048], replicated, may hold values from -1 to 1
Outputs:
- block_out: bfloat16 [4, 1024, 2048], P('head', 'blk')
- grad_in: float32 [4, 1024, 2048], P('head', 'blk')
- g_ln1_gain: float32 [2048], replicated
- g_ln1_bias: float32 [2048], replicated
- g_w_q: float32 [2048, 2048], P('blk', 'head')
- g_b_q: float32 [2048], replicated
- g_w_kv: float32 [2048, 256], replicated
- g_b_v: float32 [128], replicated
- g_w_out: float32 [2048, 2048], P('blk', 'head')
- g_b_out: float32 [2048], replicated
- g_ln2_gain: float32 [2048], replicated
- g_ln2_bias: float32 [2048], replicated
- g_w_up: float32 [2048, 8192], P('blk', 'head')
- g_b_up: float32 [8192], replicated
- g_w_down: float32 [2048, 8192], P('blk', 'head')
- g_b_down: float32 [2048], replicated
Inputs may be any that keep to these rules, and one draw needn't show every extreme that they name: `lengths`: one slot, drawn from the seed, has exactly 1024 valid positions; each other slot has between 256 and 1024.
All inputs are finite; a program needn't handle non-finite values.
Results may differ from a plain program's by a relative error of at most 0.02.
Values may be sent and summed in bfloat16 or wider, within the bound.
No kernel may reach another device: no remote copies, remote signals or barrier semaphores. Data moves between devices by JAX's collectives and lax.ppermute only.
A program may use at most 192 MiB of HBM per device.

v0:
```python
from functools import partial

import jax
import jax.numpy as jnp
from jax import lax
from jax.sharding import PartitionSpec as P

FF = 8192
HEADS = 16
HEAD_DIM = 128
KEY_TILE = 4


EPSILON = 1e-05


def layer_norm(values, gain, bias):
    center = values - jnp.mean(values, axis=-1, keepdims=True)
    spread = jnp.mean(center * center, axis=-1, keepdims=True)
    return center * lax.rsqrt(spread + EPSILON) * gain + bias


def plain_dot(left, right):
    return jnp.dot(left, right, preferred_element_type=jnp.float32)


def row_dot(left, right):
    return lax.dot_general(
        left, right, (((0,), (0,)), ((), ())), preferred_element_type=jnp.float32
    )


def col_dot(left, right):
    return lax.dot_general(
        left, right, (((1,), (1,)), ((), ())), preferred_element_type=jnp.float32
    )


def make_parts(row_q, row_pos, all_keys, lengths, seq_dev):
    score_scale = HEAD_DIM ** (-0.5)
    positions = jnp.arange(seq_dev, dtype=jnp.int32)

    def tile_parts(tile):
        block_kv = lax.dynamic_slice_in_dim(all_keys, tile * KEY_TILE, KEY_TILE, 0)
        tile_keys = block_kv[..., :HEAD_DIM]
        tile_values = block_kv[..., HEAD_DIM:]
        raw = (
            jnp.einsum("sqhd,bsjd->sqhbj", row_q, tile_keys, preferred_element_type=jnp.float32)
            * score_scale
        )
        key_pos = (tile * KEY_TILE + jnp.arange(KEY_TILE, dtype=jnp.int32))[
            :, None
        ] * seq_dev + positions[None, :]
        causal = key_pos[None, :, :] <= row_pos[:, None, None]
        inside = key_pos[None, :, :] < lengths[:, None, None]
        allowed = causal[None, :, None, :, :] & inside[:, None, None, :, :]
        return (raw, allowed, tile_keys, tile_values)

    return tile_parts


def attention_forward(tile_parts, stat_shape, tiles):

    def stats_step(tile, carry):
        run_max, run_sum = carry
        raw, allowed, tile_keys, tile_values = tile_parts(tile)
        masked = jnp.where(allowed, raw, -1e30)
        new_max = jnp.maximum(run_max, jnp.max(masked, axis=(3, 4)))
        weights = jnp.where(allowed, jnp.exp(masked - new_max[..., None, None]), 0.0)
        run_sum = run_sum * jnp.exp(run_max - new_max) + jnp.sum(weights, axis=(3, 4))
        return (new_max, run_sum)

    run_max, run_sum = lax.fori_loop(
        0,
        tiles,
        stats_step,
        (jnp.full(stat_shape, -1e30, jnp.float32), jnp.zeros(stat_shape, jnp.float32)),
    )
    log_total = run_max + jnp.log(run_sum)

    def output_step(tile, total):
        raw, allowed, tile_keys, tile_values = tile_parts(tile)
        weights = jnp.where(allowed, jnp.exp(raw - log_total[..., None, None]), 0.0).astype(
            jnp.bfloat16
        )
        return total + jnp.einsum(
            "sqhbj,bsjd->sqhd", weights, tile_values, preferred_element_type=jnp.float32
        )

    attn_full = lax.fori_loop(
        0, tiles, output_step, jnp.zeros(stat_shape + (HEAD_DIM,), jnp.float32)
    )
    return (log_total, attn_full)


def attention_backward(tile_parts, row_q, stat_shape, tiles, log_total, row_grad, delta, kv_grad):
    score_scale = HEAD_DIM ** (-0.5)

    def grad_step(tile, carry):
        query_grad, kv_total = carry
        raw, allowed, tile_keys, tile_values = tile_parts(tile)
        weights = jnp.where(allowed, jnp.exp(raw - log_total[..., None, None]), 0.0)
        weights_low = weights.astype(jnp.bfloat16)
        prob_grad = jnp.einsum(
            "sqhd,bsjd->sqhbj", row_grad, tile_values, preferred_element_type=jnp.float32
        )
        score_grad = (weights * (prob_grad - delta[..., None, None])).astype(jnp.bfloat16)
        query_grad = (
            query_grad
            + jnp.einsum(
                "sqhbj,bsjd->sqhd", score_grad, tile_keys, preferred_element_type=jnp.float32
            )
            * score_scale
        )
        key_grad = (
            jnp.einsum("sqhbj,sqhd->bsjd", score_grad, row_q, preferred_element_type=jnp.float32)
            * score_scale
        )
        value_grad = jnp.einsum(
            "sqhbj,sqhd->bsjd", weights_low, row_grad, preferred_element_type=jnp.float32
        )
        old = lax.dynamic_slice_in_dim(kv_total, tile * KEY_TILE, KEY_TILE, 0)
        kv_total = lax.dynamic_update_slice_in_dim(
            kv_total, old + jnp.concatenate([key_grad, value_grad], axis=-1), tile * KEY_TILE, 0
        )
        return (query_grad, kv_total)

    return lax.fori_loop(
        0, tiles, grad_step, (jnp.zeros(stat_shape + (HEAD_DIM,), jnp.float32), kv_grad)
    )


def on_device(
    block_in,
    lengths,
    out_cot,
    ln1_gain,
    ln1_bias,
    w_q,
    b_q,
    w_kv,
    b_v,
    w_out,
    b_out,
    ln2_gain,
    ln2_bias,
    w_up,
    b_up,
    w_down,
    b_down,
):
    blk_count = lax.axis_size("blk")
    head_count = lax.axis_size("head")
    blk_index = lax.axis_index("blk")
    head_index = lax.axis_index("head")
    seq_dev = block_in.shape[1]
    width = block_in.shape[2]
    heads_dev = HEADS // head_count
    ff_dev = w_up.shape[1]
    group_size = head_count * seq_dev
    own_rows = block_in[0].astype(jnp.float32)
    positions = jnp.arange(seq_dev, dtype=jnp.int32)
    query_pos = blk_index * seq_dev + positions
    own_valid = query_pos < lengths[head_index]
    slot_valid = query_pos[None, :] < lengths[:, None]
    full_q, full_out, full_up, full_down = (
        lax.all_gather(w_q, "blk", axis=0, tiled=True),
        lax.all_gather(w_out, "blk", axis=0, tiled=True),
        lax.all_gather(w_up, "blk", axis=0, tiled=True),
        lax.all_gather(w_down, "blk", axis=0, tiled=True),
    )
    attn_in = layer_norm(own_rows, ln1_gain, ln1_bias).astype(jnp.bfloat16)
    value_bias = jnp.concatenate([jnp.zeros((HEAD_DIM,), jnp.float32), b_v])
    key_value = (plain_dot(attn_in, w_kv) + value_bias).astype(jnp.bfloat16)
    group_in, group_cot = (
        lax.all_gather(attn_in[None], "head", axis=0, tiled=True),
        lax.all_gather(out_cot, "head", axis=0, tiled=True),
    )
    all_keys = lax.all_gather(key_value[None], ("blk", "head"), axis=0, tiled=True)
    all_keys = all_keys.reshape(blk_count, head_count, seq_dev, 2 * HEAD_DIM)
    group_in = group_in.reshape(group_size, width)
    column_start = head_index * heads_dev * HEAD_DIM
    query_bias = lax.dynamic_slice_in_dim(b_q, column_start, heads_dev * HEAD_DIM)
    queries = (plain_dot(group_in, full_q) + query_bias).astype(jnp.bfloat16)
    queries = queries.reshape(head_count, seq_dev, heads_dev, HEAD_DIM)
    row_sets = ((queries, query_pos, blk_index // KEY_TILE + 1),)
    row_q, row_pos, tiles = row_sets[0]
    stat_shape = (head_count, row_q.shape[1], heads_dev)
    tile_parts = make_parts(row_q, row_pos, all_keys, lengths, seq_dev)
    log_total, attn_full = attention_forward(tile_parts, stat_shape, tiles)
    part_funcs = (tile_parts, row_q, stat_shape, tiles)
    part_stats = (log_total, attn_full)
    attn_low4 = part_stats[1].astype(jnp.bfloat16)
    attn_low = attn_low4.reshape(group_size, heads_dev * HEAD_DIM)
    attn_part = col_dot(attn_low, full_out)
    attn_total = lax.psum_scatter(
        attn_part.reshape(head_count, seq_dev, width).astype(jnp.bfloat16),
        "head",
        scatter_dimension=0,
        tiled=True,
    ).astype(jnp.float32)[0]
    hidden_res = own_rows + attn_total + b_out
    normed_two = layer_norm(hidden_res, ln2_gain, ln2_bias).astype(jnp.bfloat16)
    ffn_in = lax.all_gather(normed_two[None], "head", axis=0, tiled=True).reshape(group_size, width)
    unit_start = head_index * ff_dev
    up_bias = lax.dynamic_slice_in_dim(b_up, unit_start, ff_dev)
    up_full = plain_dot(ffn_in, full_up) + up_bias
    activated = jax.nn.gelu(up_full, approximate=True).astype(jnp.bfloat16)
    ffn_part = col_dot(activated, full_down)
    ffn_total = lax.psum_scatter(
        ffn_part.reshape(head_count, seq_dev, width).astype(jnp.bfloat16),
        "head",
        scatter_dimension=0,
        tiled=True,
    ).astype(jnp.float32)[0]
    output = (hidden_res + ffn_total + b_down).astype(jnp.bfloat16)[None]
    back_q, back_out, back_up, back_down = (
        lax.all_gather(w_q, "blk", axis=0, tiled=True),
        lax.all_gather(w_out, "blk", axis=0, tiled=True),
        lax.all_gather(w_up, "blk", axis=0, tiled=True),
        lax.all_gather(w_down, "blk", axis=0, tiled=True),
    )
    cot_rows = jnp.where(slot_valid[:, :, None], group_cot, jnp.zeros_like(group_cot)).reshape(
        group_size, width
    )
    own_cot = jnp.where(own_valid[:, None], out_cot[0].astype(jnp.float32), 0.0)
    grad_down = row_dot(cot_rows, activated)
    grad_act = plain_dot(cot_rows, back_down)
    gelu_value, gelu_pull = jax.vjp(partial(jax.nn.gelu, approximate=True), up_full)
    grad_up_rows = gelu_pull(grad_act)[0].astype(jnp.bfloat16)
    grad_up = row_dot(ffn_in, grad_up_rows)
    grad_up_bias = jnp.sum(grad_up_rows, axis=0, dtype=jnp.float32)
    ffn_in_grad = col_dot(grad_up_rows, back_up)
    norm_two_grad = lax.psum_scatter(
        ffn_in_grad.reshape(head_count, seq_dev, width).astype(jnp.bfloat16),
        "head",
        scatter_dimension=0,
        tiled=True,
    ).astype(jnp.float32)[0]
    norm_two_value, norm_two_pull = jax.vjp(layer_norm, hidden_res, ln2_gain, ln2_bias)
    res_grad, grad_ln2_gain, grad_ln2_bias = norm_two_pull(norm_two_grad)
    res_total = own_cot + res_grad
    cot_attn = lax.all_gather(
        res_total.astype(jnp.bfloat16)[None], "head", axis=0, tiled=True
    ).reshape(group_size, width)
    grad_out = row_dot(cot_attn, attn_low)
    attn_grad = (
        plain_dot(cot_attn, back_out)
        .astype(jnp.bfloat16)
        .reshape(head_count, seq_dev, heads_dev, HEAD_DIM)
    )
    grad_sets = (attn_grad,)
    kv_grad = jnp.zeros((blk_count, head_count, seq_dev, 2 * HEAD_DIM), jnp.float32)
    tile_parts, row_q, stat_shape, tiles = part_funcs
    log_total, attn_full = part_stats
    row_grad = grad_sets[0]
    delta = jnp.sum(row_grad.astype(jnp.float32) * attn_full, axis=-1)
    query_grad, kv_grad = attention_backward(
        tile_parts, row_q, stat_shape, tiles, log_total, row_grad, delta, kv_grad
    )
    query_parts = query_grad.astype(jnp.bfloat16)
    own_kv_grad = lax.psum_scatter(
        kv_grad.reshape(blk_count * head_count, seq_dev, 2 * HEAD_DIM),
        ("blk", "head"),
        scatter_dimension=0,
        tiled=True,
    )[0].astype(jnp.bfloat16)
    query_low = query_parts.reshape(group_size, heads_dev * HEAD_DIM)
    grad_q = row_dot(group_in, query_low)
    grad_q_bias = jnp.sum(query_low, axis=0, dtype=jnp.float32)
    attn_in_grad = col_dot(query_low, back_q)
    norm_one_grad = lax.psum_scatter(
        attn_in_grad.reshape(head_count, seq_dev, width).astype(jnp.bfloat16),
        "head",
        scatter_dimension=0,
        tiled=True,
    ).astype(jnp.float32)[0] + col_dot(own_kv_grad, w_kv)
    norm_one_value, norm_one_pull = jax.vjp(layer_norm, own_rows, ln1_gain, ln1_bias)
    input_part, grad_ln1_gain, grad_ln1_bias = norm_one_pull(norm_one_grad)
    input_grad = res_total + input_part
    grad_kv = row_dot(attn_in, own_kv_grad)
    grad_v_bias = jnp.sum(own_kv_grad[:, HEAD_DIM:], axis=0, dtype=jnp.float32)
    grad_out_bias = jnp.sum(res_total, axis=0)
    grad_down_bias = jnp.sum(own_cot, axis=0)
    q_bias_full = lax.dynamic_update_slice_in_dim(
        jnp.zeros((width,), jnp.float32), grad_q_bias, column_start, 0
    )
    up_bias_full = lax.dynamic_update_slice_in_dim(
        jnp.zeros((FF,), jnp.float32), grad_up_bias, unit_start, 0
    )
    sum_q, sum_out, sum_up, sum_down = (
        lax.psum_scatter(
            grad_q.astype(jnp.bfloat16), "blk", scatter_dimension=0, tiled=True
        ).astype(jnp.float32),
        lax.psum_scatter(
            grad_out.astype(jnp.bfloat16), "blk", scatter_dimension=0, tiled=True
        ).astype(jnp.float32),
        lax.psum_scatter(
            grad_up.astype(jnp.bfloat16), "blk", scatter_dimension=0, tiled=True
        ).astype(jnp.float32),
        lax.psum_scatter(
            grad_down.astype(jnp.bfloat16), "blk", scatter_dimension=0, tiled=True
        ).astype(jnp.float32),
    )
    (
        sum_ln1_gain,
        sum_ln1_bias,
        sum_q_bias,
        sum_kv,
        sum_v_bias,
        sum_out_bias,
        sum_ln2_gain,
        sum_ln2_bias,
        sum_up_bias,
        sum_down_bias,
    ) = lax.psum(
        (
            grad_ln1_gain,
            grad_ln1_bias,
            q_bias_full,
            grad_kv,
            grad_v_bias,
            grad_out_bias,
            grad_ln2_gain,
            grad_ln2_bias,
            up_bias_full,
            grad_down_bias,
        ),
        ("blk", "head"),
    )
    return (
        output,
        input_grad[None],
        sum_ln1_gain,
        sum_ln1_bias,
        sum_q,
        sum_q_bias,
        sum_kv,
        sum_v_bias,
        sum_out,
        sum_out_bias,
        sum_ln2_gain,
        sum_ln2_bias,
        sum_up,
        sum_up_bias,
        sum_down,
        sum_down_bias,
    )


def solution(mesh):
    in_specs = (
        P("head", "blk", None),
        P(),
        P("head", "blk", None),
        P(),
        P(),
        P("blk", "head"),
        P(),
        P(),
        P(),
        P("blk", "head"),
        P(),
        P(),
        P(),
        P("blk", "head"),
        P(),
        P("blk", "head"),
        P(),
    )
    out_specs = (
        P("head", "blk", None),
        P("head", "blk", None),
        P(),
        P(),
        P("blk", "head"),
        P(),
        P(),
        P(),
        P("blk", "head"),
        P(),
        P(),
        P(),
        P("blk", "head"),
        P(),
        P("blk", "head"),
        P(),
    )
    return jax.shard_map(
        on_device, mesh=mesh, in_specs=in_specs, out_specs=out_specs, check_vma=False
    )
```

profile of v0, /device:TPU:0, one launch (start us, length us, event | category | flops | bytes accessed | tf_op | source)
XLA Modules:
  0.0 1622.3 jit_solution(2697163347062869119)
XLA Ops:
  17.7 20.5 %all-gather.11.cloned.1.call-done = bf16[4,128,2048]{2,1,0:T(8,128)(2,1)} async-done(((bf16[1,128,2048]{2,1,0:T(8,128)(2,1)}), bf16[4,128,2048]{2,1,0:T(8,128)(2,1)}) %all-gather.11.cloned.1.call-update) | async-done | bytes 2097168 | tf_op jit(solution)/shard_map/all_gather | solution.py:176
  38.2 51.4 %all-gather.13.cloned.1.call-done = bf16[2048,512]{1,0:T(8,128)(2,1)} async-done(((bf16[256,512]{1,0:T(8,128)(2,1)}), bf16[2048,512]{1,0:T(8,128)(2,1)}) %all-gather.13.cloned.1.call-update) | async-done | bytes 2097168 | tf_op jit(solution)/shard_map/all_gather | solution.py:167
  93.4 54.6 %all-gather.27.cloned.1.call-done = bf16[4096,256]{1,0:T(8,128)(2,1)} async-done(((bf16[128,256]{1,0:T(8,128)(2,1)}), bf16[4096,256]{1,0:T(8,128)(2,1)}) %all-gather.27.cloned.1.call-update) | async-done | bytes 2097168 | tf_op jit(solution)/shard_map/all_gather | solution.py:179
  159.0 39.3 %all-gather.15.cloned.1.call-done = bf16[2048,512]{1,0:T(8,128)(2,1)} async-done(((bf16[256,512]{1,0:T(8,128)(2,1)}), bf16[2048,512]{1,0:T(8,128)(2,1)}) %all-gather.15.cloned.1.call-update) | async-done | bytes 2097168 | tf_op jit(solution)/shard_map/all_gather | solution.py:168
  203.3 29.4 %reduce-scatter.10.cloned.1.call-done = bf16[1,128,2048]{2,1,0:T(8,128)(2,1)} async-done(((bf16[4,128,2048]{2,1,0:T(8,128)(2,1)}), bf16[1,128,2048]{2,1,0:T(8,128)(2,1)}) %reduce-scatter.10.cloned.1.call-update) | async-done | bytes 524304 | tf_op jit(solution)/shard_map/reduce_scatter | solution.py:196
  240.5 16.4 %all-gather.23.cloned.1.call-done = bf16[4,128,2048]{2,1,0:T(8,128)(2,1)} async-done(((bf16[1,128,2048]{2,1,0:T(8,128)(2,1)}), bf16[4,128,2048]{2,1,0:T(8,128)(2,1)}) %all-gather.23.cloned.1.call-update) | async-done | bytes 2097168 | tf_op jit(solution)/shard_map/all_gather | solution.py:177
  260.0 21.7 %all-gather.17.cloned.1.call-done = bf16[4,128,2048]{2,1,0:T(8,128)(2,1)} async-done(((bf16[1,128,2048]{2,1,0:T(8,128)(2,1)}), bf16[4,128,2048]{2,1,0:T(8,128)(2,1)}) %all-gather.17.cloned.1.call-update) | async-done | bytes 2097168 | tf_op jit(solution)/shard_map/all_gather | solution.py:204
  281.7 127.3 %all-gather.19.cloned.1.call-done = bf16[2048,2048]{1,0:T(8,128)(2,1)} async-done(((bf16[256,2048]{1,0:T(8,128)(2,1)}), bf16[2048,2048]{1,0:T(8,128)(2,1)}) %all-gather.19.cloned.1.call-update) | async-done | bytes 8388624 | tf_op jit(solution)/shard_map/all_gather | solution.py:169
  419.5 115.0 %all-gather.21.cloned.1.call-done = bf16[2048,2048]{1,0:T(8,128)(2,1)} async-done(((bf16[256,2048]{1,0:T(8,128)(2,1)}), bf16[2048,2048]{1,0:T(8,128)(2,1)}) %all-gather.21.cloned.1.call-update) | async-done | bytes 8388624 | tf_op jit(solution)/shard_map/all_gather | solution.py:170
  534.5 12.2 convert_reduce_fusion
  552.7 11.3 convolution_convert_fusion.6
  565.4 16.9 %reduce-scatter.14.cloned.1.call-done = bf16[1,128,2048]{2,1,0:T(8,128)(2,1)} async-done(((bf16[4,128,2048]{2,1,0:T(8,128)(2,1)}), bf16[1,128,2048]{2,1,0:T(8,128)(2,1)}) %reduce-scatter.14.cloned.1.call-update) | async-done | bytes 524304 | tf_op jit(solution)/shard_map/reduce_scatter | solution.py:234
  586.9 29.4 %reduce-scatter.12.cloned.1.call-done = bf16[1,128,2048]{2,1,0:T(8,128)(2,1)} async-done(((bf16[4,128,2048]{2,1,0:T(8,128)(2,1)}), bf16[1,128,2048]{2,1,0:T(8,128)(2,1)}) %reduce-scatter.12.cloned.1.call-update) | async-done | bytes 524304 | tf_op jit(solution)/shard_map/reduce_scatter | solution.py:210
  622.2 20.6 %all-gather.25.cloned.1.call-done = bf16[4,128,2048]{2,1,0:T(8,128)(2,1)} async-done(((bf16[1,128,2048]{2,1,0:T(8,128)(2,1)}), bf16[4,128,2048]{2,1,0:T(8,128)(2,1)}) %all-gather.25.cloned.1.call-update) | async-done | bytes 2097168 | tf_op jit(solution)/shard_map/all_gather | solution.py:243
  651.4 31.6 %while.39 = (s32[]{:T(128)}, f32[4,128,4,128]{3,1,2,0:T(8,128)}, f32[8,4,128,256]{3,2,1,0:T(8,128)}, s32[]{:T(128)}, s32[4]{0:T(128)S(1)}, /*index=5*/bf16[8,4,1...) while((s32[]{:T(128)}, f32[4,128,4,128]{3,1,2,0:T(8,128)}, ...), condition=%wide.region_17.18_spmd.clone, body=%wide.region_16.17_spmd.clone.sunk | while | flops 1354828416 | bytes 86412648 | solution.py:128
  708.5 10.8 convolution_convert_fusion
  720.1 135.7 %reduce-scatter.18.cloned.1.call-done = f32[1,128,256]{2,1,0:T(8,128)} async-done(((f32[32,128,256]{2,1,0:T(8,128)}), f32[1,128,256]{2,1,0:T(8,128)}) %reduce-scatter.18.cloned.1.call-update) | async-done | bytes 131088 | tf_op jit(solution)/shard_map/reduce_scatter | solution.py:262
  857.3 29.0 %reduce-scatter.16.cloned.1.call-done = bf16[1,128,2048]{2,1,0:T(8,128)(2,1)} async-done(((bf16[4,128,2048]{2,1,0:T(8,128)(2,1)}), bf16[1,128,2048]{2,1,0:T(8,128)(2,1)}) %reduce-scatter.16.cloned.1.call-update) | async-done | bytes 524304 | tf_op jit(solution)/shard_map/reduce_scatter | solution.py:272
  893.9 64.2 %reduce-scatter.20.cloned.1.call-done = bf16[256,512]{1,0:T(8,128)(2,1)} async-done(((bf16[2048,512]{1,0:T(8,128)(2,1)}), bf16[256,512]{1,0:T(8,128)(2,1)}) %reduce-scatter.20.cloned.1.call-update) | async-done | bytes 262160 | tf_op jit(solution)/shard_map/reduce_scatter | solution.py:292
  959.9 68.4 %reduce-scatter.22.cloned.1.call-done = bf16[256,512]{1,0:T(8,128)(2,1)} async-done(((bf16[2048,512]{1,0:T(8,128)(2,1)}), bf16[256,512]{1,0:T(8,128)(2,1)}) %reduce-scatter.22.cloned.1.call-update) | async-done | bytes 262160 | tf_op jit(solution)/shard_map/reduce_scatter | solution.py:295
  1030.0 149.7 %reduce-scatter.24.cloned.1.call-done = bf16[256,2048]{1,0:T(8,128)(2,1)} async-done(((bf16[2048,2048]{1,0:T(8,128)(2,1)}), bf16[256,2048]{1,0:T(8,128)(2,1)}) %reduce-scatter.24.cloned.1.call-update) | async-done | bytes 1048592 | tf_op jit(solution)/shard_map/reduce_scatter | solution.py:298
  1182.5 149.2 %reduce-scatter.26.cloned.1.call-done = bf16[256,2048]{1,0:T(8,128)(2,1)} async-done(((bf16[2048,2048]{1,0:T(8,128)(2,1)}), bf16[256,2048]{1,0:T(8,128)(2,1)}) %reduce-scatter.26.cloned.1.call-update) | async-done | bytes 1048592 | tf_op jit(solution)/shard_map/reduce_scatter | solution.py:301
  1334.5 129.1 %all-reduce.7.cloned.1.call-done = (f32[2048]{0:T(1024)}, f32[2048]{0:T(1024)}, f32[2048]{0:T(1024)}, f32[128]{0:T(128)}, f32[2048]{0:T(1024)}, /*index=5*/f32[2...) async-done(((f32[2048]{0:T(1024)}, f32[2048]{0:T(1024)}, f32[2048]{0:T(1024)}, f32[128]{0:T(128)}, f32[2048]{0:T(1024)}, /*index=5*/f32[2048]{0:T(1024)}, ...) | async-done | bytes 90640 | tf_op jit(solution)/shard_map/psum | solution.py:316
  1463.6 140.9 %all-reduce.5.cloned.1.call-done = f32[2048,256]{1,0:T(8,128)} async-done(((f32[2048,256]{1,0:T(8,128)}), f32[2048,256]{1,0:T(8,128)}) %all-reduce.5.cloned.1.call-update) | async-done | bytes 2097168 | tf_op jit(solution)/shard_map/psum | solution.py:316
  (223 shorter events, 171.1 us)
Async XLA Ops:
  7.2 31.0 %all-gather.11.cloned.1.call-start = ((), (), s32[]{:S(2)}) async-start(), calls=%async_computation.9 | async-start | bytes 2621440 | tf_op jit(solution)/shard_map/all_gather | solution.py:176
  12.7 76.9 %all-gather.13.cloned.1.call-start = ((), (), s32[]{:S(2)}) async-start(), calls=%async_computation.10 | async-start | bytes 2359296 | tf_op jit(solution)/shard_map/all_gather | solution.py:167
  13.5 134.5 %all-gather.27.cloned.1.call-start = ((), (), s32[]{:S(2)}) async-start(), calls=%async_computation.27 | async-start | bytes 2162688 | tf_op jit(solution)/shard_map/all_gather | solution.py:179
  16.3 182.0 %all-gather.15.cloned.1.call-start = ((), (), s32[]{:S(2)}) async-start(), calls=%async_computation.11 | async-start | bytes 2359296 | tf_op jit(solution)/shard_map/all_gather | solution.py:168
  16.9 215.8 %reduce-scatter.10.cloned.1.call-start = ((), (), s32[]{:S(2)}) async-start(), calls=%async_computation.12 | async-start | bytes 2621440 | tf_op jit(solution)/shard_map/reduce_scatter | solution.py:196
  202.7 54.2 %all-gather.23.cloned.1.call-start = ((), (), s32[]{:S(2)}) async-start(), calls=%async_computation.17 | async-start | bytes 2621440 | tf_op jit(solution)/shard_map/all_gather | solution.py:177
  203.3 78.4 %all-gather.17.cloned.1.call-start = ((), (), s32[]{:S(2)}) async-start(), calls=%async_computation.13 | async-start | bytes 2621440 | tf_op jit(solution)/shard_map/all_gather | solution.py:204
  237.7 171.3 %all-gather.19.cloned.1.call-start = ((), (), s32[]{:S(2)}) async-start(), calls=%async_computation.14 | async-start | bytes 9437184 | tf_op jit(solution)/shard_map/all_gather | solution.py:169
  238.4 296.1 %all-gather.21.cloned.1.call-start = ((), (), s32[]{:S(2)}) async-start(), calls=%async_computation.15 | async-start | bytes 9437184 | tf_op jit(solution)/shard_map/all_gather | solution.py:170
  239.2 343.1 %reduce-scatter.14.cloned.1.call-start = ((), (), s32[]{:S(2)}) async-start(), calls=%async_computation.18 | async-start | bytes 2621440 | tf_op jit(solution)/shard_map/reduce_scatter | solution.py:234
  552.5 63.8 %reduce-scatter.12.cloned.1.call-start = ((), (), s32[]{:S(2)}) async-start(), calls=%async_computation.16 | async-start | bytes 2621440 | tf_op jit(solution)/shard_map/reduce_scatter | solution.py:210
  564.1 78.7 %all-gather.25.cloned.1.call-start = ((), (), s32[]{:S(2)}) async-start(), calls=%async_computation.19 | async-start | bytes 2621440 | tf_op jit(solution)/shard_map/all_gather | solution.py:243
  620.1 235.7 %reduce-scatter.18.cloned.1.call-start = ((), (), s32[]{:S(2)}) async-start(), calls=%async_computation.21 | async-start | bytes 4325376 | tf_op jit(solution)/shard_map/reduce_scatter | solution.py:262
  683.0 203.2 %reduce-scatter.16.cloned.1.call-start = ((), (), s32[]{:S(2)}) async-start(), calls=%async_computation.20 | async-start | bytes 2621440 | tf_op jit(solution)/shard_map/reduce_scatter | solution.py:272
  688.8 269.2 %reduce-scatter.20.cloned.1.call-start = ((), (), s32[]{:S(2)}) async-start(), calls=%async_computation.22 | async-start | bytes 2359296 | tf_op jit(solution)/shard_map/reduce_scatter | solution.py:292
  693.5 334.7 %reduce-scatter.22.cloned.1.call-start = ((), (), s32[]{:S(2)}) async-start(), calls=%async_computation.24 | async-start | bytes 2359296 | tf_op jit(solution)/shard_map/reduce_scatter | solution.py:295
  698.2 481.6 %reduce-scatter.24.cloned.1.call-start = ((), (), s32[]{:S(2)}) async-start(), calls=%async_computation.25 | async-start | bytes 9437184 | tf_op jit(solution)/shard_map/reduce_scatter | solution.py:298
  708.5 623.2 %reduce-scatter.26.cloned.1.call-start = ((), (), s32[]{:S(2)}) async-start(), calls=%async_computation.26 | async-start | bytes 9437184 | tf_op jit(solution)/shard_map/reduce_scatter | solution.py:301
  719.3 169.3 %copy-start.29 = (f32[128]{0:T(128)S(1)}, f32[128]{0:T(128)}, u32[]{:S(2)}) copy-start(f32[128]{0:T(128)} %copy-done.28) | copy-start | bytes 1540
  719.4 170.3 %copy-start.6 = (bf16[1,128,2048]{2,1,0:T(8,128)(2,1)S(1)}, bf16[1,128,2048]{2,1,0:T(8,128)(2,1)}, u32[]{:S(2)}) copy-start(bf16[1,128,2048]{2,1,0:T(8,128)(2,1)} %param.25) | copy-start | bytes 1572868
  719.4 744.2 %all-reduce.7.cloned.1.call-start = ((), (), s32[]{:S(2)}) async-start(), calls=%async_computation.28 | async-start | bytes 181248 | tf_op jit(solution)/shard_map/psum | solution.py:316
  719.8 172.2 %copy-start.16 = (f32[8192]{0:T(1024)}, f32[8192]{0:T(1024)S(1)}, u32[]{:S(2)}) copy-start(f32[8192]{0:T(1024)S(1)} %dynamic_update_slice.10) | copy-start | bytes 98308
  720.1 171.9 %copy-start.19 = (f32[2048]{0:T(1024)}, f32[2048]{0:T(1024)S(1)}, u32[]{:S(2)}) copy-start(f32[2048]{0:T(1024)S(1)} %bitcast_dynamic-update-slice_fusion) | copy-start | bytes 24580
  892.0 712.5 %all-reduce.5.cloned.1.call-start = ((), (), s32[]{:S(2)}) async-start(), calls=%async_computation.23 | async-start | bytes 4194304 | tf_op jit(solution)/shard_map/psum | solution.py:316
  (31 other events, 2195.4 us)
Sparse Core Ops, SparseCore 0:
  12.9 25.2 all-gather.10
  40.3 49.2 all-gather.12
  93.1 54.8 all-gather.26
  150.0 48.3 all-gather.14
  202.8 29.8 reduce-scatter.9
  234.2 22.5 all-gather.22
  259.1 22.5 all-gather.16
  284.0 124.9 all-gather.18
  411.3 123.1 all-gather.20
  552.6 29.6 reduce-scatter.13
  584.8 31.4 reduce-scatter.11
  620.2 22.5 all-gather.24
  683.2 172.5 reduce-scatter.17
  858.9 27.2 reduce-scatter.15
  890.2 67.8 reduce-scatter.19
  961.4 66.7 reduce-scatter.21
  1031.7 147.9 reduce-scatter.23
  1183.7 147.9 reduce-scatter.25
  1339.3 124.2 all-reduce.6
  1469.6 134.8 all-reduce.4
where the time goes:
time: 1630 us; the launch traced here: 1620 us
  waiting for transfers between devices  1410 us (87%)
  matrix products  112 us (7%)
  other arithmetic  43.2 us (3%)
  local copies, waits for them, and re-layouts  38 us (2%)
    psum x2, waiting for transfers between devices, on_device(): lax.psum((grad_ln1_gain, grad_ln1_bias, q_bias_full, grad_kv, grad_v_bias...  270 us
    reduce_scatter x1, waiting for transfers between devices, on_device(): lax.psum_scatter(grad_up.astype(jnp.bfloat16), 'blk', scatter_dimension=0...  150 us
    reduce_scatter x1, waiting for transfers between devices, on_device(): lax.psum_scatter(grad_down.astype(jnp.bfloat16), 'blk', scatter_dimension...  149 us
    reduce_scatter x1, waiting for transfers between devices, on_device(): lax.psum_scatter(kv_grad.reshape(blk_count * head_count, seq_dev, 2 * HEA...  136 us
    all_gather x1, waiting for transfers between devices, on_device(): lax.all_gather(w_up, 'blk', axis=0, tiled=True)  127 us
    all_gather x1, waiting for transfers between devices, on_device(): lax.all_gather(w_down, 'blk', axis=0, tiled=True)  115 us
    reduce_scatter x1, waiting for transfers between devices, on_device(): lax.psum_scatter(grad_out.astype(jnp.bfloat16), 'blk', scatter_dimension=...  68.4 us
    reduce_scatter x1, waiting for transfers between devices, on_device(): lax.psum_scatter(grad_q.astype(jnp.bfloat16), 'blk', scatter_dimension=0,...  64.2 us
  transfers between devices with their start and end apart: 20, of which 20 were waited for; matrix products, arithmetic and copies ran while one was open for 7% of the time, Pallas kernels for 0%

commit v1 on v0

v1 whole, which is shorter than its diff:
```python
from functools import partial

import jax
import jax.numpy as jnp
from jax import lax
from jax.experimental import pallas as pl
from jax.experimental.pallas import tpu as pltpu
from jax.sharding import PartitionSpec as P

HEADS = 16
HEAD_DIM = 128
EPSILON = 1e-05
SCALE = HEAD_DIM ** (-0.5)
LOW = jnp.bfloat16


def layer_norm(values, gain, bias):
    center = values - jnp.mean(values, axis=-1, keepdims=True)
    spread = jnp.mean(center * center, axis=-1, keepdims=True)
    return center * lax.rsqrt(spread + EPSILON) * gain + bias


def plain_dot(left, right):
    return jnp.dot(left, right, preferred_element_type=jnp.float32)


def row_dot(left, right):
    return lax.dot_general(
        left, right, (((0,), (0,)), ((), ())), preferred_element_type=jnp.float32
    )


def col_dot(left, right):
    return lax.dot_general(
        left, right, (((1,), (1,)), ((), ())), preferred_element_type=jnp.float32
    )


def wide(values):
    return values.astype(jnp.float32)


def low(values):
    return values.astype(LOW)


def rounded(values):
    return lax.reduce_precision(values, 8, 7)


def flip(values, blk_bits=0, head_bits=0):
    blk_count = lax.axis_size("blk")
    head_count = lax.axis_size("head")
    pairs = [
        (b * head_count + h, (b ^ blk_bits) * head_count + (h ^ head_bits))
        for b in range(blk_count)
        for h in range(head_count)
    ]
    return lax.ppermute(values, ("blk", "head"), pairs)


def in_order(own, other, index, axis):
    first = index == 0
    return jnp.stack([jnp.where(first, own, other), jnp.where(first, other, own)], axis=axis)


def tie(*values):
    return lax.optimization_barrier(values)


def take(values, index, axis):
    return lax.dynamic_index_in_dim(values, index, axis, keepdims=False)


def stacked(ref, heads):
    return jnp.concatenate(
        [ref[:, h * HEAD_DIM : (h + 1) * HEAD_DIM] for h in range(heads)], axis=0
    )


def probabilities(query, key, key_pos, start, length, seq_dev):
    raw = col_dot(query, key) * SCALE
    row = lax.broadcasted_iota(jnp.int32, (query.shape[0], 1), 0)
    row_pos = start + row % seq_dev
    limit = jnp.minimum(row_pos, length - 1)
    masked = jnp.where(key_pos <= limit, raw, -1e30)
    weights = jnp.exp(masked - jnp.max(masked, axis=-1, keepdims=True))
    return weights * (1.0 / jnp.sum(weights, axis=-1, keepdims=True))


def forward_kernel(heads, scalars, q_ref, kv_ref, pos_ref, o_ref):
    seq_dev = q_ref.shape[0]
    key = kv_ref[0, :, :HEAD_DIM]
    value = kv_ref[0, :, HEAD_DIM:]
    prob = probabilities(
        stacked(q_ref, heads),
        key,
        pos_ref[...],
        scalars[0],
        scalars[1 + pl.program_id(0)],
        seq_dev,
    )
    out = plain_dot(prob.astype(LOW), value).astype(LOW)
    for h in range(heads):
        o_ref[:, h * HEAD_DIM : (h + 1) * HEAD_DIM] = out[h * seq_dev : (h + 1) * seq_dev]


def backward_kernel(heads, scalars, q_ref, go_ref, kv_ref, pos_ref, gq_ref, gkv_ref):
    seq_dev = q_ref.shape[0]
    key = kv_ref[0, :, :HEAD_DIM]
    value = kv_ref[0, :, HEAD_DIM:]
    query = stacked(q_ref, heads)
    grad = stacked(go_ref, heads)
    prob = probabilities(
        query,
        key,
        pos_ref[...],
        scalars[0],
        scalars[1 + pl.program_id(0)],
        seq_dev,
    )
    prob_low = prob.astype(LOW)
    prob_grad = col_dot(grad, value)
    delta = jnp.sum(wide(prob_low) * prob_grad, axis=-1, keepdims=True)
    score_grad = (prob * (prob_grad - delta)).astype(LOW)
    out = (plain_dot(score_grad, key) * SCALE).astype(LOW)
    for h in range(heads):
        gq_ref[:, h * HEAD_DIM : (h + 1) * HEAD_DIM] = out[h * seq_dev : (h + 1) * seq_dev]
    key_grad = row_dot(score_grad, query) * SCALE
    value_grad = row_dot(prob_low, grad)

    @pl.when(pl.program_id(1) == 0)
    def _():
        gkv_ref[0, :, :HEAD_DIM] = key_grad
        gkv_ref[0, :, HEAD_DIM:] = value_grad

    @pl.when(pl.program_id(1) > 0)
    def _():
        gkv_ref[0, :, :HEAD_DIM] += key_grad
        gkv_ref[0, :, HEAD_DIM:] += value_grad


def attention_call(kernel, outs, scalars, rows, keys, key_pos, seq_dev, flops):
    slots, key_count, _ = keys.shape
    heads_dev = rows[0].shape[1] // HEAD_DIM
    heads = max(1, min(heads_dev, heads_dev * 1024 // key_count))
    row_spec = pl.BlockSpec((seq_dev, heads * HEAD_DIM), lambda s, g, *_: (s, g))
    key_spec = pl.BlockSpec((1, key_count, 2 * HEAD_DIM), lambda s, g, *_: (s, 0, 0))
    pos_spec = pl.BlockSpec((1, key_count), lambda s, g, *_: (0, 0))
    shapes = {
        "row": (jax.ShapeDtypeStruct(rows[0].shape, LOW), row_spec),
        "key": (jax.ShapeDtypeStruct(keys.shape, jnp.float32), key_spec),
    }
    return pl.pallas_call(
        partial(kernel, heads),
        grid_spec=pltpu.PrefetchScalarGridSpec(
            num_scalar_prefetch=1,
            grid=(slots, heads_dev // heads),
            in_specs=[row_spec] * len(rows) + [key_spec, pos_spec],
            out_specs=[shapes[o][1] for o in outs],
        ),
        out_shape=[shapes[o][0] for o in outs],
        compiler_params=pltpu.CompilerParams(vmem_limit_bytes=50 * 1024 * 1024),
        cost_estimate=pl.CostEstimate(
            flops=flops * slots * heads_dev * seq_dev * key_count * HEAD_DIM * 2,
            bytes_accessed=8 * 1024 * 1024,
            transcendentals=slots * heads_dev * seq_dev * key_count,
        ),
    )(scalars, *rows, keys, key_pos)


def on_device(
    block_in,
    lengths,
    out_cot,
    ln1_gain,
    ln1_bias,
    w_q,
    b_q,
    w_kv,
    b_v,
    w_out,
    b_out,
    ln2_gain,
    ln2_bias,
    w_up,
    b_up,
    w_down,
    b_down,
):
    blk_count = lax.axis_size("blk")
    blk = lax.axis_index("blk")
    head = lax.axis_index("head")
    z_count = blk_count // 2
    z, x = blk // 2, blk % 2
    y, core = head // 2, head % 2
    slots = lax.axis_size("head")
    seq_dev = block_in.shape[1]
    width = block_in.shape[2]
    depth = w_q.shape[0]
    q_dev = w_q.shape[1]
    ff_dev = w_up.shape[1]
    unit = ff_dev // 2
    part_unit = unit // 2
    plane = [(1, 0), (0, 2), (1, 2)]
    z_groups = [[2 * i + j for i in range(z_count)] for j in range(2)]

    def gather_z(values):
        return lax.all_gather(values, "blk", axis=0, axis_index_groups=z_groups)

    def scatter_z(values):
        return lax.psum_scatter(
            values, "blk", scatter_dimension=0, axis_index_groups=z_groups
        )

    def gather_head(values):
        pair = jnp.stack([values, flip(values, head_bits=2)])
        other = flip(pair, head_bits=1)
        return jnp.stack([pair, other], axis=1).reshape((slots,) + values.shape)

    def head_core(values):
        parts = values.reshape((2, 2) + values.shape[1:])
        return wide(parts[:, 0]) + wide(flip(low(parts[:, 1]), head_bits=1))

    def head_y(half):
        return half[0] + wide(flip(low(half[1]), head_bits=2))

    def scatter_head(values):
        return head_y(head_core(values))

    def gather_xy(values):
        return jnp.stack([values] + [flip(values, *bits) for bits in plane])

    def gather_core(mine):
        return jnp.concatenate([mine, flip(mine, head_bits=1)]).reshape(-1, width)

    def plane_core(values):
        parts = values.reshape((2, 4, seq_dev, width))
        return parts[0] + wide(flip(low(parts[1]), head_bits=1))

    def plane_xy(half):
        total = half[0]
        for i, bits in enumerate(plane):
            total = total + wide(flip(low(half[i + 1]), *bits))
        return total

    def swap_units(weights):
        own = lax.dynamic_slice_in_dim(weights, x * unit, unit, 1)
        other = lax.dynamic_slice_in_dim(weights, (1 - x) * unit, unit, 1)
        return in_order(own, flip(other, blk_bits=1), x, 0).reshape(2 * depth, unit)

    def gather_x(mine):
        return in_order(mine, flip(mine, blk_bits=1), x, 1).reshape(width, -1)

    mine = gather_z(jnp.concatenate([w_q, w_out]))
    mine_q, mine_out = mine[:, :depth], mine[:, depth:]
    full_q = gather_x(mine_q)
    def gather_units(weights):
        mine = swap_units(weights)
        return [
            gather_z(mine[:, i * part_unit : (i + 1) * part_unit]).reshape(width, part_unit)
            for i in range(2)
        ]

    full_up = gather_units(w_up)
    full_down = gather_units(w_down)

    own_rows = wide(block_in[0])
    positions = jnp.arange(seq_dev, dtype=jnp.int32)
    own_valid = blk * seq_dev + positions < lengths[head]
    attn_in = layer_norm(own_rows, ln1_gain, ln1_bias).astype(LOW)
    value_bias = jnp.concatenate([jnp.zeros((HEAD_DIM,), jnp.float32), b_v])
    keys = (plain_dot(attn_in, w_kv) + value_bias).astype(LOW)[None]
    bit = blk_count // 2
    while bit:
        keys = jnp.stack([keys, flip(keys, blk_bits=bit)], axis=1)
        keys = keys.reshape((-1,) + keys.shape[2:])
        bit //= 2
    keys = gather_head(keys).reshape(slots, blk_count * seq_dev, 2 * HEAD_DIM)
    key_blocks = blk ^ jnp.arange(blk_count, dtype=jnp.int32)
    key_pos = (key_blocks[:, None] * seq_dev + positions[None, :]).reshape(1, -1)
    slot_ids = head ^ jnp.arange(slots, dtype=jnp.int32)
    scalars = jnp.concatenate([(blk * seq_dev)[None], lengths[slot_ids]]).astype(jnp.int32)
    group_in = gather_head(attn_in).reshape(slots * seq_dev, width)

    own_cot = jnp.where(own_valid[:, None], out_cot[0], jnp.zeros_like(out_cot[0]))
    cot_rows = gather_core(gather_xy(own_cot))
    own_cot = wide(own_cot)

    column_start = head * q_dev
    query_bias = lax.dynamic_slice_in_dim(b_q, column_start, q_dev)
    queries = (plain_dot(group_in, full_q) + query_bias).astype(LOW)
    queries, mine_out = tie(queries, mine_out)
    full_out = gather_x(mine_out)
    (attn_low,) = attention_call(
        forward_kernel, ("row",), scalars, (queries,), keys, key_pos, seq_dev, 2
    )
    attn_low, full_up[0] = tie(attn_low, full_up[0])
    attn_part = col_dot(attn_low, full_out).reshape(slots, seq_dev, width)
    hidden_res = own_rows + scatter_head(attn_part) + b_out

    hidden_res, full_up[1] = tie(hidden_res, full_up[1])
    normed_two = layer_norm(hidden_res, ln2_gain, ln2_bias).astype(LOW)
    mine_in, full_down[0] = tie(gather_xy(normed_two), full_down[0])
    ffn_in = gather_core(mine_in)
    unit_start = head * ff_dev + x * unit

    def gelu(i):
        bias = lax.dynamic_slice_in_dim(b_up, unit_start + i * part_unit, part_unit)
        value, pull = jax.vjp(
            partial(jax.nn.gelu, approximate=True), plain_dot(ffn_in, full_up[i]) + bias
        )
        return low(value), pull

    def scatter_units(grads):
        return scatter_z(grads.reshape(z_count, 2 * depth, part_unit))

    activated, gelu_pulls = zip(*[gelu(i) for i in range(2)])
    activated = tie(*activated)
    grad_down = [low(row_dot(cot_rows, v)) for v in activated]
    *grad_down, full_down[1] = tie(*grad_down, full_down[1])
    sums_down = [scatter_units(v) for v in grad_down]
    grad_up_rows = [
        low(gelu_pulls[i](plain_dot(cot_rows, full_down[i]))[0]) for i in range(2)
    ]
    ffn_in_grad = plane_core(sum(col_dot(grad_up_rows[i], full_up[i]) for i in range(2)))
    ffn_in_grad = plane_xy(ffn_in_grad)
    ffn_part = plane_core(sum(col_dot(activated[i], full_down[i]) for i in range(2)))
    grad_up = [low(row_dot(ffn_in, v)) for v in grad_up_rows]
    ffn_in_grad, ffn_part, sums_down[0], *grad_up = tie(
        ffn_in_grad, ffn_part, sums_down[0], *grad_up
    )
    sums_up = [scatter_units(v) for v in grad_up]
    grad_up_bias = jnp.concatenate(
        [jnp.sum(v, axis=0, dtype=jnp.float32) for v in grad_up_rows]
    )

    norm_two_value, norm_two_pull = jax.vjp(layer_norm, hidden_res, ln2_gain, ln2_bias)
    res_grad, grad_ln2_gain, grad_ln2_bias = norm_two_pull(ffn_in_grad)
    res_total = own_cot + res_grad

    cot_attn = gather_head(res_total.astype(LOW)).reshape(slots * seq_dev, width)
    cot_attn, sums_down[1], ffn_part = tie(cot_attn, sums_down[1], ffn_part)
    output = low(hidden_res + plane_xy(ffn_part) + b_down)[None]
    attn_grad = plain_dot(cot_attn, full_out).astype(LOW)
    query_low, kv_grad = attention_call(
        backward_kernel,
        ("row", "key"),
        scalars,
        (queries, attn_grad),
        keys,
        key_pos,
        seq_dev,
        5,
    )
    query_low, kv_grad, output = tie(query_low, kv_grad, output)
    half_kv = head_core(kv_grad.reshape(slots, blk_count, seq_dev, 2 * HEAD_DIM))
    half_kv, cot_late, in_late = tie(half_kv, cot_attn, group_in)

    def sides(grads):
        parts = grads.reshape(z_count, 2, depth, q_dev)
        return take(parts, x, 1), low(take(parts, 1 - x, 1))

    grad_out, out_across = sides(row_dot(cot_late, attn_low))
    grad_q, q_across = sides(row_dot(in_late, query_low))
    out_across = flip(out_across, blk_bits=1)
    part, sums_up[0], grad_out, grad_q, q_across = tie(
        head_y(half_kv), sums_up[0], grad_out, grad_q, q_across
    )
    sum_out = wide(scatter_z(low(grad_out + wide(out_across))))
    bit = 1
    while bit < blk_count:
        pair = part.reshape((-1, 2) + part.shape[1:])
        part = pair[:, 0] + wide(flip(low(pair[:, 1]), blk_bits=bit))
        if bit == 1:
            part, q_across = tie(part, q_across)
            q_across = flip(q_across, blk_bits=1)
        bit *= 2
    own_kv_grad = low(part[0])
    sum_q = wide(scatter_z(low(grad_q + wide(q_across))))
    attn_in_grad = col_dot(query_low, full_q).reshape(slots, seq_dev, width)
    norm_one_grad = scatter_head(attn_in_grad) + col_dot(own_kv_grad, w_kv)
    norm_one_value, norm_one_pull = jax.vjp(layer_norm, own_rows, ln1_gain, ln1_bias)
    input_part, grad_ln1_gain, grad_ln1_bias = norm_one_pull(norm_one_grad)
    input_grad = res_total + input_part

    def ff_sum(sums):
        parts = jnp.concatenate(sums, axis=-1).reshape(2, depth, unit)
        own, other = take(parts, x, 0), flip(take(parts, 1 - x, 0), blk_bits=1)
        first = x == 0
        return wide(
            jnp.concatenate([jnp.where(first, own, other), jnp.where(first, other, own)], axis=-1)
        )

    sum_down = ff_sum(sums_down)

    grad_kv = row_dot(attn_in, own_kv_grad)
    grad_b_q = lax.dynamic_update_slice_in_dim(
        jnp.zeros((width,), jnp.float32),
        jnp.sum(query_low, axis=0, dtype=jnp.float32),
        column_start,
        0,
    )
    grad_b_up = lax.dynamic_update_slice_in_dim(jnp.zeros_like(b_up), grad_up_bias, unit_start, 0)
    grad_b_v = jnp.sum(own_kv_grad[:, HEAD_DIM:], axis=0, dtype=jnp.float32)
    lines = jnp.concatenate(
        [
            jnp.stack(
                [
                    grad_ln1_gain,
                    grad_ln1_bias,
                    grad_b_q,
                    jnp.sum(res_total, axis=0),
                    grad_ln2_gain,
                    grad_ln2_bias,
                    jnp.sum(own_cot, axis=0),
                    jnp.pad(grad_b_v, (0, width - HEAD_DIM)),
                ]
            ),
            grad_b_up.reshape(-1, width),
        ]
    ).reshape(-1, 2 * HEAD_DIM)
    line_count = lines.shape[0]

    def exchange(lines, rows, **bits):
        first = rounded(lines)
        second = rounded(lines - first)
        got = flip(jnp.concatenate([low(first), low(second), low(rows)]), **bits)
        lines = (first + second) + (wide(got[:line_count]) + wide(got[line_count : 2 * line_count]))
        return lines, wide(got[2 * line_count :])

    def halved(lines, rows, index, **bits):
        pair = rows.reshape((2, -1) + rows.shape[1:])
        lines, got = exchange(lines, take(pair, 1 - index, 0), **bits)
        return lines, take(pair, index, 0) + got

    def joined(values, index, **bits):
        whole = in_order(values, flip(values, **bits), index, 0)
        return whole.reshape((-1,) + values.shape[1:])

    lines, rows = halved(lines, grad_kv, core, head_bits=1)
    lines, rows = halved(lines, rows, x, blk_bits=1)
    rows, sums_up[1] = tie(rows, sums_up[1])
    sum_up = ff_sum(sums_up)
    lines, rows = halved(lines, rows, y, head_bits=2)
    bit = 2
    while bit < blk_count:
        lines, got = exchange(lines, rows, blk_bits=bit)
        rows = rounded(rows) + got
        bit *= 2
    rows = joined(low(rows), y, head_bits=2)
    rows = joined(rows, x, blk_bits=1)
    sum_kv = wide(joined(rows, core, head_bits=1))
    lines = lines.reshape(-1, width)
    (
        sum_ln1_gain,
        sum_ln1_bias,
        sum_q_bias,
        sum_out_bias,
        sum_ln2_gain,
        sum_ln2_bias,
        sum_down_bias,
        sum_v_bias,
    ) = lines[:8]
    sum_v_bias = sum_v_bias[:HEAD_DIM]
    sum_up_bias = lines[8:].reshape(-1)
    return (
        output,
        input_grad[None],
        sum_ln1_gain,
        sum_ln1_bias,
        sum_q,
        sum_q_bias,
        sum_kv,
        sum_v_bias,
        sum_out,
        sum_out_bias,
        sum_ln2_gain,
        sum_ln2_bias,
        sum_up,
        sum_up_bias,
        sum_down,
        sum_down_bias,
    )


def solution(mesh):
    rows = P("head", "blk", None)
    weights = P("blk", "head")
    in_specs = (
        rows,
        P(),
        rows,
        P(),
        P(),
        weights,
        P(),
        P(),
        P(),
        weights,
        P(),
        P(),
        P(),
        weights,
        P(),
        weights,
        P(),
    )
    out_specs = (
        rows,
        rows,
        P(),
        P(),
        weights,
        P(),
        P(),
        P(),
        weights,
        P(),
        P(),
        P(),
        weights,
        P(),
        weights,
        P(),
    )
    return jax.shard_map(
        on_device, mesh=mesh, in_specs=in_specs, out_specs=out_specs, check_vma=False
    )
```

time: 1630 us -> 560 us (0.34)
  waiting for transfers between devices: 1410 us -> 243 us
  other arithmetic: 43.2 us -> 97.4 us
  matrix products: 112 us -> 59.6 us
  starting transfers between devices: 1.7 us -> 50.2 us
  local copies, waits for them, and re-layouts: 38 us -> 65.4 us
  Pallas kernels: 0 us -> 18.2 us
    reduce_scatter x9 -> x6, waiting for transfers between devices: 672 us -> 1.01 us  [scatter_z(): lax.psum_scatter(values, 'blk', scatter_dimension=0, axis_index_groups=z_...]
    all_gather x9 -> x5, waiting for transfers between devices: 467 us -> 25.5 us  [gather_z(): return lax.all_gather(values, 'blk', axis=0, axis_index_groups=z_groups)]
    psum x2 -> x0, waiting for transfers between devices: 270 us -> none  [on_device(): lax.psum((grad_ln1_gain, grad_ln1_bias, q_bias_full, grad_kv, grad_v_bias...]
    ppermute x0 -> x50, waiting for transfers between devices: none -> 216 us  [flip(): return lax.ppermute(values, ('blk', 'head'), pairs)]
    ppermute x0 -> x50, starting transfers between devices: none -> 49.1 us  [flip(): return lax.ppermute(values, ('blk', 'head'), pairs)]
    another operation x0 -> x27, other arithmetic: none -> 31.3 us  [the longest x6 10.5 us: gather_head(): return jnp.stack([pair, other], axis=1).reshape((slots,) + values.shape)]
    dot_general x7 -> x0, matrix products: 20.9 us -> none  [the longest x2 5.64 us: tile_parts(): jnp.einsum('sqhd,bsjd->sqhbj', row_q, tile_keys, preferred_element_type=j...]
    pallas_call x0 -> x2, Pallas kernels: none -> 18.2 us  [attention_call(): pl.pallas_call(partial(kernel, heads), grid_spec=pltpu.PrefetchScalarGrid...]
  transfers between devices with their start and end apart: 20 -> 61, of which waited for: 20 -> 32; matrix products, arithmetic and copies ran while one was open for 7% -> 36% of each run, Pallas kernels for 0% -> 3%
where the time goes in v1:
time: 560 us; the launch traced here: 549 us
  waiting for transfers between devices  243 us (43%)
  other arithmetic  97.4 us (17%)
  local copies, waits for them, and re-layouts  65.4 us (12%)
  matrix products  59.6 us (11%)
  starting transfers between devices  50.2 us (9%)
  Pallas kernels  18.2 us (3%)
  between operations  15.7 us (3%)
    ppermute x50, waiting for transfers between devices, flip(): return lax.ppermute(values, ('blk', 'head'), pairs)  216 us
    ppermute x50, starting transfers between devices, flip(): return lax.ppermute(values, ('blk', 'head'), pairs)  49.1 us
    unnamed x178, local copies, waits for them, and re-layouts  33.8 us
    all_gather x5, waiting for transfers between devices, gather_z(): return lax.all_gather(values, 'blk', axis=0, axis_index_groups=z_groups)  25.5 us
    dot_general x7, matrix products, col_dot(): lax.dot_general(left, right, (((1,), (1,)), ((), ())), preferred_element_...  22.6 us
    dot_general x7, matrix products, row_dot(): lax.dot_general(left, right, (((0,), (0,)), ((), ())), preferred_element_...  18.8 us
    dot_general x7, matrix products, plain_dot(): return jnp.dot(left, right, preferred_element_type=jnp.float32)  18.2 us
    pallas_call x2, Pallas kernels, attention_call(): pl.pallas_call(partial(kernel, heads), grid_spec=pltpu.PrefetchScalarGrid...  18.2 us
  transfers between devices with their start and end apart: 61, of which 32 were waited for; matrix products, arithmetic and copies ran while one was open for 36% of the time, Pallas kernels for 3%

profile of v1, /device:TPU:0, one launch (start us, length us, event | category | flops | bytes accessed | tf_op | source)
XLA Modules:
  0.0 549.2 jit_solution(15560183036649827971)
XLA Ops:
  25.7 10.7 %collective-permute-done.8 = bf16[2,128,256]{2,1,0:T(8,128)(2,1)S(1)} collective-permute-done((bf16[2,128,256]{2,1,0:T(8,128)(2,1)S(1)}, bf16[2,128,256]{2,1,0:T(8,128)(2,1)S(1)}, u32[]{:S(2)}, u32[]{:S(2)}) %collective-permute-start.8) | collective-permute-done | bytes 131104 | tf_op jit(solution)/shard_map/ppermute | solution.py:59
  38.0 6.6 %collective-permute-done.12 = bf16[256,1024]{1,0:T(8,128)(2,1)} collective-permute-done((bf16[256,1024]{1,0:T(8,128)(2,1)}, bf16[256,1024]{1,0:T(8,128)(2,1)}, u32[]{:S(2)}, u32[]{:S(2)}) %collective-permute-start.12) | collective-permute-done | bytes 524320 | tf_op jit(solution)/shard_map/ppermute | solution.py:59
  50.9 9.4 %all-gather.11.cloned.1.call-done = bf16[2048,512]{1,0:T(8,128)(2,1)} async-done(((bf16[512,512]{1,0:T(8,128)(2,1)}), bf16[2048,512]{1,0:T(8,128)(2,1)}) %all-gather.11.cloned.1.call-update) | async-done | bytes 2097168 | tf_op jit(solution)/shard_map/all_gather | solution.py:209
  66.6 12.1 %collective-permute-done.10 = bf16[8,128,256]{2,1,0:T(8,128)(2,1)S(1)} collective-permute-done((bf16[8,128,256]{2,1,0:T(8,128)(2,1)S(1)}, bf16[8,128,256]{2,1,0:T(8,128)(2,1)S(1)}, u32[]{:S(2)}, u32[]{:S(2)}) %collective-permute-start.10) | collective-permute-done | bytes 524320 | tf_op jit(solution)/shard_map/ppermute | solution.py:59
  97.6 7.4 %shard_map.288 = bf16[512,512]{1,0:T(8,128)(2,1)S(1)} custom-call(s32[5]{0:T(128)S(1)} %pad_add_fusion.scalars, bf16[512,512]{1,0:T(8,128)(2,1)S(1)} %copy-done.4, bf16[4,1024,256]{2,1,0:T(8,128)(2,1)S(1)} %bitcast.408, s32[1,1024]{1,0:T(1,128)S(1)} %bitcast.411), custom_call_target="tpu_custom_call" | custom-call | flops 1073741824 | bytes 8388608 | tf_op jit(solution)/shard_map/pallas_call | solution.py:154
  107.1 10.3 %collective-permute-done.13 = bf16[4,256,512]{2,1,0:T(8,128)(2,1)} collective-permute-done((bf16[4,256,512]{2,1,0:T(8,128)(2,1)}, bf16[4,256,512]{2,1,0:T(8,128)(2,1)}, u32[]{:S(2)}, u32[]{:S(2)}) %collective-permute-start.13) | collective-permute-done | bytes 1048608 | tf_op jit(solution)/shard_map/ppermute | solution.py:59
  140.8 24.1 %collective-permute-done.15 = bf16[128,2048]{1,0:T(8,128)(2,1)} collective-permute-done((bf16[128,2048]{1,0:T(8,128)(2,1)}, bf16[128,2048]{1,0:T(8,128)(2,1)}, u32[]{:S(2)}, u32[]{:S(2)}) %collective-permute-start.15) | collective-permute-done | bytes 524320 | tf_op jit(solution)/shard_map/ppermute | solution.py:59
  178.9 7.2 %collective-permute-done.17 = bf16[128,2048]{1,0:T(8,128)(2,1)S(1)} collective-permute-done((bf16[128,2048]{1,0:T(8,128)(2,1)S(1)}, bf16[128,2048]{1,0:T(8,128)(2,1)S(1)}, u32[]{:S(2)}, u32[]{:S(2)}) %collective-permute-start.17) | collective-permute-done | bytes 524320 | tf_op jit(solution)/shard_map/ppermute | solution.py:59
  187.6 10.5 %collective-permute-done.18 = bf16[128,2048]{1,0:T(8,128)(2,1)S(1)} collective-permute-done((bf16[128,2048]{1,0:T(8,128)(2,1)S(1)}, bf16[128,2048]{1,0:T(8,128)(2,1)S(1)}, u32[]{:S(2)}, u32[]{:S(2)}) %collective-permute-start.18) | collective-permute-done | bytes 524320 | tf_op jit(solution)/shard_map/ppermute | solution.py:59
  231.1 14.8 %all-gather.19.cloned.1.call-done = bf16[2048,512]{1,0:T(8,128)(2,1)} async-done(((bf16[512,512]{1,0:T(8,128)(2,1)}), bf16[2048,512]{1,0:T(8,128)(2,1)}) %all-gather.19.cloned.1.call-update) | async-done | bytes 2097168 | tf_op jit(solution)/shard_map/all_gather | solution.py:209
  260.7 5.7 %fusion.117 = f32[1024,2048]{1,0:T(8,128)} fusion(bf16[1024,512]{1,0:T(8,128)(2,1)S(1)} %copy-done.80, bf16[2048,512]{1,0:T(8,128)(2,1)S(1)} %copy-done.77), kind=kOutput, calls=%fused_computation.288 | convolution fusion | flops 2147483648 | bytes 11534336 | tf_op jit(solution)/shard_map/dot_general | solution.py:34
  266.6 6.9 %convolution_add_fusion = f32[1024,2048]{1,0:T(8,128)S(1)} fusion(f32[1024,2048]{1,0:T(8,128)} %fusion.117, bf16[1024,512]{1,0:T(8,128)(2,1)} %copy-done.41, bf16[2048,512]{1,0:T(8,128)(2,1)} %all-gather.19.cloned.1.call-done), kind=kOutput, calls=%fused_computation.6 | convolution fusion | flops 2149580800 | bytes 19922944 | tf_op jit(solution)/shard_map/dot_general | solution.py:34
  296.5 8.7 %collective-permute-done.22 = bf16[128,2048]{1,0:T(8,128)(2,1)S(1)} collective-permute-done((bf16[128,2048]{1,0:T(8,128)(2,1)S(1)}, bf16[128,2048]{1,0:T(8,128)(2,1)S(1)}, u32[]{:S(2)}, u32[]{:S(2)}) %collective-permute-start.22) | collective-permute-done | bytes 524320 | tf_op jit(solution)/shard_map/ppermute | solution.py:59
  305.2 11.1 %collective-permute-done.24 = bf16[128,2048]{1,0:T(8,128)(2,1)S(1)} collective-permute-done((bf16[128,2048]{1,0:T(8,128)(2,1)S(1)}, bf16[128,2048]{1,0:T(8,128)(2,1)S(1)}, u32[]{:S(2)}, u32[]{:S(2)}) %collective-permute-start.24) | collective-permute-done | bytes 524320 | tf_op jit(solution)/shard_map/ppermute | solution.py:59
  323.1 10.9 %collective-permute-done.26 = bf16[128,2048]{1,0:T(8,128)(2,1)S(1)} collective-permute-done((bf16[128,2048]{1,0:T(8,128)(2,1)S(1)}, bf16[128,2048]{1,0:T(8,128)(2,1)S(1)}, u32[]{:S(2)}, u32[]{:S(2)}) %collective-permute-start.26) | collective-permute-done | bytes 524320 | tf_op jit(solution)/shard_map/ppermute | solution.py:59
  351.1 10.8 %shard_map.289 = (bf16[512,512]{1,0:T(8,128)(2,1)S(1)}, f32[4,1024,256]{2,1,0:T(8,128)}) custom-call(s32[5]{0:T(128)S(1)} %pad_add_fusion.scalars, bf16[512,512]{1,0:T(8,128)(2,1)S(1)} %copy-done.5, bf16[512,512]{1,0:T(8,128)(2,1)S(1)} %convolution_convert_fusion.4.go_ref, bf16[4,1024,256]{2,1,0:T(8,128)(2,1)S(1)} %bitcast.409, s32[1,1024]{1,0:T(1,128)S(1)} %bitcast.412), custom_call_target="tpu_custom_call" | custom-call | flops 2684354560 | bytes 8388608 | tf_op jit(solution)/shard_map/pallas_call | solution.py:154
  361.9 10.0 %collective-permute-done.30 = bf16[128,2048]{1,0:T(8,128)(2,1)S(1)} collective-permute-done((bf16[128,2048]{1,0:T(8,128)(2,1)S(1)}, bf16[128,2048]{1,0:T(8,128)(2,1)S(1)}, u32[]{:S(2)}, u32[]{:S(2)}) %collective-permute-start.30) | collective-permute-done | bytes 524320 | tf_op jit(solution)/shard_map/ppermute | solution.py:59
  406.0 10.1 %collective-permute-done.36 = bf16[2,128,256]{2,1,0:T(8,128)(2,1)S(1)} collective-permute-done((bf16[2,128,256]{2,1,0:T(8,128)(2,1)S(1)}, bf16[2,128,256]{2,1,0:T(8,128)(2,1)S(1)}, u32[]{:S(2)}, u32[]{:S(2)}) %collective-permute-start.36) | collective-permute-done | bytes 131104 | tf_op jit(solution)/shard_map/ppermute | solution.py:59
  416.2 9.5 %collective-permute-done.37 = bf16[1,128,256]{2,1,0:T(8,128)(2,1)S(1)} collective-permute-done((bf16[1,128,256]{2,1,0:T(8,128)(2,1)S(1)}, bf16[1,128,256]{2,1,0:T(8,128)(2,1)S(1)}, u32[]{:S(2)}, u32[]{:S(2)}) %collective-permute-start.37) | collective-permute-done | bytes 65568 | tf_op jit(solution)/shard_map/ppermute | solution.py:59
  442.7 6.2 %collective-permute-done.49 = bf16[256,1024]{1,0:T(8,128)(2,1)S(1)} collective-permute-done((bf16[256,1024]{1,0:T(8,128)(2,1)S(1)}, bf16[256,1024]{1,0:T(8,128)(2,1)S(1)}, u32[]{:S(2)}, u32[]{:S(2)}) %collective-permute-start.49) | collective-permute-done | bytes 524320 | tf_op jit(solution)/shard_map/ppermute | solution.py:59
  449.9 21.4 %collective-permute-done.47 = bf16[4,256,512]{2,1,0:T(8,128)(2,1)S(1)} collective-permute-done((bf16[4,256,512]{2,1,0:T(8,128)(2,1)S(1)}, bf16[4,256,512]{2,1,0:T(8,128)(2,1)S(1)}, u32[]{:S(2)}, u32[]{:S(2)}) %collective-permute-start.47) | collective-permute-done | bytes 1048608 | tf_op jit(solution)/shard_map/ppermute | solution.py:59
  473.1 5.8 %collective-permute-done.39 = bf16[704,256]{1,0:T(8,128)(2,1)} collective-permute-done((bf16[704,256]{1,0:T(8,128)(2,1)}, bf16[704,256]{1,0:T(8,128)(2,1)}, u32[]{:S(2)}, u32[]{:S(2)}) %collective-permute-start.39) | collective-permute-done | bytes 360480 | tf_op jit(solution)/shard_map/ppermute | solution.py:59
  494.6 6.9 %collective-permute-done.41 = bf16[448,256]{1,0:T(8,128)(2,1)S(1)} collective-permute-done((bf16[448,256]{1,0:T(8,128)(2,1)S(1)}, bf16[448,256]{1,0:T(8,128)(2,1)S(1)}, u32[]{:S(2)}, u32[]{:S(2)}) %collective-permute-start.41) | collective-permute-done | bytes 229408 | tf_op jit(solution)/shard_map/ppermute | solution.py:59
  505.2 8.0 %collective-permute-done.43 = bf16[4,256,512]{2,1,0:T(8,128)(2,1)S(1)} collective-permute-done((bf16[4,256,512]{2,1,0:T(8,128)(2,1)S(1)}, bf16[4,256,512]{2,1,0:T(8,128)(2,1)S(1)}, u32[]{:S(2)}, u32[]{:S(2)}) %collective-permute-start.43) | collective-permute-done | bytes 1048608 | tf_op jit(solution)/shard_map/ppermute | solution.py:59
  (463 shorter events, 288.6 us)
Async XLA Ops:
  7.2 53.0 %all-gather.11.cloned.1.call-start = ((), (), s32[]{:S(2)}) async-start(), calls=%async_computation.12 | async-start | bytes 2621440 | tf_op jit(solution)/shard_map/all_gather | solution.py:209
  9.3 97.8 %all-gather.13.cloned.1.call-start = ((), (), s32[]{:S(2)}) async-start(), calls=%async_computation.13 | async-start | bytes 2621440 | tf_op jit(solution)/shard_map/all_gather | solution.py:209
  11.4 37.3 %collective-permute-start = (bf16[128,2048]{1,0:T(8,128)(2,1)S(1)}, bf16[128,2048]{1,0:T(8,128)(2,1)}, u32[]{:S(2)}, u32[]{:S(2)}) collective-permute-start(bf16[128,2048]{1,0:T(8,128)(2,1)S(1)} %fusion.28), channel_id=1, source_target_pairs={{0,2},{1,3},{2,0},{3,1},{4,6},{5,7},{6,4},{7,5},{8,10},{9,11},{10,... | collective-permute-start | bytes 1572872 | tf_op jit(solution)/shard_map/ppermute | solution.py:59
  36.5 27.5 %collective-permute-start.9 = (bf16[4,128,256]{2,1,0:T(8,128)(2,1)S(1)}, bf16[4,128,256]{2,1,0:T(8,128)(2,1)}, u32[]{:S(2)}, u32[]{:S(2)}) collective-permute-start(bf16[4,128,256]{2,1,0:T(8,128)(2,1)S(1)} %bitcast.461), channel_id=1, source_target_pairs={{0,4},{1,5},{2,6},{3,7},{4,0},{5,1},{6,2},{7,3},{8,12},{9,13},{10,... | collective-permute-start | bytes 786440 | tf_op jit(solution)/shard_map/ppermute | solution.py:59
  48.6 118.9 %all-gather.15.cloned.1.call-start = ((), (), s32[]{:S(2)}) async-start(), calls=%async_computation.14 | async-start | bytes 2621440 | tf_op jit(solution)/shard_map/all_gather | solution.py:209
  50.9 30.9 %collective-permute-start.1 = (bf16[2,128,2048]{2,1,0:T(8,128)(2,1)}, bf16[2,128,2048]{2,1,0:T(8,128)(2,1)}, u32[]{:S(2)}, u32[]{:S(2)}) collective-permute-start(bf16[2,128,2048]{2,1,0:T(8,128)(2,1)} %get-tuple-element.147), channel_id=1, source_target_pairs={{0,1},{1,0},{2,3},{3,2},{4,5},{5,4},{6,7},{7,6},{8,9},{9,8},{10,11... | collective-permute-start | bytes 3145736 | tf_op jit(solution)/shard_map/ppermute | solution.py:59
  95.1 104.5 %all-gather.17.cloned.1.call-start = ((), (), s32[]{:S(2)}) async-start(), calls=%async_computation.15 | async-start | bytes 2621440 | tf_op jit(solution)/shard_map/all_gather | solution.py:209
  127.8 46.4 %collective-permute-start.4 = (bf16[128,2048]{1,0:T(8,128)(2,1)}, bf16[128,2048]{1,0:T(8,128)(2,1)}, u32[]{:S(2)}, u32[]{:S(2)}) collective-permute-start(bf16[128,2048]{1,0:T(8,128)(2,1)} %bitcast_select_fusion.4), channel_id=1, source_target_pairs={{0,2},{1,3},{2,0},{3,1},{4,6},{5,7},{6,4},{7,5},{8,10},{9,11},{10,... | collective-permute-start | bytes 1572872 | tf_op jit(solution)/shard_map/ppermute | solution.py:59
  128.4 47.2 %collective-permute-start.3 = (bf16[128,2048]{1,0:T(8,128)(2,1)}, bf16[128,2048]{1,0:T(8,128)(2,1)}, u32[]{:S(2)}, u32[]{:S(2)}) collective-permute-start(bf16[128,2048]{1,0:T(8,128)(2,1)} %bitcast_select_fusion.4), channel_id=1, source_target_pairs={{0,4},{1,5},{2,6},{3,7},{4,0},{5,1},{6,2},{7,3},{8,12},{9,13},{10,... | collective-permute-start | bytes 1572872 | tf_op jit(solution)/shard_map/ppermute | solution.py:59
  129.9 45.7 %collective-permute-start.5 = (bf16[128,2048]{1,0:T(8,128)(2,1)}, bf16[128,2048]{1,0:T(8,128)(2,1)}, u32[]{:S(2)}, u32[]{:S(2)}) collective-permute-start(bf16[128,2048]{1,0:T(8,128)(2,1)} %bitcast_select_fusion.4), channel_id=1, source_target_pairs={{0,6},{1,7},{2,4},{3,5},{4,2},{5,3},{6,0},{7,1},{8,14},{9,15},{10,... | collective-permute-start | bytes 1572872 | tf_op jit(solution)/shard_map/ppermute | solution.py:59
  136.9 28.0 %collective-permute-start.15 = (bf16[128,2048]{1,0:T(8,128)(2,1)}, bf16[128,2048]{1,0:T(8,128)(2,1)}, u32[]{:S(2)}, u32[]{:S(2)}) collective-permute-start(bf16[128,2048]{1,0:T(8,128)(2,1)} %fusion.55), channel_id=1, source_target_pairs={{0,2},{1,3},{2,0},{3,1},{4,6},{5,7},{6,4},{7,5},{8,10},{9,11},{10,... | collective-permute-start | bytes 1572872 | tf_op jit(solution)/shard_map/ppermute | solution.py:59
  138.6 107.3 %all-gather.19.cloned.1.call-start = ((), (), s32[]{:S(2)}) async-start(), calls=%async_computation.16 | async-start | bytes 2621440 | tf_op jit(solution)/shard_map/all_gather | solution.py:209
  178.6 27.8 %collective-permute-start.6 = (bf16[4,128,2048]{2,1,0:T(8,128)(2,1)}, bf16[4,128,2048]{2,1,0:T(8,128)(2,1)}, u32[]{:S(2)}, u32[]{:S(2)}) collective-permute-start(bf16[4,128,2048]{2,1,0:T(8,128)(2,1)} %pad_maximum_fusion.3), channel_id=1, source_target_pairs={{0,1},{1,0},{2,3},{3,2},{4,5},{5,4},{6,7},{7,6},{8,9},{9,8},{10,11... | collective-permute-start | bytes 6291464 | tf_op jit(solution)/shard_map/ppermute | solution.py:59
  200.5 118.4 %reduce-scatter.7.cloned.1.call-start = ((), (), s32[]{:S(2)}) async-start(), calls=%async_computation.6 | async-start | bytes 2621440 | tf_op jit(solution)/shard_map/reduce_scatter | solution.py:212
  245.9 97.1 %reduce-scatter.9.cloned.1.call-start = ((), (), s32[]{:S(2)}) async-start(), calls=%async_computation.7 | async-start | bytes 2621440 | tf_op jit(solution)/shard_map/reduce_scatter | solution.py:212
  258.1 29.2 %collective-permute-start.21 = (bf16[4,128,2048]{2,1,0:T(8,128)(2,1)}, bf16[4,128,2048]{2,1,0:T(8,128)(2,1)}, u32[]{:S(2)}, u32[]{:S(2)}) collective-permute-start(bf16[4,128,2048]{2,1,0:T(8,128)(2,1)} %bitcast.56), channel_id=1, source_target_pairs={{0,1},{1,0},{2,3},{3,2},{4,5},{5,4},{6,7},{7,6},{8,9},{9,8},{10,11... | collective-permute-start | bytes 6291464 | tf_op jit(solution)/shard_map/ppermute | solution.py:59
  266.4 129.5 %reduce-scatter.11.cloned.1.call-start = ((), (), s32[]{:S(2)}) async-start(), calls=%async_computation.8 | async-start | bytes 2621440 | tf_op jit(solution)/shard_map/reduce_scatter | solution.py:212
  319.0 161.8 %reduce-scatter.13.cloned.1.call-start = ((), (), s32[]{:S(2)}) async-start(), calls=%async_computation.9 | async-start | bytes 2621440 | tf_op jit(solution)/shard_map/reduce_scatter | solution.py:212
  339.8 187.6 %reduce-scatter.17.cloned.1.call-start = ((), (), s32[]{:S(2)}) async-start(), calls=%async_computation.11 | async-start | bytes 1310720 | tf_op jit(solution)/shard_map/reduce_scatter | solution.py:212
  437.4 34.0 %collective-permute-start.47 = (bf16[4,256,512]{2,1,0:T(8,128)(2,1)S(1)}, bf16[4,256,512]{2,1,0:T(8,128)(2,1)S(1)}, u32[]{:S(2)}, u32[]{:S(2)}) collective-permute-start(bf16[4,256,512]{2,1,0:T(8,128)(2,1)S(1)} %fusion.38), channel_id=1, source_target_pairs={{0,4},{1,5},{2,6},{3,7},{4,0},{5,1},{6,2},{7,3},{8,12},{9,13},{10,... | collective-permute-start | bytes 3145736 | tf_op jit(solution)/shard_map/ppermute | solution.py:59
  441.2 37.6 %collective-permute-start.39 = (bf16[704,256]{1,0:T(8,128)(2,1)}, bf16[704,256]{1,0:T(8,128)(2,1)}, u32[]{:S(2)}, u32[]{:S(2)}) collective-permute-start(bf16[704,256]{1,0:T(8,128)(2,1)} %pad_maximum_fusion.20), channel_id=1, source_target_pairs={{0,4},{1,5},{2,6},{3,7},{4,0},{5,1},{6,2},{7,3},{8,12},{9,13},{10,... | collective-permute-start | bytes 1081352 | tf_op jit(solution)/shard_map/ppermute | solution.py:59
  472.8 67.7 %reduce-scatter.15.cloned.1.call-start = ((), (), s32[]{:S(2)}) async-start(), calls=%async_computation.10 | async-start | bytes 1310720 | tf_op jit(solution)/shard_map/reduce_scatter | solution.py:212
  487.1 26.1 %collective-permute-start.43 = (bf16[4,256,512]{2,1,0:T(8,128)(2,1)S(1)}, bf16[4,256,512]{2,1,0:T(8,128)(2,1)S(1)}, u32[]{:S(2)}, u32[]{:S(2)}) collective-permute-start(bf16[4,256,512]{2,1,0:T(8,128)(2,1)S(1)} %copy-done.53), channel_id=1, source_target_pairs={{0,4},{1,5},{2,6},{3,7},{4,0},{5,1},{6,2},{7,3},{8,12},{9,13},{10,... | collective-permute-start | bytes 3145736 | tf_op jit(solution)/shard_map/ppermute | solution.py:59
  493.1 29.9 %collective-permute-start.48 = (bf16[256,1024]{1,0:T(8,128)(2,1)}, bf16[256,1024]{1,0:T(8,128)(2,1)}, u32[]{:S(2)}, u32[]{:S(2)}) collective-permute-start(bf16[256,1024]{1,0:T(8,128)(2,1)} %dynamic-slice_bitcast_fusion.3), channel_id=1, source_target_pairs={{0,4},{1,5},{2,6},{3,7},{4,0},{5,1},{6,2},{7,3},{8,12},{9,13},{10,... | collective-permute-start | bytes 1572872 | tf_op jit(solution)/shard_map/ppermute | solution.py:59
  (121 other events, 1108.2 us)
Sparse Core Ops, SparseCore 0:
  10.2 50.0 all-gather.10
  62.4 44.6 all-gather.12
  108.6 44.6 all-gather.14
  154.7 44.6 all-gather.16
  200.8 44.6 all-gather.18
  247.7 42.5 reduce-scatter.6
  293.2 43.1 reduce-scatter.8
  338.8 43.1 reduce-scatter.10
  384.4 47.2 reduce-scatter.12
  472.9 31.2 reduce-scatter.16
  514.7 25.6 reduce-scatter.14

commit v2 on v1

--- a/solution.py
+++ b/solution.py
@@ -213,30 +213,30 @@
             values, "blk", scatter_dimension=0, axis_index_groups=z_groups
         )
 
+    def pair_y(values):
+        return jnp.stack([values, flip(values, head_bits=2)])
+
+    def pair_core(pair):
+        return jnp.concatenate([pair, flip(pair, head_bits=1)])
+
     def gather_head(values):
-        pair = jnp.stack([values, flip(values, head_bits=2)])
-        other = flip(pair, head_bits=1)
-        return jnp.stack([pair, other], axis=1).reshape((slots,) + values.shape)
-
-    def head_core(values):
-        parts = values.reshape((2, 2) + values.shape[1:])
-        return wide(parts[:, 0]) + wide(flip(low(parts[:, 1]), head_bits=1))
-
-    def head_y(half):
+        return pair_core(pair_y(values))
+
+    def add_core(left, right):
+        rows = left[0].shape[0] // 2
+        send = sum(col_dot(v[rows:], w) for v, w in zip(left, right))
+        keep = sum(col_dot(v[:rows], w) for v, w in zip(left, right))
+        keep = keep + wide(flip(low(send), head_bits=1))
+        return keep.reshape(-1, seq_dev, width)
+
+    def add_y(half):
         return half[0] + wide(flip(low(half[1]), head_bits=2))
-
-    def scatter_head(values):
-        return head_y(head_core(values))
 
     def gather_xy(values):
         return jnp.stack([values] + [flip(values, *bits) for bits in plane])
 
     def gather_core(mine):
         return jnp.concatenate([mine, flip(mine, head_bits=1)]).reshape(-1, width)
-
-    def plane_core(values):
-        parts = values.reshape((2, 4, seq_dev, width))
-        return parts[0] + wide(flip(low(parts[1]), head_bits=1))
 
     def plane_xy(half):
         total = half[0]
@@ -279,7 +279,7 @@
     keys = gather_head(keys).reshape(slots, blk_count * seq_dev, 2 * HEAD_DIM)
     key_blocks = blk ^ jnp.arange(blk_count, dtype=jnp.int32)
     key_pos = (key_blocks[:, None] * seq_dev + positions[None, :]).reshape(1, -1)
-    slot_ids = head ^ jnp.arange(slots, dtype=jnp.int32)
+    slot_ids = head ^ jnp.array([0, 2, 1, 3], jnp.int32)
     scalars = jnp.concatenate([(blk * seq_dev)[None], lengths[slot_ids]]).astype(jnp.int32)
     group_in = gather_head(attn_in).reshape(slots * seq_dev, width)
 
@@ -296,10 +296,8 @@
         forward_kernel, ("row",), scalars, (queries,), keys, key_pos, seq_dev, 2
     )
     attn_low, full_up[0] = tie(attn_low, full_up[0])
-    attn_part = col_dot(attn_low, full_out).reshape(slots, seq_dev, width)
-    hidden_res = own_rows + scatter_head(attn_part) + b_out
-
-    hidden_res, full_up[1] = tie(hidden_res, full_up[1])
+    hidden_res = own_rows + add_y(add_core([attn_low], [full_out])) + b_out
+    hidden_res, full_up[1], cot_rows = tie(hidden_res, full_up[1], cot_rows)
     normed_two = layer_norm(hidden_res, ln2_gain, ln2_bias).astype(LOW)
     mine_in, full_down[0] = tie(gather_xy(normed_two), full_down[0])
     ffn_in = gather_core(mine_in)
@@ -318,18 +316,24 @@
     activated, gelu_pulls = zip(*[gelu(i) for i in range(2)])
     activated = tie(*activated)
     grad_down = [low(row_dot(cot_rows, v)) for v in activated]
-    *grad_down, full_down[1] = tie(*grad_down, full_down[1])
-    sums_down = [scatter_units(v) for v in grad_down]
-    grad_up_rows = [
-        low(gelu_pulls[i](plain_dot(cot_rows, full_down[i]))[0]) for i in range(2)
-    ]
-    ffn_in_grad = plane_core(sum(col_dot(grad_up_rows[i], full_up[i]) for i in range(2)))
-    ffn_in_grad = plane_xy(ffn_in_grad)
-    ffn_part = plane_core(sum(col_dot(activated[i], full_down[i]) for i in range(2)))
+
+    def back(i):
+        return low(gelu_pulls[i](plain_dot(cot_rows, full_down[i]))[0])
+
+    *grad_down, first_rows, full_down[1] = tie(*grad_down, back(0), full_down[1])
+    sums_down = [scatter_units(grad_down[0])]
+    grad_up_rows = [first_rows, back(1)]
+    in_half = add_core(grad_up_rows, full_up)
+    in_half, activated, grad_up_rows, grad_down = tie(
+        in_half, activated, grad_up_rows, grad_down[1]
+    )
+    sums_down.append(scatter_units(grad_down))
+    ffn_in_grad = plane_xy(in_half)
     grad_up = [low(row_dot(ffn_in, v)) for v in grad_up_rows]
-    ffn_in_grad, ffn_part, sums_down[0], *grad_up = tie(
-        ffn_in_grad, ffn_part, sums_down[0], *grad_up
-    )
+    ffn_in_grad, sums_down[0], grad_up, activated = tie(
+        ffn_in_grad, sums_down[0], grad_up, activated
+    )
+    ffn_half = add_core(activated, full_down)
     sums_up = [scatter_units(v) for v in grad_up]
     grad_up_bias = jnp.concatenate(
         [jnp.sum(v, axis=0, dtype=jnp.float32) for v in grad_up_rows]
@@ -339,9 +343,9 @@
     res_grad, grad_ln2_gain, grad_ln2_bias = norm_two_pull(ffn_in_grad)
     res_total = own_cot + res_grad
 
-    cot_attn = gather_head(res_total.astype(LOW)).reshape(slots * seq_dev, width)
-    cot_attn, sums_down[1], ffn_part = tie(cot_attn, sums_down[1], ffn_part)
-    output = low(hidden_res + plane_xy(ffn_part) + b_down)[None]
+    cot_pair, ffn_half = tie(pair_y(low(res_total)), ffn_half)
+    cot_attn = pair_core(cot_pair).reshape(slots * seq_dev, width)
+    cot_attn, sums_down[1] = tie(cot_attn, sums_down[1])
     attn_grad = plain_dot(cot_attn, full_out).astype(LOW)
     query_low, kv_grad = attention_call(
         backward_kernel,
@@ -353,33 +357,30 @@
         seq_dev,
         5,
     )
-    query_low, kv_grad, output = tie(query_low, kv_grad, output)
-    half_kv = head_core(kv_grad.reshape(slots, blk_count, seq_dev, 2 * HEAD_DIM))
-    half_kv, cot_late, in_late = tie(half_kv, cot_attn, group_in)
+    kv_grad = kv_grad.reshape(slots, blk_count, seq_dev, 2 * HEAD_DIM)
+    half_kv = kv_grad[:2] + wide(flip(low(kv_grad[2:]), head_bits=1))
+    half_in = add_core([query_low], [full_q])
+    half_kv, half_in, cot_late, in_late = tie(half_kv, half_in, cot_attn, group_in)
 
     def sides(grads):
         parts = grads.reshape(z_count, 2, depth, q_dev)
         return take(parts, x, 1), low(take(parts, 1 - x, 1))
 
+    grad_q, q_across = sides(row_dot(in_late, query_low))
+    q_across = flip(q_across, blk_bits=1)
+    part, grad_q, cot_late, sums_up[0] = tie(add_y(half_kv), grad_q, cot_late, sums_up[0])
     grad_out, out_across = sides(row_dot(cot_late, attn_low))
-    grad_q, q_across = sides(row_dot(in_late, query_low))
-    out_across = flip(out_across, blk_bits=1)
-    part, sums_up[0], grad_out, grad_q, q_across = tie(
-        head_y(half_kv), sums_up[0], grad_out, grad_q, q_across
-    )
-    sum_out = wide(scatter_z(low(grad_out + wide(out_across))))
     bit = 1
     while bit < blk_count:
         pair = part.reshape((-1, 2) + part.shape[1:])
         part = pair[:, 0] + wide(flip(low(pair[:, 1]), blk_bits=bit))
         if bit == 1:
-            part, q_across = tie(part, q_across)
-            q_across = flip(q_across, blk_bits=1)
+            part, grad_out, out_across, q_across = tie(part, grad_out, out_across, q_across)
+            sum_q = wide(scatter_z(low(grad_q + wide(q_across))))
+            out_across = flip(out_across, blk_bits=1)
         bit *= 2
     own_kv_grad = low(part[0])
-    sum_q = wide(scatter_z(low(grad_q + wide(q_across))))
-    attn_in_grad = col_dot(query_low, full_q).reshape(slots, seq_dev, width)
-    norm_one_grad = scatter_head(attn_in_grad) + col_dot(own_kv_grad, w_kv)
+    norm_one_grad = add_y(half_in) + col_dot(own_kv_grad, w_kv)
     norm_one_value, norm_one_pull = jax.vjp(layer_norm, own_rows, ln1_gain, ln1_bias)
     input_part, grad_ln1_gain, grad_ln1_bias = norm_one_pull(norm_one_grad)
     input_grad = res_total + input_part
@@ -392,9 +393,8 @@
             jnp.concatenate([jnp.where(first, own, other), jnp.where(first, other, own)], axis=-1)
         )
 
-    sum_down = ff_sum(sums_down)
-
-    grad_kv = row_dot(attn_in, own_kv_grad)
+    grad_kv, out_across = tie(row_dot(attn_in, own_kv_grad), out_across)
+    out_total = low(grad_out + wide(out_across))
     grad_b_q = lax.dynamic_update_slice_in_dim(
         jnp.zeros((width,), jnp.float32),
         jnp.sum(query_low, axis=0, dtype=jnp.float32),
@@ -440,14 +440,21 @@
 
     lines, rows = halved(lines, grad_kv, core, head_bits=1)
     lines, rows = halved(lines, rows, x, blk_bits=1)
-    rows, sums_up[1] = tie(rows, sums_up[1])
-    sum_up = ff_sum(sums_up)
+    rows, ffn_half = tie(rows, ffn_half)
+    output = low(hidden_res + plane_xy(ffn_half) + b_down)[None]
     lines, rows = halved(lines, rows, y, head_bits=2)
+    rows, sums_down = tie(rows, sums_down)
+    sum_down = ff_sum(sums_down)
     bit = 2
     while bit < blk_count:
         lines, got = exchange(lines, rows, blk_bits=bit)
         rows = rounded(rows) + got
+        if bit == 2:
+            rows, sum_q, sums_up[1] = tie(rows, sum_q, sums_up[1])
+            sum_up = ff_sum(sums_up)
         bit *= 2
+    rows, out_total = tie(rows, out_total)
+    sum_out = wide(scatter_z(out_total))
     rows = joined(low(rows), y, head_bits=2)
     rows = joined(rows, x, blk_bits=1)
     sum_kv = wide(joined(rows, core, head_bits=1))

time: 560 us -> 546 us (0.975)
  other arithmetic: 97.4 us -> 73.5 us
  local copies, waits for them, and re-layouts: 65.4 us -> 49.8 us
  waiting for transfers between devices: 243 us -> 258 us
  matrix products: 59.6 us -> 68.8 us
    reduce_scatter x6, waiting for transfers between devices: 1.01 us -> 20.3 us  [scatter_z(): lax.psum_scatter(values, 'blk', scatter_dimension=0, axis_index_groups=z_...]
    ppermute x50, waiting for transfers between devices: 216 us -> 201 us  [flip(): return lax.ppermute(values, ('blk', 'head'), pairs)]
    unnamed x178 -> x170, local copies, waits for them, and re-layouts: 33.8 us -> 19.9 us
    another operation x8 -> x5, other arithmetic: 16.3 us -> 5.14 us  [the longest x6 10.5 us: gather_head(): return jnp.stack([pair, other], axis=1).reshape((slots,) + values.shape)]
    all_gather x5, waiting for transfers between devices: 25.5 us -> 35.9 us  [gather_z(): return lax.all_gather(values, 'blk', axis=0, axis_index_groups=z_groups)]
    add x6 -> x5, other arithmetic: 11 us -> 2.75 us  [the longest x1 1.7 us: on_device(): half_kv = kv_grad[:2] + wide(flip(low(kv_grad[2:]), head_bits=1))]
    dot_general x7 -> x13, matrix products: 22.6 us -> 27 us  [col_dot(): lax.dot_general(left, right, (((1,), (1,)), ((), ())), preferred_element_...]
  transfers between devices with their start and end apart: 61 -> 61, of which waited for: 32 -> 37; matrix products, arithmetic and copies ran while one was open for 36% -> 33% of each run, Pallas kernels for 3% -> 3%
where the time goes in v2:
time: 546 us; the launch traced here: 537 us
  waiting for transfers between devices  258 us (47%)
  other arithmetic  73.5 us (13%)
  matrix products  68.8 us (13%)
  starting transfers between devices  54.2 us (10%)
  local copies, waits for them, and re-layouts  49.8 us (9%)
  Pallas kernels  17.9 us (3%)
  between operations  15.6 us (3%)
    ppermute x50, waiting for transfers between devices, flip(): return lax.ppermute(values, ('blk', 'head'), pairs)  201 us
    ppermute x50, starting transfers between devices, flip(): return lax.ppermute(values, ('blk', 'head'), pairs)  52.6 us
    all_gather x5, waiting for transfers between devices, gather_z(): return lax.all_gather(values, 'blk', axis=0, axis_index_groups=z_groups)  35.9 us
    dot_general x13, matrix products, col_dot(): lax.dot_general(left, right, (((1,), (1,)), ((), ())), preferred_element_...  27 us
    dot_general x7, matrix products, row_dot(): lax.dot_general(left, right, (((0,), (0,)), ((), ())), preferred_element_...  22.2 us
    reduce_scatter x6, waiting for transfers between devices, scatter_z(): lax.psum_scatter(values, 'blk', scatter_dimension=0, axis_index_groups=z_...  20.3 us
    unnamed x170, local copies, waits for them, and re-layouts  19.9 us
    dot_general x7, matrix products, plain_dot(): return jnp.dot(left, right, preferred_element_type=jnp.float32)  19.6 us
  transfers between devices with their start and end apart: 61, of which 37 were waited for; matrix products, arithmetic and copies ran while one was open for 33% of the time, Pallas kernels for 3%

profile of v2, /device:TPU:0, one launch (start us, length us, event | category | flops | bytes accessed | tf_op | source)
XLA Modules:
  0.0 537.4 jit_solution(5767687100692150674)
XLA Ops:
  16.6 10.6 %collective-permute-done.19 = bf16[256,1024]{1,0:T(8,128)(2,1)S(1)} collective-permute-done((bf16[256,1024]{1,0:T(8,128)(2,1)}, bf16[256,1024]{1,0:T(8,128)(2,1)S(1)}, u32[]{:S(2)}, u32[]{:S(2)}) %collective-permute-start.19) | collective-permute-done | bytes 524320 | tf_op jit(solution)/shard_map/ppermute | solution.py:59
  27.2 10.5 %collective-permute-done.8 = bf16[256,1024]{1,0:T(8,128)(2,1)} collective-permute-done((bf16[256,1024]{1,0:T(8,128)(2,1)}, bf16[256,1024]{1,0:T(8,128)(2,1)}, u32[]{:S(2)}, u32[]{:S(2)}) %collective-permute-start.8) | collective-permute-done | bytes 524320 | tf_op jit(solution)/shard_map/ppermute | solution.py:59
  55.8 5.5 %collective-permute-done.4 = bf16[2,128,256]{2,1,0:T(8,128)(2,1)S(1)} collective-permute-done((bf16[2,128,256]{2,1,0:T(8,128)(2,1)S(1)}, bf16[2,128,256]{2,1,0:T(8,128)(2,1)S(1)}, u32[]{:S(2)}, u32[]{:S(2)}) %collective-permute-start.4) | collective-permute-done | bytes 131104 | tf_op jit(solution)/shard_map/ppermute | solution.py:59
  63.1 5.2 collective-permute-done
  77.8 11.1 %collective-permute-done.6 = bf16[8,128,256]{2,1,0:T(8,128)(2,1)S(1)} collective-permute-done((bf16[8,128,256]{2,1,0:T(8,128)(2,1)S(1)}, bf16[8,128,256]{2,1,0:T(8,128)(2,1)S(1)}, u32[]{:S(2)}, u32[]{:S(2)}) %collective-permute-start.6) | collective-permute-done | bytes 524320 | tf_op jit(solution)/shard_map/ppermute | solution.py:59
  92.3 6.8 %collective-permute-done.2 = bf16[4,256,512]{2,1,0:T(8,128)(2,1)} collective-permute-done((bf16[4,256,512]{2,1,0:T(8,128)(2,1)}, bf16[4,256,512]{2,1,0:T(8,128)(2,1)}, u32[]{:S(2)}, u32[]{:S(2)}) %collective-permute-start.2) | collective-permute-done | bytes 1048608 | tf_op jit(solution)/shard_map/ppermute | solution.py:59
  114.4 7.3 %shard_map.297 = bf16[512,512]{1,0:T(8,128)(2,1)S(1)} custom-call(s32[5]{0:T(128)S(1)} %pad_add_fusion.scalars, bf16[512,512]{1,0:T(8,128)(2,1)S(1)} %fusion.20.q_ref, bf16[4,1024,256]{2,1,0:T(8,128)(2,1)S(1)} %pad_maximum_fusion.3.kv_ref, s32[1,1024]{1,0:T(1,128)S(1)} %bitcast.348), custom_call_target="tpu_custom_call" | custom-call | flops 1073741824 | bytes 8388608 | tf_op jit(solution)/shard_map/pallas_call | solution.py:154
  123.1 9.3 %collective-permute-done.9 = bf16[4,256,512]{2,1,0:T(8,128)(2,1)} collective-permute-done((bf16[4,256,512]{2,1,0:T(8,128)(2,1)}, bf16[4,256,512]{2,1,0:T(8,128)(2,1)}, u32[]{:S(2)}, u32[]{:S(2)}) %collective-permute-start.9) | collective-permute-done | bytes 1048608 | tf_op jit(solution)/shard_map/ppermute | solution.py:59
  148.3 9.7 %collective-permute-done.11 = bf16[128,2048]{1,0:T(8,128)(2,1)S(1)} collective-permute-done((bf16[128,2048]{1,0:T(8,128)(2,1)S(1)}, bf16[128,2048]{1,0:T(8,128)(2,1)S(1)}, u32[]{:S(2)}, u32[]{:S(2)}) %collective-permute-start.11) | collective-permute-done | bytes 524320 | tf_op jit(solution)/shard_map/ppermute | solution.py:59
  162.7 10.1 %collective-permute-done.17 = bf16[128,2048]{1,0:T(8,128)(2,1)S(1)} collective-permute-done((bf16[128,2048]{1,0:T(8,128)(2,1)S(1)}, bf16[128,2048]{1,0:T(8,128)(2,1)S(1)}, u32[]{:S(2)}, u32[]{:S(2)}) %collective-permute-start.17) | collective-permute-done | bytes 524320 | tf_op jit(solution)/shard_map/ppermute | solution.py:59
  175.5 9.4 %collective-permute-done.18 = bf16[128,2048]{1,0:T(8,128)(2,1)S(1)} collective-permute-done((bf16[128,2048]{1,0:T(8,128)(2,1)S(1)}, bf16[128,2048]{1,0:T(8,128)(2,1)S(1)}, u32[]{:S(2)}, u32[]{:S(2)}) %collective-permute-start.18) | collective-permute-done | bytes 524320 | tf_op jit(solution)/shard_map/ppermute | solution.py:59
  186.5 15.6 %all-gather.17.cloned.1.call-done = bf16[2048,512]{1,0:T(8,128)(2,1)} async-done(((bf16[512,512]{1,0:T(8,128)(2,1)}), bf16[2048,512]{1,0:T(8,128)(2,1)}) %all-gather.17.cloned.1.call-update) | async-done | bytes 2097168 | tf_op jit(solution)/shard_map/all_gather | solution.py:209
  216.5 4.6 fusion.6
  228.7 20.2 %all-gather.19.cloned.1.call-done = bf16[2048,512]{1,0:T(8,128)(2,1)} async-done(((bf16[512,512]{1,0:T(8,128)(2,1)}), bf16[2048,512]{1,0:T(8,128)(2,1)}) %all-gather.19.cloned.1.call-update) | async-done | bytes 2097168 | tf_op jit(solution)/shard_map/all_gather | solution.py:209
  274.8 6.2 %convolution_convert_fusion.1 = bf16[2048,512]{1,0:T(8,128)(2,1)} fusion(bf16[1024,2048]{1,0:T(8,128)(2,1)} %bitcast.380, bf16[1024,512]{1,0:T(8,128)(2,1)} %get-tuple-element.89), kind=kOutput, calls=%fused_computation.11 | convolution fusion | flops 2148532224 | bytes 7340032 | tf_op jit(solution)/shard_map/dot_general | solution.py:28
  282.1 11.4 %collective-permute-done.24 = bf16[128,2048]{1,0:T(8,128)(2,1)} collective-permute-done((bf16[128,2048]{1,0:T(8,128)(2,1)}, bf16[128,2048]{1,0:T(8,128)(2,1)}, u32[]{:S(2)}, u32[]{:S(2)}) %collective-permute-start.24) | collective-permute-done | bytes 524320 | tf_op jit(solution)/shard_map/ppermute | solution.py:59
  306.6 12.1 %collective-permute-done.25 = bf16[128,2048]{1,0:T(8,128)(2,1)S(1)} collective-permute-done((bf16[128,2048]{1,0:T(8,128)(2,1)S(1)}, bf16[128,2048]{1,0:T(8,128)(2,1)S(1)}, u32[]{:S(2)}, u32[]{:S(2)}) %collective-permute-start.25) | collective-permute-done | bytes 524320 | tf_op jit(solution)/shard_map/ppermute | solution.py:59
  327.6 11.6 %reduce-scatter.9.cloned.1.call-done = bf16[1,512,512]{2,1,0:T(8,128)(2,1)} async-done(((bf16[4,512,512]{2,1,0:T(8,128)(2,1)}), bf16[1,512,512]{2,1,0:T(8,128)(2,1)}) %reduce-scatter.9.cloned.1.call-update) | async-done | bytes 524304 | tf_op jit(solution)/shard_map/reduce_scatter | solution.py:212
  342.9 10.6 %shard_map.298 = (bf16[512,512]{1,0:T(8,128)(2,1)S(1)}, f32[4,1024,256]{2,1,0:T(8,128)}) custom-call(s32[5]{0:T(128)S(1)} %pad_add_fusion.scalars, bf16[512,512]{1,0:T(8,128)(2,1)S(1)} %fusion.20.q_ref, bf16[512,512]{1,0:T(8,128)(2,1)S(1)} %convolution_convert_fusion.6.go_ref, bf16[4,1024,256]{2,1,0:T(8,128)(2,1)S(1)} %copy-done.2, s32[1,1024]{1,0:T(1,128)S(1)} %bitcast.349), custom_call_target="tpu_custom_call" | custom-call | flops 2684354560 | bytes 8388608 | tf_op jit(solution)/shard_map/pallas_call | solution.py:154
  375.6 7.0 %collective-permute-done.30 = bf16[8,128,256]{2,1,0:T(8,128)(2,1)S(1)} collective-permute-done((bf16[8,128,256]{2,1,0:T(8,128)(2,1)S(1)}, bf16[8,128,256]{2,1,0:T(8,128)(2,1)S(1)}, u32[]{:S(2)}, u32[]{:S(2)}) %collective-permute-start.30) | collective-permute-done | bytes 524320 | tf_op jit(solution)/shard_map/ppermute | solution.py:59
  391.8 11.4 %collective-permute-done.31 = bf16[4,128,256]{2,1,0:T(8,128)(2,1)S(1)} collective-permute-done((bf16[4,128,256]{2,1,0:T(8,128)(2,1)S(1)}, bf16[4,128,256]{2,1,0:T(8,128)(2,1)S(1)}, u32[]{:S(2)}, u32[]{:S(2)}) %collective-permute-start.31) | collective-permute-done | bytes 262176 | tf_op jit(solution)/shard_map/ppermute | solution.py:59
  423.5 12.3 %collective-permute-done.35 = bf16[4,256,512]{2,1,0:T(8,128)(2,1)} collective-permute-done((bf16[4,256,512]{2,1,0:T(8,128)(2,1)S(1)}, bf16[4,256,512]{2,1,0:T(8,128)(2,1)}, u32[]{:S(2)}, u32[]{:S(2)}) %collective-permute-start.35) | collective-permute-done | bytes 1048608 | tf_op jit(solution)/shard_map/ppermute | solution.py:59
  447.4 6.7 %collective-permute-done.38 = bf16[704,256]{1,0:T(8,128)(2,1)} collective-permute-done((bf16[704,256]{1,0:T(8,128)(2,1)}, bf16[704,256]{1,0:T(8,128)(2,1)}, u32[]{:S(2)}, u32[]{:S(2)}) %collective-permute-start.38) | collective-permute-done | bytes 360480 | tf_op jit(solution)/shard_map/ppermute | solution.py:59
  471.6 12.5 %collective-permute-done.43 = bf16[448,256]{1,0:T(8,128)(2,1)S(1)} collective-permute-done((bf16[448,256]{1,0:T(8,128)(2,1)S(1)}, bf16[448,256]{1,0:T(8,128)(2,1)S(1)}, u32[]{:S(2)}, u32[]{:S(2)}) %collective-permute-start.43) | collective-permute-done | bytes 229408 | tf_op jit(solution)/shard_map/ppermute | solution.py:59
  (450 shorter events, 284.2 us)
Async XLA Ops:
  7.2 63.2 %all-gather.11.cloned.1.call-start = ((), (), s32[]{:S(2)}) async-start(), calls=%async_computation.12 | async-start | bytes 2621440 | tf_op jit(solution)/shard_map/all_gather | solution.py:209
  9.3 113.8 %all-gather.13.cloned.1.call-start = ((), (), s32[]{:S(2)}) async-start(), calls=%async_computation.13 | async-start | bytes 2621440 | tf_op jit(solution)/shard_map/all_gather | solution.py:209
  41.5 116.6 %all-gather.15.cloned.1.call-start = ((), (), s32[]{:S(2)}) async-start(), calls=%async_computation.14 | async-start | bytes 2621440 | tf_op jit(solution)/shard_map/all_gather | solution.py:209
  42.0 26.3 %collective-permute-start = (bf16[128,2048]{1,0:T(8,128)(2,1)S(1)}, bf16[128,2048]{1,0:T(8,128)(2,1)}, u32[]{:S(2)}, u32[]{:S(2)}) collective-permute-start(bf16[128,2048]{1,0:T(8,128)(2,1)S(1)} %fusion.25), channel_id=1, source_target_pairs={{0,2},{1,3},{2,0},{3,1},{4,6},{5,7},{6,4},{7,5},{8,10},{9,11},{10,... | collective-permute-start | bytes 1572872 | tf_op jit(solution)/shard_map/ppermute | solution.py:59
  49.0 56.7 %collective-permute-start.14 = (bf16[128,2048]{1,0:T(8,128)(2,1)}, bf16[128,2048]{1,0:T(8,128)(2,1)}, u32[]{:S(2)}, u32[]{:S(2)}) collective-permute-start(bf16[128,2048]{1,0:T(8,128)(2,1)} %bitcast_select_fusion.4), channel_id=1, source_target_pairs={{0,6},{1,7},{2,4},{3,5},{4,2},{5,3},{6,0},{7,1},{8,14},{9,15},{10,... | collective-permute-start | bytes 1572872 | tf_op jit(solution)/shard_map/ppermute | solution.py:59
  50.5 55.3 %collective-permute-start.13 = (bf16[128,2048]{1,0:T(8,128)(2,1)}, bf16[128,2048]{1,0:T(8,128)(2,1)}, u32[]{:S(2)}, u32[]{:S(2)}) collective-permute-start(bf16[128,2048]{1,0:T(8,128)(2,1)} %bitcast_select_fusion.4), channel_id=1, source_target_pairs={{0,2},{1,3},{2,0},{3,1},{4,6},{5,7},{6,4},{7,5},{8,10},{9,11},{10,... | collective-permute-start | bytes 1572872 | tf_op jit(solution)/shard_map/ppermute | solution.py:59
  72.8 26.3 %collective-permute-start.2 = (bf16[4,256,512]{2,1,0:T(8,128)(2,1)}, bf16[4,256,512]{2,1,0:T(8,128)(2,1)}, u32[]{:S(2)}, u32[]{:S(2)}) collective-permute-start(bf16[4,256,512]{2,1,0:T(8,128)(2,1)} %slice.273), channel_id=1, source_target_pairs={{0,4},{1,5},{2,6},{3,7},{4,0},{5,1},{6,2},{7,3},{8,12},{9,13},{10,... | collective-permute-start | bytes 3145736 | tf_op jit(solution)/shard_map/ppermute | solution.py:59
  77.8 124.4 %all-gather.17.cloned.1.call-start = ((), (), s32[]{:S(2)}) async-start(), calls=%async_computation.15 | async-start | bytes 2621440 | tf_op jit(solution)/shard_map/all_gather | solution.py:209
  103.0 29.4 %collective-permute-start.9 = (bf16[4,256,512]{2,1,0:T(8,128)(2,1)}, bf16[4,256,512]{2,1,0:T(8,128)(2,1)}, u32[]{:S(2)}, u32[]{:S(2)}) collective-permute-start(bf16[4,256,512]{2,1,0:T(8,128)(2,1)} %get-tuple-element.75), channel_id=1, source_target_pairs={{0,4},{1,5},{2,6},{3,7},{4,0},{5,1},{6,2},{7,3},{8,12},{9,13},{10,... | collective-permute-start | bytes 3145736 | tf_op jit(solution)/shard_map/ppermute | solution.py:59
  113.2 33.3 %collective-permute-start.15 = (bf16[4,128,2048]{2,1,0:T(8,128)(2,1)}, bf16[4,128,2048]{2,1,0:T(8,128)(2,1)}, u32[]{:S(2)}, u32[]{:S(2)}) collective-permute-start(bf16[4,128,2048]{2,1,0:T(8,128)(2,1)} %pad_maximum_fusion.5), channel_id=1, source_target_pairs={{0,1},{1,0},{2,3},{3,2},{4,5},{5,4},{6,7},{7,6},{8,9},{9,8},{10,11... | collective-permute-start | bytes 6291464 | tf_op jit(solution)/shard_map/ppermute | solution.py:59
  137.2 111.7 %all-gather.19.cloned.1.call-start = ((), (), s32[]{:S(2)}) async-start(), calls=%async_computation.16 | async-start | bytes 2621440 | tf_op jit(solution)/shard_map/all_gather | solution.py:209
  203.0 94.8 %reduce-scatter.7.cloned.1.call-start = ((), (), s32[]{:S(2)}) async-start(), calls=%async_computation.6 | async-start | bytes 2621440 | tf_op jit(solution)/shard_map/reduce_scatter | solution.py:212
  248.9 90.3 %reduce-scatter.9.cloned.1.call-start = ((), (), s32[]{:S(2)}) async-start(), calls=%async_computation.7 | async-start | bytes 2621440 | tf_op jit(solution)/shard_map/reduce_scatter | solution.py:212
  268.5 25.1 %collective-permute-start.24 = (bf16[128,2048]{1,0:T(8,128)(2,1)}, bf16[128,2048]{1,0:T(8,128)(2,1)}, u32[]{:S(2)}, u32[]{:S(2)}) collective-permute-start(bf16[128,2048]{1,0:T(8,128)(2,1)} %get-tuple-element.156), channel_id=1, source_target_pairs={{0,6},{1,7},{2,4},{3,5},{4,2},{5,3},{6,0},{7,1},{8,14},{9,15},{10,... | collective-permute-start | bytes 1572872 | tf_op jit(solution)/shard_map/ppermute | solution.py:59
  274.3 110.4 %reduce-scatter.11.cloned.1.call-start = ((), (), s32[]{:S(2)}) async-start(), calls=%async_computation.8 | async-start | bytes 2621440 | tf_op jit(solution)/shard_map/reduce_scatter | solution.py:212
  322.1 141.9 %reduce-scatter.13.cloned.1.call-start = ((), (), s32[]{:S(2)}) async-start(), calls=%async_computation.9 | async-start | bytes 1310720 | tf_op jit(solution)/shard_map/reduce_scatter | solution.py:212
  372.6 30.7 %collective-permute-start.32 = (bf16[4,256,512]{2,1,0:T(8,128)(2,1)}, bf16[4,256,512]{2,1,0:T(8,128)(2,1)}, u32[]{:S(2)}, u32[]{:S(2)}) collective-permute-start(bf16[4,256,512]{2,1,0:T(8,128)(2,1)} %fusion.35), channel_id=1, source_target_pairs={{0,4},{1,5},{2,6},{3,7},{4,0},{5,1},{6,2},{7,3},{8,12},{9,13},{10,... | collective-permute-start | bytes 3145736 | tf_op jit(solution)/shard_map/ppermute | solution.py:59
  413.0 74.5 %reduce-scatter.15.cloned.1.call-start = ((), (), s32[]{:S(2)}) async-start(), calls=%async_computation.10 | async-start | bytes 2621440 | tf_op jit(solution)/shard_map/reduce_scatter | solution.py:212
  436.9 92.0 %reduce-scatter.17.cloned.1.call-start = ((), (), s32[]{:S(2)}) async-start(), calls=%async_computation.11 | async-start | bytes 1310720 | tf_op jit(solution)/shard_map/reduce_scatter | solution.py:212
  460.5 31.0 %collective-permute-start.39 = (bf16[128,2048]{1,0:T(8,128)(2,1)}, bf16[128,2048]{1,0:T(8,128)(2,1)}, u32[]{:S(2)}, u32[]{:S(2)}) collective-permute-start(bf16[128,2048]{1,0:T(8,128)(2,1)} %get-tuple-element.152), channel_id=1, source_target_pairs={{0,4},{1,5},{2,6},{3,7},{4,0},{5,1},{6,2},{7,3},{8,12},{9,13},{10,... | collective-permute-start | bytes 1572872 | tf_op jit(solution)/shard_map/ppermute | solution.py:59
  462.0 31.0 %collective-permute-start.41 = (bf16[128,2048]{1,0:T(8,128)(2,1)}, bf16[128,2048]{1,0:T(8,128)(2,1)}, u32[]{:S(2)}, u32[]{:S(2)}) collective-permute-start(bf16[128,2048]{1,0:T(8,128)(2,1)} %get-tuple-element.153), channel_id=1, source_target_pairs={{0,6},{1,7},{2,4},{3,5},{4,2},{5,3},{6,0},{7,1},{8,14},{9,15},{10,... | collective-permute-start | bytes 1572872 | tf_op jit(solution)/shard_map/ppermute | solution.py:59
  463.5 29.6 %collective-permute-start.40 = (bf16[128,2048]{1,0:T(8,128)(2,1)}, bf16[128,2048]{1,0:T(8,128)(2,1)}, u32[]{:S(2)}, u32[]{:S(2)}) collective-permute-start(bf16[128,2048]{1,0:T(8,128)(2,1)} %get-tuple-element.154), channel_id=1, source_target_pairs={{0,2},{1,3},{2,0},{3,1},{4,6},{5,7},{6,4},{7,5},{8,10},{9,11},{10,... | collective-permute-start | bytes 1572872 | tf_op jit(solution)/shard_map/ppermute | solution.py:59
  470.1 39.1 %collective-permute-start.49 = (bf16[256,1024]{1,0:T(8,128)(2,1)}, bf16[256,1024]{1,0:T(8,128)(2,1)}, u32[]{:S(2)}, u32[]{:S(2)}) collective-permute-start(bf16[256,1024]{1,0:T(8,128)(2,1)} %dynamic-slice_bitcast_fusion.2), channel_id=1, source_target_pairs={{0,4},{1,5},{2,6},{3,7},{4,0},{5,1},{6,2},{7,3},{8,12},{9,13},{10,... | collective-permute-start | bytes 1572872 | tf_op jit(solution)/shard_map/ppermute | solution.py:59
  491.6 29.5 %collective-permute-start.48 = (bf16[256,1024]{1,0:T(8,128)(2,1)}, bf16[256,1024]{1,0:T(8,128)(2,1)}, u32[]{:S(2)}, u32[]{:S(2)}) collective-permute-start(bf16[256,1024]{1,0:T(8,128)(2,1)} %dynamic-slice_bitcast_fusion.3), channel_id=1, source_target_pairs={{0,4},{1,5},{2,6},{3,7},{4,0},{5,1},{6,2},{7,3},{8,12},{9,13},{10,... | collective-permute-start | bytes 1572872 | tf_op jit(solution)/shard_map/ppermute | solution.py:59
  (115 other events, 1157.3 us)
Sparse Core Ops, SparseCore 0:
  10.2 51.4 all-gather.10
  63.2 45.9 all-gather.12
  110.8 44.6 all-gather.14
  157.5 44.6 all-gather.16
  204.2 44.6 all-gather.18
  251.0 42.5 reduce-scatter.6
  296.0 43.1 reduce-scatter.8
  341.5 43.1 reduce-scatter.10
  413.1 24.9 reduce-scatter.12
  440.2 47.2 reduce-scatter.14
  501.4 27.3 reduce-scatter.16

commit v3 on v2

--- a/solution.py
+++ b/solution.py
@@ -105,7 +105,7 @@
         o_ref[:, h * HEAD_DIM : (h + 1) * HEAD_DIM] = out[h * seq_dev : (h + 1) * seq_dev]
 
 
-def backward_kernel(heads, scalars, q_ref, go_ref, kv_ref, pos_ref, gq_ref, gkv_ref):
+def backward_kernel(heads, scalars, q_ref, go_ref, kv_ref, pos_ref, gq_ref, gkv_ref, total_ref):
     seq_dev = q_ref.shape[0]
     key = kv_ref[0, :, :HEAD_DIM]
     value = kv_ref[0, :, HEAD_DIM:]
@@ -128,16 +128,21 @@
         gq_ref[:, h * HEAD_DIM : (h + 1) * HEAD_DIM] = out[h * seq_dev : (h + 1) * seq_dev]
     key_grad = row_dot(score_grad, query) * SCALE
     value_grad = row_dot(prob_low, grad)
+    last = pl.num_programs(1) - 1
+
+    @pl.when(pl.program_id(1) > 0)
+    def _():
+        total_ref[:, :HEAD_DIM] += key_grad
+        total_ref[:, HEAD_DIM:] += value_grad
 
     @pl.when(pl.program_id(1) == 0)
     def _():
-        gkv_ref[0, :, :HEAD_DIM] = key_grad
-        gkv_ref[0, :, HEAD_DIM:] = value_grad
-
-    @pl.when(pl.program_id(1) > 0)
+        total_ref[:, :HEAD_DIM] = key_grad
+        total_ref[:, HEAD_DIM:] = value_grad
+
+    @pl.when(pl.program_id(1) == last)
     def _():
-        gkv_ref[0, :, :HEAD_DIM] += key_grad
-        gkv_ref[0, :, HEAD_DIM:] += value_grad
+        gkv_ref[0] = total_ref[...].astype(LOW)
 
 
 def attention_call(kernel, outs, scalars, rows, keys, key_pos, seq_dev, flops):
@@ -149,7 +154,7 @@
     pos_spec = pl.BlockSpec((1, key_count), lambda s, g, *_: (0, 0))
     shapes = {
         "row": (jax.ShapeDtypeStruct(rows[0].shape, LOW), row_spec),
-        "key": (jax.ShapeDtypeStruct(keys.shape, jnp.float32), key_spec),
+        "key": (jax.ShapeDtypeStruct(keys.shape, LOW), key_spec),
     }
     return pl.pallas_call(
         partial(kernel, heads),
@@ -158,6 +163,7 @@
             grid=(slots, heads_dev // heads),
             in_specs=[row_spec] * len(rows) + [key_spec, pos_spec],
             out_specs=[shapes[o][1] for o in outs],
+            scratch_shapes=[pltpu.VMEM(keys.shape[1:], jnp.float32) for o in outs if o == "key"],
         ),
         out_shape=[shapes[o][0] for o in outs],
         compiler_params=pltpu.CompilerParams(vmem_limit_bytes=50 * 1024 * 1024),
@@ -167,6 +173,81 @@
             transcendentals=slots * heads_dev * seq_dev * key_count,
         ),
     )(scalars, *rows, keys, key_pos)
+
+
+def at(index, count):
+    return pl.ds(pl.multiple_of(index * count, count), count)
+
+
+def put_lines(ref, start, lines):
+    first = lines.astype(LOW)
+    count = lines.shape[0]
+    ref[start : start + count] = first
+    ref[start + count : start + 2 * count] = (lines - wide(first)).astype(LOW)
+
+
+def get_lines(ref, start):
+    count = (ref.shape[0] - start) // 2
+    return wide(ref[start : start + count]) + wide(ref[start + count : start + 2 * count])
+
+
+def first_stage(where, in_ref, grad_ref, lines_ref, send_ref, keep_ref, total_ref):
+    total_ref[...] = row_dot(in_ref[...], grad_ref[...])
+    count = keep_ref.shape[0]
+    send_ref[:count] = total_ref[at(1 - where[0], count)].astype(LOW)
+    keep_ref[...] = total_ref[at(where[0], count)]
+    put_lines(send_ref, count, lines_ref[...])
+
+
+def plane_stage(where, got_ref, sent_ref, keep_ref, *rest):
+    *sends, mine_ref, total_ref = rest
+    count, part = keep_ref.shape[0], mine_ref.shape[0]
+    total_ref[...] = keep_ref[...] + wide(got_ref[:count])
+    lines = get_lines(sent_ref, count) + get_lines(got_ref, count)
+    mine_ref[...] = total_ref[at(where[1], part)]
+    for i, send in enumerate(sends):
+        send[:part] = total_ref[at(where[2 + i], part)].astype(LOW)
+        put_lines(send, part, lines)
+
+
+def plane_sum(x_ref, y_ref, xy_ref, sent_ref, mine_ref, send_ref):
+    part = mine_ref.shape[0]
+    total = mine_ref[...] + wide(x_ref[:part]) + wide(y_ref[:part]) + wide(xy_ref[:part])
+    send_ref[:part] = total.astype(LOW)
+    lines = get_lines(sent_ref, part) + get_lines(x_ref, part)
+    put_lines(send_ref, part, lines + (get_lines(y_ref, part) + get_lines(xy_ref, part)))
+
+
+def pair_sum(part, got_ref, sent_ref, send_ref):
+    send_ref[:part] = (wide(sent_ref[:part]) + wide(got_ref[:part])).astype(LOW)
+    put_lines(send_ref, part, get_lines(sent_ref, part) + get_lines(got_ref, part))
+
+
+def last_sum(part, got_ref, sent_ref, rows_ref, lines_ref):
+    rows_ref[...] = (wide(sent_ref[:part]) + wide(got_ref[:part])).astype(LOW)
+    lines_ref[...] = get_lines(sent_ref, part) + get_lines(got_ref, part)
+
+
+def join_stage(first, where, *refs):
+    *parts, whole_ref = refs
+    for i, part in enumerate(parts):
+        whole_ref[at(where[first + i], part.shape[0])] = part[...].astype(whole_ref.dtype)
+
+
+def small_call(kernel, outs, *args, scratch=(), where=None):
+    lead = [] if where is None else [where]
+    specs = [pl.BlockSpec(memory_space=pltpu.SMEM)] * len(lead)
+    return pl.pallas_call(
+        kernel,
+        in_specs=specs + [pl.BlockSpec(memory_space=pltpu.VMEM)] * len(args),
+        out_specs=[pl.BlockSpec(memory_space=pltpu.VMEM)] * len(outs),
+        out_shape=[jax.ShapeDtypeStruct(*o) for o in outs],
+        scratch_shapes=[pltpu.VMEM(*v) for v in scratch],
+        compiler_params=pltpu.CompilerParams(vmem_limit_bytes=24 * 1024 * 1024),
+        cost_estimate=pl.CostEstimate(
+            flops=1024 * 1024, bytes_accessed=2 * 1024 * 1024, transcendentals=0
+        ),
+    )(*lead, *args)
 
 
 def on_device(
@@ -202,7 +283,7 @@
     ff_dev = w_up.shape[1]
     unit = ff_dev // 2
     part_unit = unit // 2
-    plane = [(1, 0), (0, 2), (1, 2)]
+    plane = [(0, 2), (1, 0), (1, 2)]
     z_groups = [[2 * i + j for i in range(z_count)] for j in range(2)]
 
     def gather_z(values):
@@ -255,15 +336,14 @@
     mine = gather_z(jnp.concatenate([w_q, w_out]))
     mine_q, mine_out = mine[:, :depth], mine[:, depth:]
     full_q = gather_x(mine_q)
-    def gather_units(weights):
-        mine = swap_units(weights)
+    def gather_units(mine):
         return [
             gather_z(mine[:, i * part_unit : (i + 1) * part_unit]).reshape(width, part_unit)
             for i in range(2)
         ]
 
-    full_up = gather_units(w_up)
-    full_down = gather_units(w_down)
+    full_up = gather_units(swap_units(w_up))
+    mine_down = swap_units(w_down)
 
     own_rows = wide(block_in[0])
     positions = jnp.arange(seq_dev, dtype=jnp.int32)
@@ -276,6 +356,8 @@
         keys = jnp.stack([keys, flip(keys, blk_bits=bit)], axis=1)
         keys = keys.reshape((-1,) + keys.shape[2:])
         bit //= 2
+    keys, mine_down = tie(keys, mine_down)
+    full_down = gather_z(mine_down).reshape(width, unit)
     keys = gather_head(keys).reshape(slots, blk_count * seq_dev, 2 * HEAD_DIM)
     key_blocks = blk ^ jnp.arange(blk_count, dtype=jnp.int32)
     key_pos = (key_blocks[:, None] * seq_dev + positions[None, :]).reshape(1, -1)
@@ -284,23 +366,23 @@
     group_in = gather_head(attn_in).reshape(slots * seq_dev, width)
 
     own_cot = jnp.where(own_valid[:, None], out_cot[0], jnp.zeros_like(out_cot[0]))
-    cot_rows = gather_core(gather_xy(own_cot))
+    cot_mine = pair_y(own_cot)
     own_cot = wide(own_cot)
 
     column_start = head * q_dev
     query_bias = lax.dynamic_slice_in_dim(b_q, column_start, q_dev)
     queries = (plain_dot(group_in, full_q) + query_bias).astype(LOW)
-    queries, mine_out = tie(queries, mine_out)
+    queries, mine_out, cot_mine = tie(queries, mine_out, cot_mine)
     full_out = gather_x(mine_out)
     (attn_low,) = attention_call(
         forward_kernel, ("row",), scalars, (queries,), keys, key_pos, seq_dev, 2
     )
-    attn_low, full_up[0] = tie(attn_low, full_up[0])
+    attn_low, full_up[0], cot_mine = tie(attn_low, full_up[0], cot_mine)
+    cot_rows = gather_core(jnp.concatenate([cot_mine, flip(cot_mine, blk_bits=1)]))
     hidden_res = own_rows + add_y(add_core([attn_low], [full_out])) + b_out
     hidden_res, full_up[1], cot_rows = tie(hidden_res, full_up[1], cot_rows)
     normed_two = layer_norm(hidden_res, ln2_gain, ln2_bias).astype(LOW)
-    mine_in, full_down[0] = tie(gather_xy(normed_two), full_down[0])
-    ffn_in = gather_core(mine_in)
+    ffn_in = gather_core(gather_xy(normed_two))
     unit_start = head * ff_dev + x * unit
 
     def gelu(i):
@@ -317,12 +399,12 @@
     activated = tie(*activated)
     grad_down = [low(row_dot(cot_rows, v)) for v in activated]
 
-    def back(i):
-        return low(gelu_pulls[i](plain_dot(cot_rows, full_down[i]))[0])
-
-    *grad_down, first_rows, full_down[1] = tie(*grad_down, back(0), full_down[1])
+    *grad_down, full_down = tie(*grad_down, full_down)
     sums_down = [scatter_units(grad_down[0])]
-    grad_up_rows = [first_rows, back(1)]
+    grad_act = plain_dot(cot_rows, full_down)
+    grad_up_rows = [
+        low(gelu_pulls[i](grad_act[:, i * part_unit : (i + 1) * part_unit])[0]) for i in range(2)
+    ]
     in_half = add_core(grad_up_rows, full_up)
     in_half, activated, grad_up_rows, grad_down = tie(
         in_half, activated, grad_up_rows, grad_down[1]
@@ -333,7 +415,7 @@
     ffn_in_grad, sums_down[0], grad_up, activated = tie(
         ffn_in_grad, sums_down[0], grad_up, activated
     )
-    ffn_half = add_core(activated, full_down)
+    ffn_half = add_core([jnp.concatenate(activated, axis=-1)], [full_down])
     sums_up = [scatter_units(v) for v in grad_up]
     grad_up_bias = jnp.concatenate(
         [jnp.sum(v, axis=0, dtype=jnp.float32) for v in grad_up_rows]
@@ -358,9 +440,9 @@
         5,
     )
     kv_grad = kv_grad.reshape(slots, blk_count, seq_dev, 2 * HEAD_DIM)
-    half_kv = kv_grad[:2] + wide(flip(low(kv_grad[2:]), head_bits=1))
+    half_kv = wide(kv_grad[:2]) + wide(flip(kv_grad[2:], head_bits=1))
+    half_kv, query_low, cot_late, in_late = tie(half_kv, query_low, cot_attn, group_in)
     half_in = add_core([query_low], [full_q])
-    half_kv, half_in, cot_late, in_late = tie(half_kv, half_in, cot_attn, group_in)
 
     def sides(grads):
         parts = grads.reshape(z_count, 2, depth, q_dev)
@@ -368,7 +450,9 @@
 
     grad_q, q_across = sides(row_dot(in_late, query_low))
     q_across = flip(q_across, blk_bits=1)
-    part, grad_q, cot_late, sums_up[0] = tie(add_y(half_kv), grad_q, cot_late, sums_up[0])
+    part, half_in, grad_q, cot_late, sums_up[0] = tie(
+        add_y(half_kv), half_in, grad_q, cot_late, sums_up[0]
+    )
     grad_out, out_across = sides(row_dot(cot_late, attn_low))
     bit = 1
     while bit < blk_count:
@@ -393,8 +477,6 @@
             jnp.concatenate([jnp.where(first, own, other), jnp.where(first, other, own)], axis=-1)
         )
 
-    grad_kv, out_across = tie(row_dot(attn_in, own_kv_grad), out_across)
-    out_total = low(grad_out + wide(out_across))
     grad_b_q = lax.dynamic_update_slice_in_dim(
         jnp.zeros((width,), jnp.float32),
         jnp.sum(query_low, axis=0, dtype=jnp.float32),
@@ -422,42 +504,64 @@
     ).reshape(-1, 2 * HEAD_DIM)
     line_count = lines.shape[0]
 
-    def exchange(lines, rows, **bits):
-        first = rounded(lines)
-        second = rounded(lines - first)
-        got = flip(jnp.concatenate([low(first), low(second), low(rows)]), **bits)
-        lines = (first + second) + (wide(got[:line_count]) + wide(got[line_count : 2 * line_count]))
-        return lines, wide(got[2 * line_count :])
-
-    def halved(lines, rows, index, **bits):
-        pair = rows.reshape((2, -1) + rows.shape[1:])
-        lines, got = exchange(lines, take(pair, 1 - index, 0), **bits)
-        return lines, take(pair, index, 0) + got
-
-    def joined(values, index, **bits):
-        whole = in_order(values, flip(values, **bits), index, 0)
-        return whole.reshape((-1,) + values.shape[1:])
-
-    lines, rows = halved(lines, grad_kv, core, head_bits=1)
-    lines, rows = halved(lines, rows, x, blk_bits=1)
-    rows, ffn_half = tie(rows, ffn_half)
+    columns = 2 * HEAD_DIM
+    rows_half, rows_part = width // 2, width // 8
+    message = (rows_part + 2 * line_count, columns)
+    where = jnp.stack(
+        [core, 2 * x + y, 2 * x + 1 - y, 2 * (1 - x) + y, 2 * (1 - x) + 1 - y, core, 1 - core]
+    ).astype(jnp.int32)
+    sent, keep = small_call(
+        first_stage,
+        [((rows_half + 2 * line_count, columns), LOW), ((rows_half, columns), jnp.float32)],
+        attn_in,
+        own_kv_grad,
+        lines,
+        scratch=[((width, columns), jnp.float32)],
+        where=where,
+    )
+    *sent, keep = small_call(
+        plane_stage,
+        [(message, LOW)] * 3 + [((rows_part, columns), jnp.float32)],
+        flip(sent, head_bits=1),
+        sent,
+        keep,
+        scratch=[((rows_half, columns), jnp.float32)],
+        where=where,
+    )
+    got = [flip(v, *bits) for v, bits in zip(sent, plane)]
+    (sent,) = small_call(plane_sum, [(message, LOW)], *got, sent[0], keep)
+    sent, ffn_half, sums_down, out_across = tie(sent, ffn_half, sums_down, out_across)
+    sum_out = wide(scatter_z(low(grad_out + wide(out_across))))
     output = low(hidden_res + plane_xy(ffn_half) + b_down)[None]
-    lines, rows = halved(lines, rows, y, head_bits=2)
-    rows, sums_down = tie(rows, sums_down)
     sum_down = ff_sum(sums_down)
     bit = 2
-    while bit < blk_count:
-        lines, got = exchange(lines, rows, blk_bits=bit)
-        rows = rounded(rows) + got
-        if bit == 2:
-            rows, sum_q, sums_up[1] = tie(rows, sum_q, sums_up[1])
-            sum_up = ff_sum(sums_up)
+    while 2 * bit < blk_count:
+        (sent,) = small_call(
+            partial(pair_sum, rows_part), [(message, LOW)], flip(sent, blk_bits=bit), sent
+        )
         bit *= 2
-    rows, out_total = tie(rows, out_total)
-    sum_out = wide(scatter_z(out_total))
-    rows = joined(low(rows), y, head_bits=2)
-    rows = joined(rows, x, blk_bits=1)
-    sum_kv = wide(joined(rows, core, head_bits=1))
+    rows, lines = small_call(
+        partial(last_sum, rows_part),
+        [((rows_part, columns), LOW), ((line_count, columns), jnp.float32)],
+        flip(sent, blk_bits=bit),
+        sent,
+    )
+    rows, sum_q, sums_up[1] = tie(rows, sum_q, sums_up[1])
+    sum_up = ff_sum(sums_up)
+    (rows,) = small_call(
+        partial(join_stage, 1),
+        [((rows_half, columns), LOW)],
+        rows,
+        *[flip(rows, *bits) for bits in plane],
+        where=where,
+    )
+    (sum_kv,) = small_call(
+        partial(join_stage, 5),
+        [((width, columns), jnp.float32)],
+        rows,
+        flip(rows, head_bits=1),
+        where=where,
+    )
     lines = lines.reshape(-1, width)
     (
         sum_ln1_gain,

time: 546 us -> 536 us (0.982)
  waiting for transfers between devices: 258 us -> 247 us
  local copies, waits for them, and re-layouts: 49.8 us -> 43.6 us
    all_gather x5 -> x4, waiting for transfers between devices: 35.9 us -> 24.5 us  [gather_z(): return lax.all_gather(values, 'blk', axis=0, axis_index_groups=z_groups)]
    unnamed x170 -> x167, local copies, waits for them, and re-layouts: 19.9 us -> 15.7 us
    ppermute x50 -> x51, waiting for transfers between devices: 201 us -> 205 us  [flip(): return lax.ppermute(values, ('blk', 'head'), pairs)]
    dot_general x7 -> x6, matrix products: 19.6 us -> 23.1 us  [plain_dot(): return jnp.dot(left, right, preferred_element_type=jnp.float32)]
    ppermute x50 -> x51, starting transfers between devices: 52.6 us -> 49.6 us  [flip(): return lax.ppermute(values, ('blk', 'head'), pairs)]
    dot_general x13 -> x11, matrix products: 27 us -> 24.4 us  [col_dot(): lax.dot_general(left, right, (((1,), (1,)), ((), ())), preferred_element_...]
    dot_general x7 -> x6, matrix products: 22.2 us -> 21.7 us  [row_dot(): lax.dot_general(left, right, (((0,), (0,)), ((), ())), preferred_element_...]
  transfers between devices with their start and end apart: 61 -> 61, of which waited for: 37 -> 35; matrix products, arithmetic and copies ran while one was open for 33% -> 31% of each run, Pallas kernels for 3% -> 4%
where the time goes in v3:
time: 536 us; the launch traced here: 528 us
  waiting for transfers between devices  247 us (46%)
  other arithmetic  78.4 us (15%)
  matrix products  69.2 us (13%)
  starting transfers between devices  50.8 us (9%)
  local copies, waits for them, and re-layouts  43.6 us (8%)
  Pallas kernels  22.6 us (4%)
  between operations  15.7 us (3%)
    ppermute x51, waiting for transfers between devices, flip(): return lax.ppermute(values, ('blk', 'head'), pairs)  205 us
    ppermute x51, starting transfers between devices, flip(): return lax.ppermute(values, ('blk', 'head'), pairs)  49.6 us
    all_gather x4, waiting for transfers between devices, gather_z(): return lax.all_gather(values, 'blk', axis=0, axis_index_groups=z_groups)  24.5 us
    dot_general x11, matrix products, col_dot(): lax.dot_general(left, right, (((1,), (1,)), ((), ())), preferred_element_...  24.4 us
    dot_general x6, matrix products, plain_dot(): return jnp.dot(left, right, preferred_element_type=jnp.float32)  23.1 us
    dot_general x6, matrix products, row_dot(): lax.dot_general(left, right, (((0,), (0,)), ((), ())), preferred_element_...  21.7 us
    pallas_call x2, Pallas kernels, attention_call(): pl.pallas_call(partial(kernel, heads), grid_spec=pltpu.PrefetchScalarGrid...  17.9 us
    reduce_scatter x6, waiting for transfers between devices, scatter_z(): lax.psum_scatter(values, 'blk', scatter_dimension=0, axis_index_groups=z_...  17.4 us
  transfers between devices with their start and end apart: 61, of which 35 were waited for; matrix products, arithmetic and copies ran while one was open for 31% of the time, Pallas kernels for 4%

profile of v3, /device:TPU:0, one launch (start us, length us, event | category | flops | bytes accessed | tf_op | source)
XLA Modules:
  0.0 527.7 jit_solution(3586416011280612964)
XLA Ops:
  29.4 12.9 %collective-permute-done.5 = bf16[2,128,256]{2,1,0:T(8,128)(2,1)S(1)} collective-permute-done((bf16[2,128,256]{2,1,0:T(8,128)(2,1)S(1)}, bf16[2,128,256]{2,1,0:T(8,128)(2,1)S(1)}, u32[]{:S(2)}, u32[]{:S(2)}) %collective-permute-start.5) | collective-permute-done | bytes 131104 | tf_op jit(solution)/shard_map/ppermute | solution.py:59
  65.4 7.0 %collective-permute-done.8 = bf16[8,128,256]{2,1,0:T(8,128)(2,1)} collective-permute-done((bf16[8,128,256]{2,1,0:T(8,128)(2,1)}, bf16[8,128,256]{2,1,0:T(8,128)(2,1)}, u32[]{:S(2)}, u32[]{:S(2)}) %collective-permute-start.8) | collective-permute-done | bytes 524320 | tf_op jit(solution)/shard_map/ppermute | solution.py:59
  76.2 10.3 %collective-permute-done.2 = bf16[4,256,512]{2,1,0:T(8,128)(2,1)S(1)} collective-permute-done((bf16[4,256,512]{2,1,0:T(8,128)(2,1)S(1)}, bf16[4,256,512]{2,1,0:T(8,128)(2,1)S(1)}, u32[]{:S(2)}, u32[]{:S(2)}) %collective-permute-start.2) | collective-permute-done | bytes 1048608 | tf_op jit(solution)/shard_map/ppermute | solution.py:59
  93.4 7.3 %shard_map.297 = bf16[512,512]{1,0:T(8,128)(2,1)S(1)} custom-call(s32[5]{0:T(128)S(1)} %pad_add_fusion.scalars, bf16[512,512]{1,0:T(8,128)(2,1)S(1)} %fusion.20.q_ref, bf16[4,1024,256]{2,1,0:T(8,128)(2,1)S(1)} %pad_maximum_fusion.3.kv_ref, s32[1,1024]{1,0:T(1,128)S(1)} %bitcast.307), custom_call_target="tpu_custom_call" | custom-call | flops 1073741824 | bytes 8388608 | tf_op jit(solution)/shard_map/pallas_call | solution.py:159
  102.0 7.0 %all-gather.11.cloned.1.call-done = bf16[2048,512]{1,0:T(8,128)(2,1)} async-done(((bf16[512,512]{1,0:T(8,128)(2,1)}), bf16[2048,512]{1,0:T(8,128)(2,1)}) %all-gather.11.cloned.1.call-update) | async-done | bytes 2097168 | tf_op jit(solution)/shard_map/all_gather | solution.py:290
  118.7 17.4 %collective-permute-done.14 = bf16[2,128,2048]{2,1,0:T(8,128)(2,1)S(1)} collective-permute-done((bf16[2,128,2048]{2,1,0:T(8,128)(2,1)}, bf16[2,128,2048]{2,1,0:T(8,128)(2,1)S(1)}, u32[]{:S(2)}, u32[]{:S(2)}) %collective-permute-start.14) | collective-permute-done | bytes 1048608 | tf_op jit(solution)/shard_map/ppermute | solution.py:59
  141.7 13.1 %collective-permute-done.13 = bf16[128,2048]{1,0:T(8,128)(2,1)} collective-permute-done((bf16[128,2048]{1,0:T(8,128)(2,1)}, bf16[128,2048]{1,0:T(8,128)(2,1)}, u32[]{:S(2)}, u32[]{:S(2)}) %collective-permute-start.13) | collective-permute-done | bytes 524320 | tf_op jit(solution)/shard_map/ppermute | solution.py:59
  170.0 10.5 %collective-permute-done.16 = bf16[128,2048]{1,0:T(8,128)(2,1)S(1)} collective-permute-done((bf16[128,2048]{1,0:T(8,128)(2,1)S(1)}, bf16[128,2048]{1,0:T(8,128)(2,1)S(1)}, u32[]{:S(2)}, u32[]{:S(2)}) %collective-permute-start.16) | collective-permute-done | bytes 524320 | tf_op jit(solution)/shard_map/ppermute | solution.py:59
  182.7 9.6 %collective-permute-done.18 = bf16[128,2048]{1,0:T(8,128)(2,1)S(1)} collective-permute-done((bf16[128,2048]{1,0:T(8,128)(2,1)S(1)}, bf16[128,2048]{1,0:T(8,128)(2,1)S(1)}, u32[]{:S(2)}, u32[]{:S(2)}) %collective-permute-start.18) | collective-permute-done | bytes 524320 | tf_op jit(solution)/shard_map/ppermute | solution.py:59
  201.8 6.4 %multiply_convert_fusion.1 = (bf16[1024,512]{1,0:T(8,128)(2,1)S(1)}, f32[1024,512]{1,0:T(8,128)}) fusion(f32[512]{0:T(512)S(1)} %get-tuple-element.193, bf16[1024,2048]{1,0:T(8,128)(2,1)} %bitcast.367, bf16[2048,512]{1,0:T(8,128)(2,1)S(1)} %copy-done.29), kind=kOutput, calls=%fused_computation.48 | convolution fusion | flops 2152726528 | bytes 9439232 | tf_op jit(solution)/shard_map/dot_general | solution.py:24
  219.8 16.4 %all-gather.15.cloned.1.call-done = bf16[2048,1024]{1,0:T(8,128)(2,1)} async-done(((bf16[512,1024]{1,0:T(8,128)(2,1)}), bf16[2048,1024]{1,0:T(8,128)(2,1)}) %all-gather.15.cloned.1.call-update) | async-done | bytes 4194320 | tf_op jit(solution)/shard_map/all_gather | solution.py:290
  236.2 7.6 %fusion.89 = f32[1024,1024]{1,0:T(8,128)S(1)} fusion(bf16[1024,2048]{1,0:T(8,128)(2,1)} %bitcast.334, bf16[2048,1024]{1,0:T(8,128)(2,1)} %all-gather.15.cloned.1.call-done), kind=kOutput, calls=%fused_computation.221 | convolution fusion | flops 4294967296 | bytes 12582912 | tf_op jit(solution)/shard_map/dot_general | solution.py:24
  272.3 6.3 %convolution_convert_fusion.1 = bf16[2048,512]{1,0:T(8,128)(2,1)} fusion(bf16[1024,2048]{1,0:T(8,128)(2,1)} %bitcast.368, bf16[1024,512]{1,0:T(8,128)(2,1)} %get-tuple-element.97), kind=kOutput, calls=%fused_computation.10 | convolution fusion | flops 2148532224 | bytes 7340032 | tf_op jit(solution)/shard_map/dot_general | solution.py:28
  280.5 10.6 %collective-permute-done.22 = bf16[128,2048]{1,0:T(8,128)(2,1)} collective-permute-done((bf16[128,2048]{1,0:T(8,128)(2,1)}, bf16[128,2048]{1,0:T(8,128)(2,1)}, u32[]{:S(2)}, u32[]{:S(2)}) %collective-permute-start.22) | collective-permute-done | bytes 524320 | tf_op jit(solution)/shard_map/ppermute | solution.py:59
  303.6 12.9 %collective-permute-done.24 = bf16[128,2048]{1,0:T(8,128)(2,1)S(1)} collective-permute-done((bf16[128,2048]{1,0:T(8,128)(2,1)S(1)}, bf16[128,2048]{1,0:T(8,128)(2,1)S(1)}, u32[]{:S(2)}, u32[]{:S(2)}) %collective-permute-start.24) | collective-permute-done | bytes 524320 | tf_op jit(solution)/shard_map/ppermute | solution.py:59
  328.1 11.2 %reduce-scatter.9.cloned.1.call-done = bf16[1,512,512]{2,1,0:T(8,128)(2,1)} async-done(((bf16[4,512,512]{2,1,0:T(8,128)(2,1)}), bf16[1,512,512]{2,1,0:T(8,128)(2,1)}) %reduce-scatter.9.cloned.1.call-update) | async-done | bytes 524304 | tf_op jit(solution)/shard_map/reduce_scatter | solution.py:293
  342.8 10.6 %shard_map.298 = (bf16[512,512]{1,0:T(8,128)(2,1)S(1)}, bf16[4,1024,256]{2,1,0:T(8,128)(2,1)S(1)}) custom-call(s32[5]{0:T(128)S(1)} %pad_add_fusion.scalars, bf16[512,512]{1,0:T(8,128)(2,1)S(1)} %fusion.20.q_ref, bf16[512,512]{1,0:T(8,128)(2,1)S(1)} %convolution_convert_fusion.7.go_ref, bf16[4,1024,256]{2,1,0:T(8,128)(2,1)} %copy-done.1, s32[1,1024]{1,0:T(1,128)S(1)} %bitcast.308), custom_call_target="tpu_custom_call" | custom-call | flops 2684354560 | bytes 8388608 | tf_op jit(solution)/shard_map/pallas_call | solution.py:159
  368.1 7.3 %collective-permute-done.28 = bf16[8,128,256]{2,1,0:T(8,128)(2,1)S(1)} collective-permute-done((bf16[8,128,256]{2,1,0:T(8,128)(2,1)S(1)}, bf16[8,128,256]{2,1,0:T(8,128)(2,1)S(1)}, u32[]{:S(2)}, u32[]{:S(2)}) %collective-permute-start.28) | collective-permute-done | bytes 524320 | tf_op jit(solution)/shard_map/ppermute | solution.py:59
  378.6 6.3 %reduce-scatter.11.cloned.1.call-done = bf16[1,512,512]{2,1,0:T(8,128)(2,1)} async-done(((bf16[4,512,512]{2,1,0:T(8,128)(2,1)}), bf16[1,512,512]{2,1,0:T(8,128)(2,1)}) %reduce-scatter.11.cloned.1.call-update) | async-done | bytes 524304 | tf_op jit(solution)/shard_map/reduce_scatter | solution.py:293
  405.1 7.1 %collective-permute-done.32 = bf16[2,128,256]{2,1,0:T(8,128)(2,1)S(1)} collective-permute-done((bf16[2,128,256]{2,1,0:T(8,128)(2,1)S(1)}, bf16[2,128,256]{2,1,0:T(8,128)(2,1)S(1)}, u32[]{:S(2)}, u32[]{:S(2)}) %collective-permute-start.32) | collective-permute-done | bytes 131104 | tf_op jit(solution)/shard_map/ppermute | solution.py:59
  415.5 7.4 %collective-permute-done.33 = bf16[1,128,256]{2,1,0:T(8,128)(2,1)S(1)} collective-permute-done((bf16[1,128,256]{2,1,0:T(8,128)(2,1)S(1)}, bf16[1,128,256]{2,1,0:T(8,128)(2,1)S(1)}, u32[]{:S(2)}, u32[]{:S(2)}) %collective-permute-start.33) | collective-permute-done | bytes 65568 | tf_op jit(solution)/shard_map/ppermute | solution.py:59
  452.0 15.9 %collective-permute-done.43.got_ref = bf16[448,256]{1,0:T(8,128)(2,1)S(1)} collective-permute-done((bf16[448,256]{1,0:T(8,128)(2,1)S(1)}, bf16[448,256]{1,0:T(8,128)(2,1)S(1)}, u32[]{:S(2)}, u32[]{:S(2)}) %collective-permute-start.43) | collective-permute-done | bytes 229408 | tf_op jit(solution)/shard_map/ppermute | solution.py:59
  469.7 13.2 %collective-permute-done.44.got_ref = bf16[448,256]{1,0:T(8,128)(2,1)S(1)} collective-permute-done((bf16[448,256]{1,0:T(8,128)(2,1)S(1)}, bf16[448,256]{1,0:T(8,128)(2,1)S(1)}, u32[]{:S(2)}, u32[]{:S(2)}) %collective-permute-start.44) | collective-permute-done | bytes 229408 | tf_op jit(solution)/shard_map/ppermute | solution.py:59
  502.5 9.6 %collective-permute-done.46.refs_2_ = bf16[256,256]{1,0:T(8,128)(2,1)S(1)} collective-permute-done((bf16[256,256]{1,0:T(8,128)(2,1)S(1)}, bf16[256,256]{1,0:T(8,128)(2,1)S(1)}, u32[]{:S(2)}, u32[]{:S(2)}) %collective-permute-start.46) | collective-permute-done | bytes 131104 | tf_op jit(solution)/shard_map/ppermute | solution.py:59
  (420 shorter events, 268.1 us)
Async XLA Ops:
  7.3 53.0 %all-gather.9.cloned.1.call-start = ((), (), s32[]{:S(2)}) async-start(), calls=%async_computation.12 | async-start | bytes 2621440 | tf_op jit(solution)/shard_map/all_gather | solution.py:290
  9.3 99.7 %all-gather.11.cloned.1.call-start = ((), (), s32[]{:S(2)}) async-start(), calls=%async_computation.13 | async-start | bytes 2621440 | tf_op jit(solution)/shard_map/all_gather | solution.py:290
  11.3 41.2 %collective-permute-start = (bf16[128,2048]{1,0:T(8,128)(2,1)S(1)}, bf16[128,2048]{1,0:T(8,128)(2,1)}, u32[]{:S(2)}, u32[]{:S(2)}) collective-permute-start(bf16[128,2048]{1,0:T(8,128)(2,1)S(1)} %fusion.25.in_ref), channel_id=1, source_target_pairs={{0,2},{1,3},{2,0},{3,1},{4,6},{5,7},{6,4},{7,5},{8,10},{9,11},{10,... | collective-permute-start | bytes 1572872 | tf_op jit(solution)/shard_map/ppermute | solution.py:59
  16.5 46.7 %collective-permute-start.3 = (bf16[128,2048]{1,0:T(8,128)(2,1)}, bf16[128,2048]{1,0:T(8,128)(2,1)}, u32[]{:S(2)}, u32[]{:S(2)}) collective-permute-start(bf16[128,2048]{1,0:T(8,128)(2,1)} %bitcast_select_fusion.4), channel_id=1, source_target_pairs={{0,2},{1,3},{2,0},{3,1},{4,6},{5,7},{6,4},{7,5},{8,10},{9,11},{10,... | collective-permute-start | bytes 1572872 | tf_op jit(solution)/shard_map/ppermute | solution.py:59
  25.3 23.1 %collective-permute-start.7 = (bf16[256,1024]{1,0:T(8,128)(2,1)}, bf16[256,1024]{1,0:T(8,128)(2,1)}, u32[]{:S(2)}, u32[]{:S(2)}) collective-permute-start(bf16[256,1024]{1,0:T(8,128)(2,1)} %constant_dynamic-slice_fusion.1), channel_id=1, source_target_pairs={{0,4},{1,5},{2,6},{3,7},{4,0},{5,1},{6,2},{7,3},{8,12},{9,13},{10,... | collective-permute-start | bytes 1572872 | tf_op jit(solution)/shard_map/ppermute | solution.py:59
  52.5 108.5 %all-gather.13.cloned.1.call-start = ((), (), s32[]{:S(2)}) async-start(), calls=%async_computation.14 | async-start | bytes 2621440 | tf_op jit(solution)/shard_map/all_gather | solution.py:290
  61.6 25.0 %collective-permute-start.2 = (bf16[4,256,512]{2,1,0:T(8,128)(2,1)S(1)}, bf16[4,256,512]{2,1,0:T(8,128)(2,1)S(1)}, u32[]{:S(2)}, u32[]{:S(2)}) collective-permute-start(bf16[4,256,512]{2,1,0:T(8,128)(2,1)S(1)} %slice.204), channel_id=1, source_target_pairs={{0,4},{1,5},{2,6},{3,7},{4,0},{5,1},{6,2},{7,3},{8,12},{9,13},{10,... | collective-permute-start | bytes 3145736 | tf_op jit(solution)/shard_map/ppermute | solution.py:59
  89.3 26.4 %collective-permute-start.11 = (bf16[4,256,512]{2,1,0:T(8,128)(2,1)}, bf16[4,256,512]{2,1,0:T(8,128)(2,1)}, u32[]{:S(2)}, u32[]{:S(2)}) collective-permute-start(bf16[4,256,512]{2,1,0:T(8,128)(2,1)} %get-tuple-element.83), channel_id=1, source_target_pairs={{0,4},{1,5},{2,6},{3,7},{4,0},{5,1},{6,2},{7,3},{8,12},{9,13},{10,... | collective-permute-start | bytes 3145736 | tf_op jit(solution)/shard_map/ppermute | solution.py:59
  91.6 144.6 %all-gather.15.cloned.1.call-start = ((), (), s32[]{:S(2)}) async-start(), calls=%async_computation.15 | async-start | bytes 5242880 | tf_op jit(solution)/shard_map/all_gather | solution.py:290
  109.0 27.1 %collective-permute-start.14 = (bf16[2,128,2048]{2,1,0:T(8,128)(2,1)}, bf16[2,128,2048]{2,1,0:T(8,128)(2,1)S(1)}, u32[]{:S(2)}, u32[]{:S(2)}) collective-permute-start(bf16[2,128,2048]{2,1,0:T(8,128)(2,1)} %pad_maximum_fusion.9), channel_id=1, source_target_pairs={{0,4},{1,5},{2,6},{3,7},{4,0},{5,1},{6,2},{7,3},{8,12},{9,13},{10,... | collective-permute-start | bytes 3145736 | tf_op jit(solution)/shard_map/ppermute | solution.py:59
  141.6 152.3 %reduce-scatter.7.cloned.1.call-start = ((), (), s32[]{:S(2)}) async-start(), calls=%async_computation.6 | async-start | bytes 2621440 | tf_op jit(solution)/shard_map/reduce_scatter | solution.py:293
  251.3 88.0 %reduce-scatter.9.cloned.1.call-start = ((), (), s32[]{:S(2)}) async-start(), calls=%async_computation.7 | async-start | bytes 2621440 | tf_op jit(solution)/shard_map/reduce_scatter | solution.py:293
  267.0 24.1 %collective-permute-start.22 = (bf16[128,2048]{1,0:T(8,128)(2,1)}, bf16[128,2048]{1,0:T(8,128)(2,1)}, u32[]{:S(2)}, u32[]{:S(2)}) collective-permute-start(bf16[128,2048]{1,0:T(8,128)(2,1)} %get-tuple-element.167), channel_id=1, source_target_pairs={{0,4},{1,5},{2,6},{3,7},{4,0},{5,1},{6,2},{7,3},{8,12},{9,13},{10,... | collective-permute-start | bytes 1572872 | tf_op jit(solution)/shard_map/ppermute | solution.py:59
  267.6 23.5 %collective-permute-start.21 = (bf16[128,2048]{1,0:T(8,128)(2,1)}, bf16[128,2048]{1,0:T(8,128)(2,1)}, u32[]{:S(2)}, u32[]{:S(2)}) collective-permute-start(bf16[128,2048]{1,0:T(8,128)(2,1)} %get-tuple-element.165), channel_id=1, source_target_pairs={{0,2},{1,3},{2,0},{3,1},{4,6},{5,7},{6,4},{7,5},{8,10},{9,11},{10,... | collective-permute-start | bytes 1572872 | tf_op jit(solution)/shard_map/ppermute | solution.py:59
  271.8 113.0 %reduce-scatter.11.cloned.1.call-start = ((), (), s32[]{:S(2)}) async-start(), calls=%async_computation.8 | async-start | bytes 2621440 | tf_op jit(solution)/shard_map/reduce_scatter | solution.py:293
  322.1 169.4 %reduce-scatter.13.cloned.1.call-start = ((), (), s32[]{:S(2)}) async-start(), calls=%async_computation.9 | async-start | bytes 1310720 | tf_op jit(solution)/shard_map/reduce_scatter | solution.py:293
  365.1 31.8 %collective-permute-start.31 = (bf16[4,256,512]{2,1,0:T(8,128)(2,1)}, bf16[4,256,512]{2,1,0:T(8,128)(2,1)}, u32[]{:S(2)}, u32[]{:S(2)}) collective-permute-start(bf16[4,256,512]{2,1,0:T(8,128)(2,1)} %fusion.35), channel_id=1, source_target_pairs={{0,4},{1,5},{2,6},{3,7},{4,0},{5,1},{6,2},{7,3},{8,12},{9,13},{10,... | collective-permute-start | bytes 3145736 | tf_op jit(solution)/shard_map/ppermute | solution.py:59
  399.6 93.8 %reduce-scatter.15.cloned.1.call-start = ((), (), s32[]{:S(2)}) async-start(), calls=%async_computation.10 | async-start | bytes 2621440 | tf_op jit(solution)/shard_map/reduce_scatter | solution.py:293
  401.6 117.2 %reduce-scatter.17.cloned.1.call-start = ((), (), s32[]{:S(2)}) async-start(), calls=%async_computation.11 | async-start | bytes 1310720 | tf_op jit(solution)/shard_map/reduce_scatter | solution.py:293
  413.6 30.6 %collective-permute-start.39 = (bf16[4,256,512]{2,1,0:T(8,128)(2,1)}, bf16[4,256,512]{2,1,0:T(8,128)(2,1)S(1)}, u32[]{:S(2)}, u32[]{:S(2)}) collective-permute-start(bf16[4,256,512]{2,1,0:T(8,128)(2,1)} %fusion.34), channel_id=1, source_target_pairs={{0,4},{1,5},{2,6},{3,7},{4,0},{5,1},{6,2},{7,3},{8,12},{9,13},{10,... | collective-permute-start | bytes 3145736 | tf_op jit(solution)/shard_map/ppermute | solution.py:59
  446.4 42.0 %collective-permute-start.42 = (bf16[128,2048]{1,0:T(8,128)(2,1)}, bf16[128,2048]{1,0:T(8,128)(2,1)}, u32[]{:S(2)}, u32[]{:S(2)}) collective-permute-start(bf16[128,2048]{1,0:T(8,128)(2,1)} %get-tuple-element.161), channel_id=1, source_target_pairs={{0,6},{1,7},{2,4},{3,5},{4,2},{5,3},{6,0},{7,1},{8,14},{9,15},{10,... | collective-permute-start | bytes 1572872 | tf_op jit(solution)/shard_map/ppermute | solution.py:59
  449.0 39.4 %collective-permute-start.41 = (bf16[128,2048]{1,0:T(8,128)(2,1)}, bf16[128,2048]{1,0:T(8,128)(2,1)}, u32[]{:S(2)}, u32[]{:S(2)}) collective-permute-start(bf16[128,2048]{1,0:T(8,128)(2,1)} %get-tuple-element.162), channel_id=1, source_target_pairs={{0,4},{1,5},{2,6},{3,7},{4,0},{5,1},{6,2},{7,3},{8,12},{9,13},{10,... | collective-permute-start | bytes 1572872 | tf_op jit(solution)/shard_map/ppermute | solution.py:59
  449.6 38.9 %collective-permute-start.40 = (bf16[128,2048]{1,0:T(8,128)(2,1)}, bf16[128,2048]{1,0:T(8,128)(2,1)}, u32[]{:S(2)}, u32[]{:S(2)}) collective-permute-start(bf16[128,2048]{1,0:T(8,128)(2,1)} %get-tuple-element.160), channel_id=1, source_target_pairs={{0,2},{1,3},{2,0},{3,1},{4,6},{5,7},{6,4},{7,5},{8,10},{9,11},{10,... | collective-permute-start | bytes 1572872 | tf_op jit(solution)/shard_map/ppermute | solution.py:59
  450.5 45.7 %collective-permute-start.50 = (bf16[256,1024]{1,0:T(8,128)(2,1)S(1)}, bf16[256,1024]{1,0:T(8,128)(2,1)}, u32[]{:S(2)}, u32[]{:S(2)}) collective-permute-start(bf16[256,1024]{1,0:T(8,128)(2,1)S(1)} %dynamic-slice_bitcast_fusion.2), channel_id=1, source_target_pairs={{0,4},{1,5},{2,6},{3,7},{4,0},{5,1},{6,2},{7,3},{8,12},{9,13},{10,... | collective-permute-start | bytes 1572872 | tf_op jit(solution)/shard_map/ppermute | solution.py:59
  (113 other events, 1063.7 us)
Sparse Core Ops, SparseCore 0:
  10.2 50.0 all-gather.8
  62.4 46.5 all-gather.10
  110.6 44.6 all-gather.12
  156.7 79.4 all-gather.14
  251.4 42.3 reduce-scatter.6
  296.1 43.1 reduce-scatter.8
  341.6 43.1 reduce-scatter.10
  399.8 28.1 reduce-scatter.12
  430.2 51.5 reduce-scatter.14
  484.0 26.4 reduce-scatter.16

commit v4 on v3

--- a/solution.py
+++ b/solution.py
@@ -392,6 +392,16 @@
         )
         return low(value), pull
 
+    def ff_send(sums):
+        parts = jnp.concatenate(sums, axis=-1).reshape(2, depth, unit)
+        return take(parts, x, 0), flip(take(parts, 1 - x, 0), blk_bits=1)
+
+    def ff_join(own, other):
+        first = x == 0
+        return wide(
+            jnp.concatenate([jnp.where(first, own, other), jnp.where(first, other, own)], axis=-1)
+        )
+
     def scatter_units(grads):
         return scatter_z(grads.reshape(z_count, 2 * depth, part_unit))
 
@@ -427,7 +437,6 @@
 
     cot_pair, ffn_half = tie(pair_y(low(res_total)), ffn_half)
     cot_attn = pair_core(cot_pair).reshape(slots * seq_dev, width)
-    cot_attn, sums_down[1] = tie(cot_attn, sums_down[1])
     attn_grad = plain_dot(cot_attn, full_out).astype(LOW)
     query_low, kv_grad = attention_call(
         backward_kernel,
@@ -441,7 +450,9 @@
     )
     kv_grad = kv_grad.reshape(slots, blk_count, seq_dev, 2 * HEAD_DIM)
     half_kv = wide(kv_grad[:2]) + wide(flip(kv_grad[2:], head_bits=1))
-    half_kv, query_low, cot_late, in_late = tie(half_kv, query_low, cot_attn, group_in)
+    half_kv, query_low, cot_late, in_late, sums_down[1] = tie(
+        half_kv, query_low, cot_attn, group_in, sums_down[1]
+    )
     half_in = add_core([query_low], [full_q])
 
     def sides(grads):
@@ -450,32 +461,25 @@
 
     grad_q, q_across = sides(row_dot(in_late, query_low))
     q_across = flip(q_across, blk_bits=1)
-    part, half_in, grad_q, cot_late, sums_up[0] = tie(
-        add_y(half_kv), half_in, grad_q, cot_late, sums_up[0]
-    )
+    part, half_in, grad_q, cot_late = tie(add_y(half_kv), half_in, grad_q, cot_late)
     grad_out, out_across = sides(row_dot(cot_late, attn_low))
     bit = 1
     while bit < blk_count:
         pair = part.reshape((-1, 2) + part.shape[1:])
         part = pair[:, 0] + wide(flip(low(pair[:, 1]), blk_bits=bit))
         if bit == 1:
-            part, grad_out, out_across, q_across = tie(part, grad_out, out_across, q_across)
-            sum_q = wide(scatter_z(low(grad_q + wide(q_across))))
+            part, grad_out, out_across, q_across, sums_up[0] = tie(
+                part, grad_out, out_across, q_across, sums_up[0]
+            )
             out_across = flip(out_across, blk_bits=1)
         bit *= 2
-    own_kv_grad = low(part[0])
+    own_kv_grad, grad_q, sums_down = tie(low(part[0]), grad_q, sums_down)
+    sum_q = wide(scatter_z(low(grad_q + wide(q_across))))
+    down_own, down_other = ff_send(sums_down)
     norm_one_grad = add_y(half_in) + col_dot(own_kv_grad, w_kv)
     norm_one_value, norm_one_pull = jax.vjp(layer_norm, own_rows, ln1_gain, ln1_bias)
     input_part, grad_ln1_gain, grad_ln1_bias = norm_one_pull(norm_one_grad)
     input_grad = res_total + input_part
-
-    def ff_sum(sums):
-        parts = jnp.concatenate(sums, axis=-1).reshape(2, depth, unit)
-        own, other = take(parts, x, 0), flip(take(parts, 1 - x, 0), blk_bits=1)
-        first = x == 0
-        return wide(
-            jnp.concatenate([jnp.where(first, own, other), jnp.where(first, other, own)], axis=-1)
-        )
 
     grad_b_q = lax.dynamic_update_slice_in_dim(
         jnp.zeros((width,), jnp.float32),
@@ -530,10 +534,13 @@
     )
     got = [flip(v, *bits) for v, bits in zip(sent, plane)]
     (sent,) = small_call(plane_sum, [(message, LOW)], *got, sent[0], keep)
-    sent, ffn_half, sums_down, out_across = tie(sent, ffn_half, sums_down, out_across)
+    sent, ffn_half, out_across, sums_up[1], down_own = tie(
+        sent, ffn_half, out_across, sums_up[1], down_own
+    )
+    sum_down = ff_join(down_own, down_other)
+    up_own, up_other = ff_send(sums_up)
+    ffn_got = [flip(low(ffn_half[i + 1]), *bits) for i, bits in enumerate(plane)]
     sum_out = wide(scatter_z(low(grad_out + wide(out_across))))
-    output = low(hidden_res + plane_xy(ffn_half) + b_down)[None]
-    sum_down = ff_sum(sums_down)
     bit = 2
     while 2 * bit < blk_count:
         (sent,) = small_call(
@@ -546,8 +553,7 @@
         flip(sent, blk_bits=bit),
         sent,
     )
-    rows, sum_q, sums_up[1] = tie(rows, sum_q, sums_up[1])
-    sum_up = ff_sum(sums_up)
+    rows, sum_q, up_other, ffn_got = tie(rows, sum_q, up_other, ffn_got)
     (rows,) = small_call(
         partial(join_stage, 1),
         [((rows_half, columns), LOW)],
@@ -555,6 +561,9 @@
         *[flip(rows, *bits) for bits in plane],
         where=where,
     )
+    rows, up_own, ffn_total = tie(rows, up_own, ffn_half[0])
+    sum_up = ff_join(up_own, up_other)
+    output = low(hidden_res + ffn_total + sum(wide(v) for v in ffn_got) + b_down)[None]
     (sum_kv,) = small_call(
         partial(join_stage, 5),
         [((width, columns), jnp.float32)],

time: 536 us -> 514 us (0.959)
  waiting for transfers between devices: 247 us -> 217 us
    reduce_scatter x6, waiting for transfers between devices: 17.4 us -> 0.05 us  [scatter_z(): lax.psum_scatter(values, 'blk', scatter_dimension=0, axis_index_groups=z_...]
    ppermute x51, waiting for transfers between devices: 205 us -> 196 us  [flip(): return lax.ppermute(values, ('blk', 'head'), pairs)]
    unnamed x167 -> x159, local copies, waits for them, and re-layouts: 15.7 us -> 18 us
  transfers between devices with their start and end apart: 61 -> 61, of which waited for: 35 -> 34; matrix products, arithmetic and copies ran while one was open for 31% -> 35% of each run, Pallas kernels for 4% -> 4%
where the time goes in v4:
time: 514 us; the launch traced here: 505 us
  waiting for transfers between devices  217 us (42%)
  other arithmetic  78.2 us (15%)
  matrix products  71.3 us (14%)
  starting transfers between devices  52.3 us (10%)
  local copies, waits for them, and re-layouts  47.6 us (9%)
  Pallas kernels  22.6 us (4%)
  between operations  15.9 us (3%)
    ppermute x51, waiting for transfers between devices, flip(): return lax.ppermute(values, ('blk', 'head'), pairs)  196 us
    ppermute x51, starting transfers between devices, flip(): return lax.ppermute(values, ('blk', 'head'), pairs)  50.9 us
    dot_general x11, matrix products, col_dot(): lax.dot_general(left, right, (((1,), (1,)), ((), ())), preferred_element_...  27.4 us
    dot_general x6, matrix products, plain_dot(): return jnp.dot(left, right, preferred_element_type=jnp.float32)  23.6 us
    all_gather x4, waiting for transfers between devices, gather_z(): return lax.all_gather(values, 'blk', axis=0, axis_index_groups=z_groups)  20.6 us
    dot_general x6, matrix products, row_dot(): lax.dot_general(left, right, (((0,), (0,)), ((), ())), preferred_element_...  20.3 us
    unnamed x159, local copies, waits for them, and re-layouts  18 us
    pallas_call x2, Pallas kernels, attention_call(): pl.pallas_call(partial(kernel, heads), grid_spec=pltpu.PrefetchScalarGrid...  17.9 us
  transfers between devices with their start and end apart: 61, of which 34 were waited for; matrix products, arithmetic and copies ran while one was open for 35% of the time, Pallas kernels for 4%

profile of v4, /device:TPU:0, one launch (start us, length us, event | category | flops | bytes accessed | tf_op | source)
XLA Modules:
  0.0 504.8 jit_solution(2541385666244015753)
XLA Ops:
  29.4 12.9 %collective-permute-done.5 = bf16[2,128,256]{2,1,0:T(8,128)(2,1)S(1)} collective-permute-done((bf16[2,128,256]{2,1,0:T(8,128)(2,1)S(1)}, bf16[2,128,256]{2,1,0:T(8,128)(2,1)S(1)}, u32[]{:S(2)}, u32[]{:S(2)}) %collective-permute-start.5) | collective-permute-done | bytes 131104 | tf_op jit(solution)/shard_map/ppermute | solution.py:59
  65.4 7.0 %collective-permute-done.8 = bf16[8,128,256]{2,1,0:T(8,128)(2,1)} collective-permute-done((bf16[8,128,256]{2,1,0:T(8,128)(2,1)}, bf16[8,128,256]{2,1,0:T(8,128)(2,1)}, u32[]{:S(2)}, u32[]{:S(2)}) %collective-permute-start.8) | collective-permute-done | bytes 524320 | tf_op jit(solution)/shard_map/ppermute | solution.py:59
  76.3 10.3 %collective-permute-done.2 = bf16[4,256,512]{2,1,0:T(8,128)(2,1)S(1)} collective-permute-done((bf16[4,256,512]{2,1,0:T(8,128)(2,1)S(1)}, bf16[4,256,512]{2,1,0:T(8,128)(2,1)S(1)}, u32[]{:S(2)}, u32[]{:S(2)}) %collective-permute-start.2) | collective-permute-done | bytes 1048608 | tf_op jit(solution)/shard_map/ppermute | solution.py:59
  94.7 7.3 %shard_map.297 = bf16[512,512]{1,0:T(8,128)(2,1)S(1)} custom-call(s32[5]{0:T(128)S(1)} %pad_add_fusion.scalars, bf16[512,512]{1,0:T(8,128)(2,1)S(1)} %fusion.20.q_ref, bf16[4,1024,256]{2,1,0:T(8,128)(2,1)S(1)} %pad_maximum_fusion.3.kv_ref, s32[1,1024]{1,0:T(1,128)S(1)} %bitcast.293), custom_call_target="tpu_custom_call" | custom-call | flops 1073741824 | bytes 8388608 | tf_op jit(solution)/shard_map/pallas_call | solution.py:159
  109.9 7.1 %collective-permute-done.11 = bf16[4,256,512]{2,1,0:T(8,128)(2,1)} collective-permute-done((bf16[4,256,512]{2,1,0:T(8,128)(2,1)}, bf16[4,256,512]{2,1,0:T(8,128)(2,1)}, u32[]{:S(2)}, u32[]{:S(2)}) %collective-permute-start.11) | collective-permute-done | bytes 1048608 | tf_op jit(solution)/shard_map/ppermute | solution.py:59
  120.0 17.4 %collective-permute-done.14 = bf16[2,128,2048]{2,1,0:T(8,128)(2,1)S(1)} collective-permute-done((bf16[2,128,2048]{2,1,0:T(8,128)(2,1)}, bf16[2,128,2048]{2,1,0:T(8,128)(2,1)S(1)}, u32[]{:S(2)}, u32[]{:S(2)}) %collective-permute-start.14) | collective-permute-done | bytes 1048608 | tf_op jit(solution)/shard_map/ppermute | solution.py:59
  143.6 13.1 %collective-permute-done.13 = bf16[128,2048]{1,0:T(8,128)(2,1)} collective-permute-done((bf16[128,2048]{1,0:T(8,128)(2,1)}, bf16[128,2048]{1,0:T(8,128)(2,1)}, u32[]{:S(2)}, u32[]{:S(2)}) %collective-permute-start.13) | collective-permute-done | bytes 524320 | tf_op jit(solution)/shard_map/ppermute | solution.py:59
  171.9 10.5 %collective-permute-done.16 = bf16[128,2048]{1,0:T(8,128)(2,1)S(1)} collective-permute-done((bf16[128,2048]{1,0:T(8,128)(2,1)S(1)}, bf16[128,2048]{1,0:T(8,128)(2,1)S(1)}, u32[]{:S(2)}, u32[]{:S(2)}) %collective-permute-start.16) | collective-permute-done | bytes 524320 | tf_op jit(solution)/shard_map/ppermute | solution.py:59
  184.7 9.6 %collective-permute-done.18 = bf16[128,2048]{1,0:T(8,128)(2,1)S(1)} collective-permute-done((bf16[128,2048]{1,0:T(8,128)(2,1)S(1)}, bf16[128,2048]{1,0:T(8,128)(2,1)S(1)}, u32[]{:S(2)}, u32[]{:S(2)}) %collective-permute-start.18) | collective-permute-done | bytes 524320 | tf_op jit(solution)/shard_map/ppermute | solution.py:59
  203.8 6.4 %multiply_convert_fusion.1 = (bf16[1024,512]{1,0:T(8,128)(2,1)S(1)}, f32[1024,512]{1,0:T(8,128)}) fusion(f32[512]{0:T(512)S(1)} %get-tuple-element.215, bf16[1024,2048]{1,0:T(8,128)(2,1)} %bitcast.350, bf16[2048,512]{1,0:T(8,128)(2,1)S(1)} %copy-done.31), kind=kOutput, calls=%fused_computation.48 | convolution fusion | flops 2152726528 | bytes 9439232 | tf_op jit(solution)/shard_map/dot_general | solution.py:24
  221.8 14.4 %all-gather.15.cloned.1.call-done = bf16[2048,1024]{1,0:T(8,128)(2,1)} async-done(((bf16[512,1024]{1,0:T(8,128)(2,1)}), bf16[2048,1024]{1,0:T(8,128)(2,1)}) %all-gather.15.cloned.1.call-update) | async-done | bytes 4194320 | tf_op jit(solution)/shard_map/all_gather | solution.py:290
  236.2 10.3 %fusion.84 = f32[1024,1024]{1,0:T(8,128)} fusion(bf16[1024,2048]{1,0:T(8,128)(2,1)} %bitcast.320, bf16[2048,1024]{1,0:T(8,128)(2,1)} %all-gather.15.cloned.1.call-done), kind=kOutput, calls=%fused_computation.219 | convolution fusion | flops 4294967296 | bytes 12582912 | tf_op jit(solution)/shard_map/dot_general | solution.py:24
  246.6 5.3 %fusion.13 = (bf16[1024,512]{1,0:T(8,128)(2,1)S(1)}, bf16[1024,512]{1,0:T(8,128)(2,1)S(1)}) fusion(f32[1024,1024]{1,0:T(8,128)} %fusion.84, f32[1024,512]{1,0:T(8,128)} %get-tuple-element.219, f32[512]{0:T(512)S(1)} %get-tuple-element.214, f32[1024,512]{1,0:T(8,128)} %get-tuple-element.217, f32[512]{0:T(512)S(1)} %get-tuple-element.215), kind=kLoop, calls=%fused_computation.29 | loop fusion | flops 22020096 | bytes 10489856 | tf_op jit(solution)/shard_map/convert_element_type | solution.py:44
  268.1 6.4 %convolution_convert_fusion.2 = bf16[2048,512]{1,0:T(8,128)(2,1)} fusion(bf16[1024,2048]{1,0:T(8,128)(2,1)} %bitcast.351, bf16[1024,512]{1,0:T(8,128)(2,1)} %copy-done.12), kind=kOutput, calls=%fused_computation.11 | convolution fusion | flops 2148532224 | bytes 7340032 | tf_op jit(solution)/shard_map/dot_general | solution.py:28
  280.2 10.6 %collective-permute-done.22 = bf16[128,2048]{1,0:T(8,128)(2,1)} collective-permute-done((bf16[128,2048]{1,0:T(8,128)(2,1)}, bf16[128,2048]{1,0:T(8,128)(2,1)}, u32[]{:S(2)}, u32[]{:S(2)}) %collective-permute-start.22) | collective-permute-done | bytes 524320 | tf_op jit(solution)/shard_map/ppermute | solution.py:59
  295.3 6.8 %convolution_convert_fusion = bf16[512,2048]{1,0:T(8,128)(2,1)} fusion(bf16[2048,1024]{1,0:T(8,128)(2,1)} %all-gather.15.cloned.1.call-done, bf16[1024,1024]{1,0:T(8,128)(2,1)S(1)} %constant_dynamic-update-slice_fusion.5), kind=kOutput, calls=%fused_computation.9 | convolution fusion | flops 2148532224 | bytes 7340032 | tf_op jit(solution)/shard_map/dot_general | solution.py:34
  306.2 12.5 %collective-permute-done.24 = bf16[128,2048]{1,0:T(8,128)(2,1)} collective-permute-done((bf16[128,2048]{1,0:T(8,128)(2,1)S(1)}, bf16[128,2048]{1,0:T(8,128)(2,1)}, u32[]{:S(2)}, u32[]{:S(2)}) %collective-permute-start.24) | collective-permute-done | bytes 524320 | tf_op jit(solution)/shard_map/ppermute | solution.py:59
  319.9 7.3 %convert_add_fusion = f32[512,2048]{1,0:T(8,128)} fusion(bf16[512,2048]{1,0:T(8,128)(2,1)} %collective-permute-done.25, bf16[2048,1024]{1,0:T(8,128)(2,1)} %all-gather.15.cloned.1.call-done, bf16[1024,1024]{1,0:T(8,128)(2,1)S(1)} %copy-done.50), kind=kOutput, calls=%fused_computation.2 | convolution fusion | flops 2149580800 | bytes 11534336 | tf_op jit(solution)/shard_map/dot_general | solution.py:34
  331.4 10.6 %shard_map.298 = (bf16[512,512]{1,0:T(8,128)(2,1)S(1)}, bf16[4,1024,256]{2,1,0:T(8,128)(2,1)S(1)}) custom-call(s32[5]{0:T(128)S(1)} %pad_add_fusion.scalars, bf16[512,512]{1,0:T(8,128)(2,1)S(1)} %fusion.20.q_ref, bf16[512,512]{1,0:T(8,128)(2,1)S(1)} %convolution_convert_fusion.7.go_ref, bf16[4,1024,256]{2,1,0:T(8,128)(2,1)} %copy-done.1, s32[1,1024]{1,0:T(1,128)S(1)} %bitcast.294), custom_call_target="tpu_custom_call" | custom-call | flops 2684354560 | bytes 8388608 | tf_op jit(solution)/shard_map/pallas_call | solution.py:159
  360.2 6.9 %collective-permute-done.28 = bf16[8,128,256]{2,1,0:T(8,128)(2,1)S(1)} collective-permute-done((bf16[8,128,256]{2,1,0:T(8,128)(2,1)S(1)}, bf16[8,128,256]{2,1,0:T(8,128)(2,1)S(1)}, u32[]{:S(2)}, u32[]{:S(2)}) %collective-permute-start.28) | collective-permute-done | bytes 524320 | tf_op jit(solution)/shard_map/ppermute | solution.py:59
  375.0 12.9 %collective-permute-done.30 = bf16[4,128,256]{2,1,0:T(8,128)(2,1)S(1)} collective-permute-done((bf16[4,128,256]{2,1,0:T(8,128)(2,1)S(1)}, bf16[4,128,256]{2,1,0:T(8,128)(2,1)S(1)}, u32[]{:S(2)}, u32[]{:S(2)}) %collective-permute-start.30) | collective-permute-done | bytes 262176 | tf_op jit(solution)/shard_map/ppermute | solution.py:59
  388.2 11.0 %collective-permute-done.32 = bf16[2,128,256]{2,1,0:T(8,128)(2,1)S(1)} collective-permute-done((bf16[2,128,256]{2,1,0:T(8,128)(2,1)S(1)}, bf16[2,128,256]{2,1,0:T(8,128)(2,1)S(1)}, u32[]{:S(2)}, u32[]{:S(2)}) %collective-permute-start.32) | collective-permute-done | bytes 131104 | tf_op jit(solution)/shard_map/ppermute | solution.py:59
  429.3 6.1 %collective-permute-done.38.xy_ref = bf16[448,256]{1,0:T(8,128)(2,1)S(1)} collective-permute-done((bf16[448,256]{1,0:T(8,128)(2,1)S(1)}, bf16[448,256]{1,0:T(8,128)(2,1)S(1)}, u32[]{:S(2)}, u32[]{:S(2)}) %collective-permute-start.38) | collective-permute-done | bytes 229408 | tf_op jit(solution)/shard_map/ppermute | solution.py:59
  453.8 14.6 %collective-permute-done.41.got_ref = bf16[448,256]{1,0:T(8,128)(2,1)S(1)} collective-permute-done((bf16[448,256]{1,0:T(8,128)(2,1)S(1)}, bf16[448,256]{1,0:T(8,128)(2,1)S(1)}, u32[]{:S(2)}, u32[]{:S(2)}) %collective-permute-start.41) | collective-permute-done | bytes 229408 | tf_op jit(solution)/shard_map/ppermute | solution.py:59
  (413 shorter events, 251.5 us)
Async XLA Ops:
  7.3 53.0 %all-gather.9.cloned.1.call-start = ((), (), s32[]{:S(2)}) async-start(), calls=%async_computation.12 | async-start | bytes 2621440 | tf_op jit(solution)/shard_map/all_gather | solution.py:290
  9.3 99.2 %all-gather.11.cloned.1.call-start = ((), (), s32[]{:S(2)}) async-start(), calls=%async_computation.13 | async-start | bytes 2621440 | tf_op jit(solution)/shard_map/all_gather | solution.py:290
  11.3 41.3 %collective-permute-start = (bf16[128,2048]{1,0:T(8,128)(2,1)S(1)}, bf16[128,2048]{1,0:T(8,128)(2,1)}, u32[]{:S(2)}, u32[]{:S(2)}) collective-permute-start(bf16[128,2048]{1,0:T(8,128)(2,1)S(1)} %fusion.25.in_ref), channel_id=1, source_target_pairs={{0,2},{1,3},{2,0},{3,1},{4,6},{5,7},{6,4},{7,5},{8,10},{9,11},{10,... | collective-permute-start | bytes 1572872 | tf_op jit(solution)/shard_map/ppermute | solution.py:59
  16.5 46.7 %collective-permute-start.3 = (bf16[128,2048]{1,0:T(8,128)(2,1)}, bf16[128,2048]{1,0:T(8,128)(2,1)}, u32[]{:S(2)}, u32[]{:S(2)}) collective-permute-start(bf16[128,2048]{1,0:T(8,128)(2,1)} %bitcast_select_fusion), channel_id=1, source_target_pairs={{0,2},{1,3},{2,0},{3,1},{4,6},{5,7},{6,4},{7,5},{8,10},{9,11},{10,... | collective-permute-start | bytes 1572872 | tf_op jit(solution)/shard_map/ppermute | solution.py:59
  25.3 23.0 %collective-permute-start.7 = (bf16[256,1024]{1,0:T(8,128)(2,1)}, bf16[256,1024]{1,0:T(8,128)(2,1)}, u32[]{:S(2)}, u32[]{:S(2)}) collective-permute-start(bf16[256,1024]{1,0:T(8,128)(2,1)} %constant_dynamic-slice_fusion.1), channel_id=1, source_target_pairs={{0,4},{1,5},{2,6},{3,7},{4,0},{5,1},{6,2},{7,3},{8,12},{9,13},{10,... | collective-permute-start | bytes 1572872 | tf_op jit(solution)/shard_map/ppermute | solution.py:59
  52.6 110.5 %all-gather.13.cloned.1.call-start = ((), (), s32[]{:S(2)}) async-start(), calls=%async_computation.14 | async-start | bytes 2621440 | tf_op jit(solution)/shard_map/all_gather | solution.py:290
  61.6 25.0 %collective-permute-start.2 = (bf16[4,256,512]{2,1,0:T(8,128)(2,1)S(1)}, bf16[4,256,512]{2,1,0:T(8,128)(2,1)S(1)}, u32[]{:S(2)}, u32[]{:S(2)}) collective-permute-start(bf16[4,256,512]{2,1,0:T(8,128)(2,1)S(1)} %slice.204), channel_id=1, source_target_pairs={{0,4},{1,5},{2,6},{3,7},{4,0},{5,1},{6,2},{7,3},{8,12},{9,13},{10,... | collective-permute-start | bytes 3145736 | tf_op jit(solution)/shard_map/ppermute | solution.py:59
  90.5 26.5 %collective-permute-start.11 = (bf16[4,256,512]{2,1,0:T(8,128)(2,1)}, bf16[4,256,512]{2,1,0:T(8,128)(2,1)}, u32[]{:S(2)}, u32[]{:S(2)}) collective-permute-start(bf16[4,256,512]{2,1,0:T(8,128)(2,1)} %get-tuple-element.92), channel_id=1, source_target_pairs={{0,4},{1,5},{2,6},{3,7},{4,0},{5,1},{6,2},{7,3},{8,12},{9,13},{10,... | collective-permute-start | bytes 3145736 | tf_op jit(solution)/shard_map/ppermute | solution.py:59
  92.9 143.4 %all-gather.15.cloned.1.call-start = ((), (), s32[]{:S(2)}) async-start(), calls=%async_computation.15 | async-start | bytes 5242880 | tf_op jit(solution)/shard_map/all_gather | solution.py:290
  108.5 28.9 %collective-permute-start.14 = (bf16[2,128,2048]{2,1,0:T(8,128)(2,1)}, bf16[2,128,2048]{2,1,0:T(8,128)(2,1)S(1)}, u32[]{:S(2)}, u32[]{:S(2)}) collective-permute-start(bf16[2,128,2048]{2,1,0:T(8,128)(2,1)} %pad_maximum_fusion.9), channel_id=1, source_target_pairs={{0,4},{1,5},{2,6},{3,7},{4,0},{5,1},{6,2},{7,3},{8,12},{9,13},{10,... | collective-permute-start | bytes 3145736 | tf_op jit(solution)/shard_map/ppermute | solution.py:59
  143.6 150.1 %reduce-scatter.7.cloned.1.call-start = ((), (), s32[]{:S(2)}) async-start(), calls=%async_computation.6 | async-start | bytes 2621440 | tf_op jit(solution)/shard_map/reduce_scatter | solution.py:293
  246.6 103.5 %reduce-scatter.9.cloned.1.call-start = ((), (), s32[]{:S(2)}) async-start(), calls=%async_computation.7 | async-start | bytes 2621440 | tf_op jit(solution)/shard_map/reduce_scatter | solution.py:293
  266.7 24.1 %collective-permute-start.22 = (bf16[128,2048]{1,0:T(8,128)(2,1)}, bf16[128,2048]{1,0:T(8,128)(2,1)}, u32[]{:S(2)}, u32[]{:S(2)}) collective-permute-start(bf16[128,2048]{1,0:T(8,128)(2,1)} %get-tuple-element.185), channel_id=1, source_target_pairs={{0,4},{1,5},{2,6},{3,7},{4,0},{5,1},{6,2},{7,3},{8,12},{9,13},{10,... | collective-permute-start | bytes 1572872 | tf_op jit(solution)/shard_map/ppermute | solution.py:59
  267.3 23.5 %collective-permute-start.21 = (bf16[128,2048]{1,0:T(8,128)(2,1)}, bf16[128,2048]{1,0:T(8,128)(2,1)}, u32[]{:S(2)}, u32[]{:S(2)}) collective-permute-start(bf16[128,2048]{1,0:T(8,128)(2,1)} %get-tuple-element.183), channel_id=1, source_target_pairs={{0,2},{1,3},{2,0},{3,1},{4,6},{5,7},{6,4},{7,5},{8,10},{9,11},{10,... | collective-permute-start | bytes 1572872 | tf_op jit(solution)/shard_map/ppermute | solution.py:59
  267.8 120.1 %reduce-scatter.11.cloned.1.call-start = ((), (), s32[]{:S(2)}) async-start(), calls=%async_computation.8 | async-start | bytes 2621440 | tf_op jit(solution)/shard_map/reduce_scatter | solution.py:293
  305.9 129.7 %reduce-scatter.13.cloned.1.call-start = ((), (), s32[]{:S(2)}) async-start(), calls=%async_computation.9 | async-start | bytes 2621440 | tf_op jit(solution)/shard_map/reduce_scatter | solution.py:293
  346.6 126.0 %reduce-scatter.15.cloned.1.call-start = ((), (), s32[]{:S(2)}) async-start(), calls=%async_computation.10 | async-start | bytes 1310720 | tf_op jit(solution)/shard_map/reduce_scatter | solution.py:293
  357.2 30.8 %collective-permute-start.31 = (bf16[4,256,512]{2,1,0:T(8,128)(2,1)}, bf16[4,256,512]{2,1,0:T(8,128)(2,1)}, u32[]{:S(2)}, u32[]{:S(2)}) collective-permute-start(bf16[4,256,512]{2,1,0:T(8,128)(2,1)} %fusion.35), channel_id=1, source_target_pairs={{0,4},{1,5},{2,6},{3,7},{4,0},{5,1},{6,2},{7,3},{8,12},{9,13},{10,... | collective-permute-start | bytes 3145736 | tf_op jit(solution)/shard_map/ppermute | solution.py:59
  401.7 33.9 %collective-permute-start.39 = (bf16[4,256,512]{2,1,0:T(8,128)(2,1)}, bf16[4,256,512]{2,1,0:T(8,128)(2,1)}, u32[]{:S(2)}, u32[]{:S(2)}) collective-permute-start(bf16[4,256,512]{2,1,0:T(8,128)(2,1)} %fusion.34), channel_id=1, source_target_pairs={{0,4},{1,5},{2,6},{3,7},{4,0},{5,1},{6,2},{7,3},{8,12},{9,13},{10,... | collective-permute-start | bytes 3145736 | tf_op jit(solution)/shard_map/ppermute | solution.py:59
  411.1 84.6 %reduce-scatter.17.cloned.1.call-start = ((), (), s32[]{:S(2)}) async-start(), calls=%async_computation.11 | async-start | bytes 1310720 | tf_op jit(solution)/shard_map/reduce_scatter | solution.py:293
  438.0 36.4 %collective-permute-start.42 = (bf16[256,1024]{1,0:T(8,128)(2,1)}, bf16[256,1024]{1,0:T(8,128)(2,1)}, u32[]{:S(2)}, u32[]{:S(2)}) collective-permute-start(bf16[256,1024]{1,0:T(8,128)(2,1)} %get-tuple-element.201), channel_id=1, source_target_pairs={{0,4},{1,5},{2,6},{3,7},{4,0},{5,1},{6,2},{7,3},{8,12},{9,13},{10,... | collective-permute-start | bytes 1572872 | tf_op jit(solution)/shard_map/ppermute | solution.py:59
  440.7 33.7 %collective-permute-start.43 = (bf16[128,2048]{1,0:T(8,128)(2,1)}, bf16[128,2048]{1,0:T(8,128)(2,1)}, u32[]{:S(2)}, u32[]{:S(2)}) collective-permute-start(bf16[128,2048]{1,0:T(8,128)(2,1)} %get-tuple-element.180), channel_id=1, source_target_pairs={{0,2},{1,3},{2,0},{3,1},{4,6},{5,7},{6,4},{7,5},{8,10},{9,11},{10,... | collective-permute-start | bytes 1572872 | tf_op jit(solution)/shard_map/ppermute | solution.py:59
  441.0 33.4 %collective-permute-start.44 = (bf16[128,2048]{1,0:T(8,128)(2,1)}, bf16[128,2048]{1,0:T(8,128)(2,1)}, u32[]{:S(2)}, u32[]{:S(2)}) collective-permute-start(bf16[128,2048]{1,0:T(8,128)(2,1)} %get-tuple-element.179), channel_id=1, source_target_pairs={{0,4},{1,5},{2,6},{3,7},{4,0},{5,1},{6,2},{7,3},{8,12},{9,13},{10,... | collective-permute-start | bytes 1572872 | tf_op jit(solution)/shard_map/ppermute | solution.py:59
  445.6 33.7 %collective-permute-start.45 = (bf16[128,2048]{1,0:T(8,128)(2,1)}, bf16[128,2048]{1,0:T(8,128)(2,1)}, u32[]{:S(2)}, u32[]{:S(2)}) collective-permute-start(bf16[128,2048]{1,0:T(8,128)(2,1)} %get-tuple-element.178), channel_id=1, source_target_pairs={{0,6},{1,7},{2,4},{3,5},{4,2},{5,3},{6,0},{7,1},{8,14},{9,15},{10,... | collective-permute-start | bytes 1572872 | tf_op jit(solution)/shard_map/ppermute | solution.py:59
  (109 other events, 925.1 us)
Sparse Core Ops, SparseCore 0:
  10.2 50.0 all-gather.8
  61.8 46.5 all-gather.10
  110.0 44.6 all-gather.12
  156.7 79.4 all-gather.14
  246.7 42.3 reduce-scatter.6
  291.4 43.1 reduce-scatter.8
  336.9 43.1 reduce-scatter.10
  382.5 46.0 reduce-scatter.12
  431.5 33.5 reduce-scatter.14
  467.4 27.6 reduce-scatter.16

commit v5 on v4

--- a/solution.py
+++ b/solution.py
@@ -473,7 +473,10 @@
             )
             out_across = flip(out_across, blk_bits=1)
         bit *= 2
-    own_kv_grad, grad_q, sums_down = tie(low(part[0]), grad_q, sums_down)
+    query_sum = jnp.sum(query_low, axis=0, dtype=jnp.float32)
+    own_kv_grad, grad_q, sums_down, query_sum = tie(
+        low(part[0]), grad_q, sums_down, query_sum
+    )
     sum_q = wide(scatter_z(low(grad_q + wide(q_across))))
     down_own, down_other = ff_send(sums_down)
     norm_one_grad = add_y(half_in) + col_dot(own_kv_grad, w_kv)
@@ -483,7 +486,7 @@
 
     grad_b_q = lax.dynamic_update_slice_in_dim(
         jnp.zeros((width,), jnp.float32),
-        jnp.sum(query_low, axis=0, dtype=jnp.float32),
+        query_sum,
         column_start,
         0,
     )

time: 514 us -> 513 us (level)
  no operation moved by 1% of the time
where the time goes in v5:
time: 513 us; the launch traced here: 504 us
  waiting for transfers between devices  216 us (42%)
  other arithmetic  78.1 us (15%)
  matrix products  71.3 us (14%)
  starting transfers between devices  52.7 us (10%)
  local copies, waits for them, and re-layouts  47.7 us (9%)
  Pallas kernels  22.6 us (4%)
  between operations  15.9 us (3%)
    ppermute x51, waiting for transfers between devices, flip(): return lax.ppermute(values, ('blk', 'head'), pairs)  195 us
    ppermute x51, starting transfers between devices, flip(): return lax.ppermute(values, ('blk', 'head'), pairs)  51.4 us
    dot_general x11, matrix products, col_dot(): lax.dot_general(left, right, (((1,), (1,)), ((), ())), preferred_element_...  27.4 us
    dot_general x6, matrix products, plain_dot(): return jnp.dot(left, right, preferred_element_type=jnp.float32)  23.6 us
    all_gather x4, waiting for transfers between devices, gather_z(): return lax.all_gather(values, 'blk', axis=0, axis_index_groups=z_groups)  20.6 us
    dot_general x6, matrix products, row_dot(): lax.dot_general(left, right, (((0,), (0,)), ((), ())), preferred_element_...  20.4 us
    unnamed x159, local copies, waits for them, and re-layouts  18.1 us
    pallas_call x2, Pallas kernels, attention_call(): pl.pallas_call(partial(kernel, heads), grid_spec=pltpu.PrefetchScalarGrid...  17.9 us
  transfers between devices with their start and end apart: 61, of which 34 were waited for; matrix products, arithmetic and copies ran while one was open for 35% of the time, Pallas kernels for 4%

profile of v5, /device:TPU:0, one launch (start us, length us, event | category | flops | bytes accessed | tf_op | source)
XLA Modules:
  0.0 504.4 jit_solution(2780814247306317687)
XLA Ops:
  29.4 12.9 %collective-permute-done.5 = bf16[2,128,256]{2,1,0:T(8,128)(2,1)S(1)} collective-permute-done((bf16[2,128,256]{2,1,0:T(8,128)(2,1)S(1)}, bf16[2,128,256]{2,1,0:T(8,128)(2,1)S(1)}, u32[]{:S(2)}, u32[]{:S(2)}) %collective-permute-start.5) | collective-permute-done | bytes 131104 | tf_op jit(solution)/shard_map/ppermute | solution.py:59
  65.4 7.0 %collective-permute-done.8 = bf16[8,128,256]{2,1,0:T(8,128)(2,1)} collective-permute-done((bf16[8,128,256]{2,1,0:T(8,128)(2,1)}, bf16[8,128,256]{2,1,0:T(8,128)(2,1)}, u32[]{:S(2)}, u32[]{:S(2)}) %collective-permute-start.8) | collective-permute-done | bytes 524320 | tf_op jit(solution)/shard_map/ppermute | solution.py:59
  76.3 10.3 %collective-permute-done.2 = bf16[4,256,512]{2,1,0:T(8,128)(2,1)S(1)} collective-permute-done((bf16[4,256,512]{2,1,0:T(8,128)(2,1)S(1)}, bf16[4,256,512]{2,1,0:T(8,128)(2,1)S(1)}, u32[]{:S(2)}, u32[]{:S(2)}) %collective-permute-start.2) | collective-permute-done | bytes 1048608 | tf_op jit(solution)/shard_map/ppermute | solution.py:59
  94.7 7.3 %shard_map.297 = bf16[512,512]{1,0:T(8,128)(2,1)S(1)} custom-call(s32[5]{0:T(128)S(1)} %pad_add_fusion.scalars, bf16[512,512]{1,0:T(8,128)(2,1)S(1)} %fusion.20.q_ref, bf16[4,1024,256]{2,1,0:T(8,128)(2,1)S(1)} %pad_maximum_fusion.3.kv_ref, s32[1,1024]{1,0:T(1,128)S(1)} %bitcast.293), custom_call_target="tpu_custom_call" | custom-call | flops 1073741824 | bytes 8388608 | tf_op jit(solution)/shard_map/pallas_call | solution.py:159
  109.9 7.1 %collective-permute-done.11 = bf16[4,256,512]{2,1,0:T(8,128)(2,1)} collective-permute-done((bf16[4,256,512]{2,1,0:T(8,128)(2,1)}, bf16[4,256,512]{2,1,0:T(8,128)(2,1)}, u32[]{:S(2)}, u32[]{:S(2)}) %collective-permute-start.11) | collective-permute-done | bytes 1048608 | tf_op jit(solution)/shard_map/ppermute | solution.py:59
  120.0 17.4 %collective-permute-done.14 = bf16[2,128,2048]{2,1,0:T(8,128)(2,1)S(1)} collective-permute-done((bf16[2,128,2048]{2,1,0:T(8,128)(2,1)}, bf16[2,128,2048]{2,1,0:T(8,128)(2,1)S(1)}, u32[]{:S(2)}, u32[]{:S(2)}) %collective-permute-start.14) | collective-permute-done | bytes 1048608 | tf_op jit(solution)/shard_map/ppermute | solution.py:59
  143.6 13.1 %collective-permute-done.13 = bf16[128,2048]{1,0:T(8,128)(2,1)} collective-permute-done((bf16[128,2048]{1,0:T(8,128)(2,1)}, bf16[128,2048]{1,0:T(8,128)(2,1)}, u32[]{:S(2)}, u32[]{:S(2)}) %collective-permute-start.13) | collective-permute-done | bytes 524320 | tf_op jit(solution)/shard_map/ppermute | solution.py:59
  171.9 10.5 %collective-permute-done.16 = bf16[128,2048]{1,0:T(8,128)(2,1)S(1)} collective-permute-done((bf16[128,2048]{1,0:T(8,128)(2,1)S(1)}, bf16[128,2048]{1,0:T(8,128)(2,1)S(1)}, u32[]{:S(2)}, u32[]{:S(2)}) %collective-permute-start.16) | collective-permute-done | bytes 524320 | tf_op jit(solution)/shard_map/ppermute | solution.py:59
  184.7 9.6 %collective-permute-done.18 = bf16[128,2048]{1,0:T(8,128)(2,1)S(1)} collective-permute-done((bf16[128,2048]{1,0:T(8,128)(2,1)S(1)}, bf16[128,2048]{1,0:T(8,128)(2,1)S(1)}, u32[]{:S(2)}, u32[]{:S(2)}) %collective-permute-start.18) | collective-permute-done | bytes 524320 | tf_op jit(solution)/shard_map/ppermute | solution.py:59
  203.8 6.4 %multiply_convert_fusion.1 = (bf16[1024,512]{1,0:T(8,128)(2,1)S(1)}, f32[1024,512]{1,0:T(8,128)}) fusion(f32[512]{0:T(512)S(1)} %get-tuple-element.217, bf16[1024,2048]{1,0:T(8,128)(2,1)} %bitcast.350, bf16[2048,512]{1,0:T(8,128)(2,1)S(1)} %copy-done.31), kind=kOutput, calls=%fused_computation.48 | convolution fusion | flops 2152726528 | bytes 9439232 | tf_op jit(solution)/shard_map/dot_general | solution.py:24
  221.8 14.4 %all-gather.15.cloned.1.call-done = bf16[2048,1024]{1,0:T(8,128)(2,1)} async-done(((bf16[512,1024]{1,0:T(8,128)(2,1)}), bf16[2048,1024]{1,0:T(8,128)(2,1)}) %all-gather.15.cloned.1.call-update) | async-done | bytes 4194320 | tf_op jit(solution)/shard_map/all_gather | solution.py:290
  236.2 10.3 %fusion.84 = f32[1024,1024]{1,0:T(8,128)} fusion(bf16[1024,2048]{1,0:T(8,128)(2,1)} %bitcast.320, bf16[2048,1024]{1,0:T(8,128)(2,1)} %all-gather.15.cloned.1.call-done), kind=kOutput, calls=%fused_computation.219 | convolution fusion | flops 4294967296 | bytes 12582912 | tf_op jit(solution)/shard_map/dot_general | solution.py:24
  246.6 5.3 %fusion.13 = (bf16[1024,512]{1,0:T(8,128)(2,1)S(1)}, bf16[1024,512]{1,0:T(8,128)(2,1)S(1)}) fusion(f32[1024,1024]{1,0:T(8,128)} %fusion.84, f32[1024,512]{1,0:T(8,128)} %get-tuple-element.221, f32[512]{0:T(512)S(1)} %get-tuple-element.216, f32[1024,512]{1,0:T(8,128)} %get-tuple-element.219, f32[512]{0:T(512)S(1)} %get-tuple-element.217), kind=kLoop, calls=%fused_computation.29 | loop fusion | flops 22020096 | bytes 10489856 | tf_op jit(solution)/shard_map/convert_element_type | solution.py:44
  268.1 6.4 %convolution_convert_fusion.2 = bf16[2048,512]{1,0:T(8,128)(2,1)} fusion(bf16[1024,2048]{1,0:T(8,128)(2,1)} %bitcast.351, bf16[1024,512]{1,0:T(8,128)(2,1)} %copy-done.12), kind=kOutput, calls=%fused_computation.11 | convolution fusion | flops 2148532224 | bytes 7340032 | tf_op jit(solution)/shard_map/dot_general | solution.py:28
  280.2 10.6 %collective-permute-done.22 = bf16[128,2048]{1,0:T(8,128)(2,1)} collective-permute-done((bf16[128,2048]{1,0:T(8,128)(2,1)}, bf16[128,2048]{1,0:T(8,128)(2,1)}, u32[]{:S(2)}, u32[]{:S(2)}) %collective-permute-start.22) | collective-permute-done | bytes 524320 | tf_op jit(solution)/shard_map/ppermute | solution.py:59
  295.3 6.8 %convolution_convert_fusion = bf16[512,2048]{1,0:T(8,128)(2,1)} fusion(bf16[2048,1024]{1,0:T(8,128)(2,1)} %all-gather.15.cloned.1.call-done, bf16[1024,1024]{1,0:T(8,128)(2,1)S(1)} %constant_dynamic-update-slice_fusion.5), kind=kOutput, calls=%fused_computation.9 | convolution fusion | flops 2148532224 | bytes 7340032 | tf_op jit(solution)/shard_map/dot_general | solution.py:34
  306.2 12.5 %collective-permute-done.24 = bf16[128,2048]{1,0:T(8,128)(2,1)} collective-permute-done((bf16[128,2048]{1,0:T(8,128)(2,1)S(1)}, bf16[128,2048]{1,0:T(8,128)(2,1)}, u32[]{:S(2)}, u32[]{:S(2)}) %collective-permute-start.24) | collective-permute-done | bytes 524320 | tf_op jit(solution)/shard_map/ppermute | solution.py:59
  319.9 7.3 %convert_add_fusion = f32[512,2048]{1,0:T(8,128)} fusion(bf16[512,2048]{1,0:T(8,128)(2,1)} %collective-permute-done.25, bf16[2048,1024]{1,0:T(8,128)(2,1)} %all-gather.15.cloned.1.call-done, bf16[1024,1024]{1,0:T(8,128)(2,1)S(1)} %copy-done.50), kind=kOutput, calls=%fused_computation.2 | convolution fusion | flops 2149580800 | bytes 11534336 | tf_op jit(solution)/shard_map/dot_general | solution.py:34
  331.3 10.6 %shard_map.298 = (bf16[512,512]{1,0:T(8,128)(2,1)S(1)}, bf16[4,1024,256]{2,1,0:T(8,128)(2,1)S(1)}) custom-call(s32[5]{0:T(128)S(1)} %pad_add_fusion.scalars, bf16[512,512]{1,0:T(8,128)(2,1)S(1)} %fusion.20.q_ref, bf16[512,512]{1,0:T(8,128)(2,1)S(1)} %convolution_convert_fusion.7.go_ref, bf16[4,1024,256]{2,1,0:T(8,128)(2,1)} %copy-done.1, s32[1,1024]{1,0:T(1,128)S(1)} %bitcast.294), custom_call_target="tpu_custom_call" | custom-call | flops 2684354560 | bytes 8388608 | tf_op jit(solution)/shard_map/pallas_call | solution.py:159
  360.1 6.9 %collective-permute-done.28 = bf16[8,128,256]{2,1,0:T(8,128)(2,1)S(1)} collective-permute-done((bf16[8,128,256]{2,1,0:T(8,128)(2,1)S(1)}, bf16[8,128,256]{2,1,0:T(8,128)(2,1)S(1)}, u32[]{:S(2)}, u32[]{:S(2)}) %collective-permute-start.28) | collective-permute-done | bytes 524320 | tf_op jit(solution)/shard_map/ppermute | solution.py:59
  374.9 12.9 %collective-permute-done.30 = bf16[4,128,256]{2,1,0:T(8,128)(2,1)S(1)} collective-permute-done((bf16[4,128,256]{2,1,0:T(8,128)(2,1)S(1)}, bf16[4,128,256]{2,1,0:T(8,128)(2,1)S(1)}, u32[]{:S(2)}, u32[]{:S(2)}) %collective-permute-start.30) | collective-permute-done | bytes 262176 | tf_op jit(solution)/shard_map/ppermute | solution.py:59
  388.2 10.9 %collective-permute-done.32 = bf16[2,128,256]{2,1,0:T(8,128)(2,1)S(1)} collective-permute-done((bf16[2,128,256]{2,1,0:T(8,128)(2,1)S(1)}, bf16[2,128,256]{2,1,0:T(8,128)(2,1)S(1)}, u32[]{:S(2)}, u32[]{:S(2)}) %collective-permute-start.32) | collective-permute-done | bytes 131104 | tf_op jit(solution)/shard_map/ppermute | solution.py:59
  429.0 6.0 %collective-permute-done.38.xy_ref = bf16[448,256]{1,0:T(8,128)(2,1)S(1)} collective-permute-done((bf16[448,256]{1,0:T(8,128)(2,1)S(1)}, bf16[448,256]{1,0:T(8,128)(2,1)S(1)}, u32[]{:S(2)}, u32[]{:S(2)}) %collective-permute-start.38) | collective-permute-done | bytes 229408 | tf_op jit(solution)/shard_map/ppermute | solution.py:59
  453.4 14.8 %collective-permute-done.41.got_ref = bf16[448,256]{1,0:T(8,128)(2,1)S(1)} collective-permute-done((bf16[448,256]{1,0:T(8,128)(2,1)S(1)}, bf16[448,256]{1,0:T(8,128)(2,1)S(1)}, u32[]{:S(2)}, u32[]{:S(2)}) %collective-permute-start.41) | collective-permute-done | bytes 229408 | tf_op jit(solution)/shard_map/ppermute | solution.py:59
  (413 shorter events, 251.2 us)
Async XLA Ops:
  7.3 53.0 %all-gather.9.cloned.1.call-start = ((), (), s32[]{:S(2)}) async-start(), calls=%async_computation.12 | async-start | bytes 2621440 | tf_op jit(solution)/shard_map/all_gather | solution.py:290
  9.3 99.2 %all-gather.11.cloned.1.call-start = ((), (), s32[]{:S(2)}) async-start(), calls=%async_computation.13 | async-start | bytes 2621440 | tf_op jit(solution)/shard_map/all_gather | solution.py:290
  11.3 41.3 %collective-permute-start = (bf16[128,2048]{1,0:T(8,128)(2,1)S(1)}, bf16[128,2048]{1,0:T(8,128)(2,1)}, u32[]{:S(2)}, u32[]{:S(2)}) collective-permute-start(bf16[128,2048]{1,0:T(8,128)(2,1)S(1)} %fusion.25.in_ref), channel_id=1, source_target_pairs={{0,2},{1,3},{2,0},{3,1},{4,6},{5,7},{6,4},{7,5},{8,10},{9,11},{10,... | collective-permute-start | bytes 1572872 | tf_op jit(solution)/shard_map/ppermute | solution.py:59
  16.5 46.7 %collective-permute-start.3 = (bf16[128,2048]{1,0:T(8,128)(2,1)}, bf16[128,2048]{1,0:T(8,128)(2,1)}, u32[]{:S(2)}, u32[]{:S(2)}) collective-permute-start(bf16[128,2048]{1,0:T(8,128)(2,1)} %bitcast_select_fusion), channel_id=1, source_target_pairs={{0,2},{1,3},{2,0},{3,1},{4,6},{5,7},{6,4},{7,5},{8,10},{9,11},{10,... | collective-permute-start | bytes 1572872 | tf_op jit(solution)/shard_map/ppermute | solution.py:59
  25.3 23.0 %collective-permute-start.7 = (bf16[256,1024]{1,0:T(8,128)(2,1)}, bf16[256,1024]{1,0:T(8,128)(2,1)}, u32[]{:S(2)}, u32[]{:S(2)}) collective-permute-start(bf16[256,1024]{1,0:T(8,128)(2,1)} %constant_dynamic-slice_fusion.1), channel_id=1, source_target_pairs={{0,4},{1,5},{2,6},{3,7},{4,0},{5,1},{6,2},{7,3},{8,12},{9,13},{10,... | collective-permute-start | bytes 1572872 | tf_op jit(solution)/shard_map/ppermute | solution.py:59
  52.6 110.5 %all-gather.13.cloned.1.call-start = ((), (), s32[]{:S(2)}) async-start(), calls=%async_computation.14 | async-start | bytes 2621440 | tf_op jit(solution)/shard_map/all_gather | solution.py:290
  61.6 25.0 %collective-permute-start.2 = (bf16[4,256,512]{2,1,0:T(8,128)(2,1)S(1)}, bf16[4,256,512]{2,1,0:T(8,128)(2,1)S(1)}, u32[]{:S(2)}, u32[]{:S(2)}) collective-permute-start(bf16[4,256,512]{2,1,0:T(8,128)(2,1)S(1)} %slice.204), channel_id=1, source_target_pairs={{0,4},{1,5},{2,6},{3,7},{4,0},{5,1},{6,2},{7,3},{8,12},{9,13},{10,... | collective-permute-start | bytes 3145736 | tf_op jit(solution)/shard_map/ppermute | solution.py:59
  90.5 26.5 %collective-permute-start.11 = (bf16[4,256,512]{2,1,0:T(8,128)(2,1)}, bf16[4,256,512]{2,1,0:T(8,128)(2,1)}, u32[]{:S(2)}, u32[]{:S(2)}) collective-permute-start(bf16[4,256,512]{2,1,0:T(8,128)(2,1)} %get-tuple-element.93), channel_id=1, source_target_pairs={{0,4},{1,5},{2,6},{3,7},{4,0},{5,1},{6,2},{7,3},{8,12},{9,13},{10,... | collective-permute-start | bytes 3145736 | tf_op jit(solution)/shard_map/ppermute | solution.py:59
  92.9 143.4 %all-gather.15.cloned.1.call-start = ((), (), s32[]{:S(2)}) async-start(), calls=%async_computation.15 | async-start | bytes 5242880 | tf_op jit(solution)/shard_map/all_gather | solution.py:290
  108.5 28.9 %collective-permute-start.14 = (bf16[2,128,2048]{2,1,0:T(8,128)(2,1)}, bf16[2,128,2048]{2,1,0:T(8,128)(2,1)S(1)}, u32[]{:S(2)}, u32[]{:S(2)}) collective-permute-start(bf16[2,128,2048]{2,1,0:T(8,128)(2,1)} %pad_maximum_fusion.9), channel_id=1, source_target_pairs={{0,4},{1,5},{2,6},{3,7},{4,0},{5,1},{6,2},{7,3},{8,12},{9,13},{10,... | collective-permute-start | bytes 3145736 | tf_op jit(solution)/shard_map/ppermute | solution.py:59
  143.6 150.1 %reduce-scatter.7.cloned.1.call-start = ((), (), s32[]{:S(2)}) async-start(), calls=%async_computation.6 | async-start | bytes 2621440 | tf_op jit(solution)/shard_map/reduce_scatter | solution.py:293
  246.6 103.4 %reduce-scatter.9.cloned.1.call-start = ((), (), s32[]{:S(2)}) async-start(), calls=%async_computation.7 | async-start | bytes 2621440 | tf_op jit(solution)/shard_map/reduce_scatter | solution.py:293
  266.7 24.1 %collective-permute-start.22 = (bf16[128,2048]{1,0:T(8,128)(2,1)}, bf16[128,2048]{1,0:T(8,128)(2,1)}, u32[]{:S(2)}, u32[]{:S(2)}) collective-permute-start(bf16[128,2048]{1,0:T(8,128)(2,1)} %get-tuple-element.187), channel_id=1, source_target_pairs={{0,4},{1,5},{2,6},{3,7},{4,0},{5,1},{6,2},{7,3},{8,12},{9,13},{10,... | collective-permute-start | bytes 1572872 | tf_op jit(solution)/shard_map/ppermute | solution.py:59
  267.3 23.5 %collective-permute-start.21 = (bf16[128,2048]{1,0:T(8,128)(2,1)}, bf16[128,2048]{1,0:T(8,128)(2,1)}, u32[]{:S(2)}, u32[]{:S(2)}) collective-permute-start(bf16[128,2048]{1,0:T(8,128)(2,1)} %get-tuple-element.185), channel_id=1, source_target_pairs={{0,2},{1,3},{2,0},{3,1},{4,6},{5,7},{6,4},{7,5},{8,10},{9,11},{10,... | collective-permute-start | bytes 1572872 | tf_op jit(solution)/shard_map/ppermute | solution.py:59
  267.8 120.1 %reduce-scatter.11.cloned.1.call-start = ((), (), s32[]{:S(2)}) async-start(), calls=%async_computation.8 | async-start | bytes 2621440 | tf_op jit(solution)/shard_map/reduce_scatter | solution.py:293
  305.9 129.3 %reduce-scatter.13.cloned.1.call-start = ((), (), s32[]{:S(2)}) async-start(), calls=%async_computation.9 | async-start | bytes 2621440 | tf_op jit(solution)/shard_map/reduce_scatter | solution.py:293
  346.5 125.9 %reduce-scatter.15.cloned.1.call-start = ((), (), s32[]{:S(2)}) async-start(), calls=%async_computation.10 | async-start | bytes 1310720 | tf_op jit(solution)/shard_map/reduce_scatter | solution.py:293
  357.1 30.8 %collective-permute-start.31 = (bf16[4,256,512]{2,1,0:T(8,128)(2,1)}, bf16[4,256,512]{2,1,0:T(8,128)(2,1)}, u32[]{:S(2)}, u32[]{:S(2)}) collective-permute-start(bf16[4,256,512]{2,1,0:T(8,128)(2,1)} %fusion.35), channel_id=1, source_target_pairs={{0,4},{1,5},{2,6},{3,7},{4,0},{5,1},{6,2},{7,3},{8,12},{9,13},{10,... | collective-permute-start | bytes 3145736 | tf_op jit(solution)/shard_map/ppermute | solution.py:59
  401.6 33.6 %collective-permute-start.39 = (bf16[4,256,512]{2,1,0:T(8,128)(2,1)}, bf16[4,256,512]{2,1,0:T(8,128)(2,1)}, u32[]{:S(2)}, u32[]{:S(2)}) collective-permute-start(bf16[4,256,512]{2,1,0:T(8,128)(2,1)} %fusion.34), channel_id=1, source_target_pairs={{0,4},{1,5},{2,6},{3,7},{4,0},{5,1},{6,2},{7,3},{8,12},{9,13},{10,... | collective-permute-start | bytes 3145736 | tf_op jit(solution)/shard_map/ppermute | solution.py:59
  411.0 84.3 %reduce-scatter.17.cloned.1.call-start = ((), (), s32[]{:S(2)}) async-start(), calls=%async_computation.11 | async-start | bytes 1310720 | tf_op jit(solution)/shard_map/reduce_scatter | solution.py:293
  437.5 36.7 %collective-permute-start.42 = (bf16[256,1024]{1,0:T(8,128)(2,1)}, bf16[256,1024]{1,0:T(8,128)(2,1)}, u32[]{:S(2)}, u32[]{:S(2)}) collective-permute-start(bf16[256,1024]{1,0:T(8,128)(2,1)} %get-tuple-element.203), channel_id=1, source_target_pairs={{0,4},{1,5},{2,6},{3,7},{4,0},{5,1},{6,2},{7,3},{8,12},{9,13},{10,... | collective-permute-start | bytes 1572872 | tf_op jit(solution)/shard_map/ppermute | solution.py:59
  440.5 33.7 %collective-permute-start.43 = (bf16[128,2048]{1,0:T(8,128)(2,1)}, bf16[128,2048]{1,0:T(8,128)(2,1)}, u32[]{:S(2)}, u32[]{:S(2)}) collective-permute-start(bf16[128,2048]{1,0:T(8,128)(2,1)} %get-tuple-element.182), channel_id=1, source_target_pairs={{0,2},{1,3},{2,0},{3,1},{4,6},{5,7},{6,4},{7,5},{8,10},{9,11},{10,... | collective-permute-start | bytes 1572872 | tf_op jit(solution)/shard_map/ppermute | solution.py:59
  440.9 33.4 %collective-permute-start.44 = (bf16[128,2048]{1,0:T(8,128)(2,1)}, bf16[128,2048]{1,0:T(8,128)(2,1)}, u32[]{:S(2)}, u32[]{:S(2)}) collective-permute-start(bf16[128,2048]{1,0:T(8,128)(2,1)} %get-tuple-element.181), channel_id=1, source_target_pairs={{0,4},{1,5},{2,6},{3,7},{4,0},{5,1},{6,2},{7,3},{8,12},{9,13},{10,... | collective-permute-start | bytes 1572872 | tf_op jit(solution)/shard_map/ppermute | solution.py:59
  445.4 33.5 %collective-permute-start.45 = (bf16[128,2048]{1,0:T(8,128)(2,1)}, bf16[128,2048]{1,0:T(8,128)(2,1)}, u32[]{:S(2)}, u32[]{:S(2)}) collective-permute-start(bf16[128,2048]{1,0:T(8,128)(2,1)} %get-tuple-element.180), channel_id=1, source_target_pairs={{0,6},{1,7},{2,4},{3,5},{4,2},{5,3},{6,0},{7,1},{8,14},{9,15},{10,... | collective-permute-start | bytes 1572872 | tf_op jit(solution)/shard_map/ppermute | solution.py:59
  (109 other events, 921.9 us)
Sparse Core Ops, SparseCore 0:
  10.2 50.0 all-gather.8
  61.8 46.5 all-gather.10
  110.0 44.6 all-gather.12
  156.7 79.4 all-gather.14
  246.7 42.3 reduce-scatter.6
  291.4 43.1 reduce-scatter.8
  336.9 43.1 reduce-scatter.10
  382.5 45.9 reduce-scatter.12
  431.4 33.5 reduce-scatter.14
  467.3 27.4 reduce-scatter.16
